TPU v7x, 256 devices: a whole 4x4x8 slice. The times are simulated.
256 devices in a mesh: section: 4 (over y), tp: 4 (over x_hi, core), cp: 16 (over z, x_lo).
Axes of the slice: x: 4 (x_hi: 2, x_lo: 2; x = x_hi * 2 + x_lo), y: 4, z: 8, core: 2. Of those that a mesh axis runs over, the one named last changes fastest.
Arguments:
- query_fwd: bfloat16 [4, 2048, 8192], P('section', 'cp', 'tp')
- key_fwd: bfloat16 [4, 2048, 1024], P('section', 'cp', 'tp')
- value_forward: bfloat16 [4, 2048, 1024], P('section', 'cp', 'tp'), may hold values from -6 to 6
- segment_fwd: int32 [4, 2048], P('section', 'cp'), may hold values from 0 to 3, never falling along the last dimension, each value on 1 to 1024 neighbouring positions
- query_bwd: bfloat16 [4, 2048, 8192], P('section', 'cp', 'tp')
- key_bwd: bfloat16 [4, 2048, 1024], P('section', 'cp', 'tp')
- value_backward: bfloat16 [4, 2048, 1024], P('section', 'cp', 'tp'), may hold values from -6 to 6
- segment_bwd: int32 [4, 2048], P('section', 'cp'), may hold values from 0 to 3, never falling along the last dimension, each value on 1 to 1024 neighbouring positions
- grad_out: bfloat16 [4, 2048, 8192], P('section', 'cp', 'tp'), may hold values from -6 to 6
Outputs:
- attn_out: bfloat16 [4, 2048, 8192], P('section', 'cp', 'tp')
- grad_query: bfloat16 [4, 2048, 8192], P('section', 'cp', 'tp')
- grad_key: bfloat16 [4, 2048, 1024], P('section', 'cp', 'tp')
- grad_value: bfloat16 [4, 2048, 1024], P('section', 'cp', 'tp')
Inputs may be any that keep to these rules, and one draw needn't show every extreme that they name: `segment_fwd`: document numbers never fall along a sequence. `segment_bwd`: document numbers never fall along a sequence.
All inputs are finite; a program needn't handle non-finite values.
Results may differ from a plain program's by a relative error of at most 0.013.
Values may be sent and summed in bfloat16 or wider, within the bound.
No kernel may reach another device: no remote copies, remote signals or barrier semaphores. Data moves between devices by JAX's collectives and lax.ppermute only.
A program may use at most 128 MiB of HBM per device.

v0:
```python
import jax
import jax.numpy as jnp
from jax import lax
from jax.sharding import PartitionSpec as P

QUERY_HEADS = 64
KEY_VALUE_HEADS = 8
HEAD_SIZE = 128


def shifted(block, axis, distance):
    devices = range(lax.axis_size(axis))
    route = [((i - distance) % len(devices), i) for i in devices]
    return lax.ppermute(block, axis, route)


def make_attend(q_heads, q_seg, first_row):
    rows = q_heads.shape[0]
    local_heads = q_heads.shape[1]
    scale = HEAD_SIZE ** (-0.5)
    q_pos = first_row + jnp.arange(rows)
    last_row = first_row + rows - 1

    def attend(carry, piece, start):
        k_part, v_part, s_part = piece
        count = k_part.shape[0]
        k_heads = k_part.reshape(count, local_heads, HEAD_SIZE)
        v_heads = v_part.reshape(count, local_heads, HEAD_SIZE)

        def compute(state):
            peak, total, accum = state
            k_pos = jnp.arange(count)
            visible = (k_pos[None, :] <= q_pos[:, None]) & (s_part[None, :] == q_seg[:, None])
            score = (
                jnp.einsum("igha,jga->ghij", q_heads, k_heads, preferred_element_type=jnp.float32)
                * scale
            )
            masked = jnp.where(visible, score, -jnp.inf)
            fresh = jnp.max(masked, axis=-1)
            safe = jnp.where(fresh == -jnp.inf, 0.0, fresh)
            factor = jnp.exp(peak - safe)
            expo = jnp.where(visible, jnp.exp(score - safe[..., None]), 0.0)
            total = total * factor + jnp.sum(expo, axis=-1)
            weights = expo.astype(jnp.bfloat16)
            added = jnp.einsum(
                "ghij,jga->igha", weights, v_heads, preferred_element_type=jnp.float32
            )
            accum = accum * factor.transpose(2, 0, 1)[..., None] + added
            return (fresh, total, accum)

        return lax.cond(start <= last_row, compute, lambda state: state, carry)

    return attend


def empty_state(rows, local_heads, group_factor):
    peak = jnp.full((local_heads, group_factor, rows), -jnp.inf, jnp.float32)
    total = jnp.zeros((local_heads, group_factor, rows), jnp.float32)
    accum = jnp.zeros((rows, local_heads, group_factor, HEAD_SIZE), jnp.float32)
    return (peak, total, accum)


def forward_pass(query_fwd, key_fwd, value_forward, segment_fwd, first_row):
    group_factor = QUERY_HEADS // KEY_VALUE_HEADS
    query_rows = query_fwd[0]
    rows = query_rows.shape[0]
    local_heads = key_fwd.shape[2] // HEAD_SIZE
    q_heads = query_rows.reshape(rows, local_heads, group_factor, HEAD_SIZE)
    attend = make_attend(q_heads, segment_fwd[0], first_row)
    peak, total, accum = attend(
        empty_state(rows, local_heads, group_factor),
        (
            lax.all_gather(key_fwd[0], "cp", axis=0, tiled=True),
            lax.all_gather(value_forward[0], "cp", axis=0, tiled=True),
            lax.all_gather(segment_fwd[0], "cp", axis=0, tiled=True),
        ),
        jnp.int32(0),
    )
    output = (
        (accum / total.transpose(2, 0, 1)[..., None])
        .astype(jnp.bfloat16)
        .reshape(rows, query_rows.shape[1])
    )
    passed = shifted(output, "section", 1)
    return passed[None]


def backward_pass(query_bwd, key_bwd, value_backward, segment_bwd, grad_out, first_row):
    group_factor = QUERY_HEADS // KEY_VALUE_HEADS
    scale = HEAD_SIZE ** (-0.5)
    query_rows = query_bwd[0]
    rows = query_rows.shape[0]
    q_width = query_rows.shape[1]
    kv_width = key_bwd.shape[2]
    local_heads = kv_width // HEAD_SIZE
    q_heads = query_rows.reshape(rows, local_heads, group_factor, HEAD_SIZE)
    q_seg = segment_bwd[0]
    attend = make_attend(q_heads, q_seg, first_row)
    all_keys, all_values, all_segs = (
        lax.all_gather(key_bwd[0], "cp", axis=0, tiled=True),
        lax.all_gather(value_backward[0], "cp", axis=0, tiled=True),
        lax.all_gather(segment_bwd[0], "cp", axis=0, tiled=True),
    )
    length = all_keys.shape[0]
    peak, total, accum = attend(
        empty_state(rows, local_heads, group_factor),
        (
            lax.all_gather(key_bwd[0], "cp", axis=0, tiled=True),
            lax.all_gather(value_backward[0], "cp", axis=0, tiled=True),
            lax.all_gather(segment_bwd[0], "cp", axis=0, tiled=True),
        ),
        jnp.int32(0),
    )
    out_full = accum / total.transpose(2, 0, 1)[..., None]
    lse = peak + jnp.log(total)
    d_heads = grad_out[0].reshape(rows, local_heads, group_factor, HEAD_SIZE)
    delta = jnp.sum(d_heads.astype(jnp.float32) * out_full, axis=-1).transpose(1, 2, 0)
    k_heads = all_keys.reshape(length, local_heads, HEAD_SIZE)
    v_heads = all_values.reshape(length, local_heads, HEAD_SIZE)
    q_pos = first_row + jnp.arange(rows)
    k_pos = jnp.arange(length)
    visible = (k_pos[None, :] <= q_pos[:, None]) & (all_segs[None, :] == q_seg[:, None])
    score = (
        jnp.einsum("igha,jga->ghij", q_heads, k_heads, preferred_element_type=jnp.float32) * scale
    )
    prob = jnp.where(visible, jnp.exp(score - lse[..., None]), 0.0)
    prob_half = prob.astype(jnp.bfloat16)
    value_terms = jnp.einsum(
        "ghij,igha->jga", prob_half, d_heads, preferred_element_type=jnp.float32
    )
    dprob = jnp.einsum("igha,jga->ghij", d_heads, v_heads, preferred_element_type=jnp.float32)
    dscore = (prob * (dprob - delta[..., None])).astype(jnp.bfloat16)
    dquery = (
        jnp.einsum("ghij,jga->igha", dscore, k_heads, preferred_element_type=jnp.float32) * scale
    ).astype(jnp.bfloat16)
    key_terms = (
        jnp.einsum("ghij,igha->jga", dscore, q_heads, preferred_element_type=jnp.float32) * scale
    )
    terms = jnp.concatenate(
        [key_terms.reshape(length, kv_width), value_terms.reshape(length, kv_width)], axis=1
    )
    owned = lax.psum_scatter(
        terms.astype(jnp.bfloat16), "cp", scatter_dimension=0, tiled=True
    ).astype(jnp.float32)
    dkey = owned[:, :kv_width].astype(jnp.bfloat16)
    dvalue = owned[:, kv_width:].astype(jnp.bfloat16)
    joined = jnp.concatenate([dquery.reshape(rows, q_width), dkey, dvalue], axis=1)
    returned = shifted(joined, "section", -1)
    grad_query = returned[:, :q_width][None]
    grad_key = returned[:, q_width : q_width + kv_width][None]
    grad_value = returned[:, q_width + kv_width :][None]
    return (grad_query, grad_key, grad_value)


def per_device(
    query_fwd,
    key_fwd,
    value_forward,
    segment_fwd,
    query_bwd,
    key_bwd,
    value_backward,
    segment_bwd,
    grad_out,
):
    rows = query_fwd.shape[1]
    first_row = lax.axis_index("cp") * rows
    attn_out = forward_pass(query_fwd, key_fwd, value_forward, segment_fwd, first_row)
    grad_query, grad_key, grad_value = backward_pass(
        query_bwd, key_bwd, value_backward, segment_bwd, grad_out, first_row
    )
    return (attn_out, grad_query, grad_key, grad_value)


def solution(mesh):
    placed = (
        P("section", "cp", "tp"),
        P("section", "cp", "tp"),
        P("section", "cp", "tp"),
        P("section", "cp"),
        P("section", "cp", "tp"),
        P("section", "cp", "tp"),
        P("section", "cp", "tp"),
        P("section", "cp"),
        P("section", "cp", "tp"),
    )
    return jax.shard_map(
        per_device,
        mesh=mesh,
        in_specs=placed,
        out_specs=(
            P("section", "cp", "tp"),
            P("section", "cp", "tp"),
            P("section", "cp", "tp"),
            P("section", "cp", "tp"),
        ),
        check_vma=False,
    )
```

profile of v0, /device:TPU:56, one launch (start us, length us, event | category | flops | bytes accessed | tf_op | source)
XLA Modules:
  0.0 389.0 jit_solution(13322412720380093558)
XLA Ops:
  7.2 0.0 copy-start.6
  7.2 0.0 all-gather.15.cloned.1.call-start
  7.2 1.6 copy.35
  8.8 0.0 all-gather.15.cloned.1.call-update
  8.8 0.0 all-gather.17.cloned.1.call-start
  8.9 1.6 copy.39
  10.4 0.0 all-gather.17.cloned.1.call-update
  10.5 0.0 all-gather.11.cloned.1.call-start
  10.5 0.7 all-gather.11.cloned.1.call-update
  11.2 0.0 all-gather.13.cloned.1.call-start
  11.3 0.5 all-gather.13.cloned.1.call-update
  11.8 0.0 reduce-scatter.2.cloned.1.call-start
  11.8 1.3 copy.36
  13.2 33.7 %all-gather.3 = s32[1,2048]{1,0:T(1,128)S(1)} all-gather(s32[1,128]{1,0:T(1,128)} %param.20), channel_id=5, replica_groups=mesh['section'=4,'tp'=4,'cp'=16] {'cp'}, dimensions={1}, use_global_device_ids=true | all-gather | bytes 8704 | tf_op jit(solution)/shard_map/all_gather | solution.py:102
  46.9 1.3 copy.43
  48.2 1.7 fusion.64
  49.9 30.8 %all-gather.15.cloned.1.call-done = bf16[1,2048,256]{1,2,0:T(8,128)(2,1)} async-done(((bf16[1,128,256]{1,2,0:T(8,128)(2,1)}), bf16[1,2048,256]{1,2,0:T(8,128)(2,1)}) %all-gather.15.cloned.1.call-update) | async-done | bytes 1048592 | tf_op jit(solution)/shard_map/all_gather | solution.py:100
  80.7 9.4 %fusion.68 = f32[2,2048,128,8]{2,1,3,0:T(8,128)} fusion(bf16[2048,2,128,1]{0,2,3,1:T(8,128)(2,1)} %bitcast.158, bf16[128,2,8,128]{0,3,2,1:T(8,128)(2,1)S(1)} %bitcast.155), kind=kOutput, calls=%fused_computation.79 | convolution fusion | flops 1073741824 | bytes 18350080 | tf_op jit(solution)/shard_map/igha,jga->ghij/dot_general | solution.py:124
  90.1 60.1 %all-gather.17.cloned.1.call-done = bf16[1,2048,256]{1,2,0:T(8,128)(2,1)} async-done(((bf16[1,128,256]{1,2,0:T(8,128)(2,1)}), bf16[1,2048,256]{1,2,0:T(8,128)(2,1)}) %all-gather.17.cloned.1.call-update) | async-done | bytes 1048592 | tf_op jit(solution)/shard_map/all_gather | solution.py:109
  150.2 32.5 %conditional.3 = (f32[2,8,128]{2,1,0:T(8,128)}, f32[2,8,128]{2,1,0:T(8,128)S(1)}, f32[2,8,128]{2,1,0:T(8,128)S(1)}, f32[128,2,8,128]{0,3,2,1:T(8,128)S(1)}) conditional(s32[]{:T(128)} %convert_element_type.32, () %tuple.28, (s32[128]{0:T(128)S(1)}, s32[2048]{0:T(1024)S(1)}, s32[1,128]{1,0:T(1,128)S(1)}, bf16[2048,2,128]{0,2,1:T(8,128)(2,1)S(1)}, ...), branch_computations={%region_4.5_spmd, %region_5.8_spmd} | conditional | flops 2194688000 | bytes 57263136 | solution.py:51
  150.2 0.3 fusion.41
  150.5 7.8 %fusion.24 = (f32[2,8,128]{2,1,0:T(8,128)}, f32[2,2048,128,8]{2,1,3,0:T(8,128)}) fusion(pred[128,2048]{0,1:T(8,128)(4,1)S(1)} %fusion.41, bf16[128,2,8,128]{0,3,2,1:T(8,128)(2,1)S(1)} %get-tuple-element.62, bf16[2048,2,128]{0,2,1:T(8,128)(2,1)S(1)} %get-tuple-element.61), kind=kOutput, calls=%fused_computation.27 | convolution fusion | flops 1086322688 | bytes 18620416 | tf_op jit(solution)/shard_map/cond/branch_1_fun/igha,jga->ghij/dot_general | solution.py:35
  158.4 0.7 compare_select_fusion.3
  159.1 9.1 %fusion.28 = f32[2,8,128]{2,1,0:T(8,128)S(1)} fusion(f32[2,2048,128,8]{2,1,3,0:T(8,128)} %get-tuple-element.70, f32[2,8,128]{2,1,0:T(8,128)S(1)} %compare_select_fusion.3, pred[128,2048]{0,1:T(8,128)(4,1)S(1)} %fusion.41), kind=kLoop, calls=%fused_computation.31 | loop fusion | flops 16775168 | bytes 17055744 | tf_op jit(solution)/shard_map/cond/branch_1_fun/reduce_sum | solution.py:43
  168.2 0.7 fusion.67
  168.9 0.7 fusion.44
  169.6 11.5 %fusion.35 = f32[128,2,8,128]{3,0,2,1:T(8,128)} fusion(f32[2,2048,128,8]{2,1,3,0:T(8,128)} %get-tuple-element.70, f32[2,8,128]{2,1,0:T(8,128)S(1)} %compare_select_fusion.3, pred[128,2048]{0,1:T(8,128)(4,1)S(1)} %fusion.41, bf16[2048,2,128]{0,2,1:T(8,128)(2,1)} %get-tuple-element.63, f32[128,2,8]{0,2,1:T(8,128)S(1)} %fusion.44), kind=kOutput, calls=%fused_computation.35 | convolution fusion | flops 1090781184 | bytes 19152896 | tf_op jit(solution)/shard_map/cond/branch_1_fun/ghij,jga->igha/dot_general | solution.py:45
  181.1 1.6 copy.83
  182.7 0.7 add.38
  183.4 0.2 multiply_reduce_fusion
  183.6 0.0 copy-start.5
  183.6 11.9 %fusion.48 = bf16[2,8,128,2048]{2,3,1,0:T(8,128)(2,1)S(1)} fusion(f32[2,2048,128,8]{2,1,3,0:T(8,128)} %fusion.68, f32[2,8,128]{2,1,0:T(8,128)S(1)} %bitcast.181, f32[2,8,128]{2,1,0:T(8,128)S(1)} %add.38, pred[128,2048]{0,1:T(8,128)(4,1)} %fusion.64, bf16[2048,2,128,1]{0,2,3,1:T(8,128)(2,1)} %bitcast.186, bf16[128,2,8,128]{0,3,2,1:T(8,128)(2,1)S(1)} %bitcast.164), kind=kOutput, calls=%fused_computation.51 | convolution fusion | flops 1098907648 | bytes 27017216 | tf_op jit(solution)/shard_map/igha,jga->ghij/dot_general | solution.py:131
  195.5 3.2 copy-done
  198.7 2.8 fusion.62
  201.5 1.4 copy.50
  202.9 8.9 %fusion.59 = bf16[2,2048,128]{1,2,0:T(8,128)(2,1)} fusion(bf16[128,2,8,128]{0,3,2,1:T(8,128)(2,1)S(1)} %bitcast.165, f32[2,2048,128,8]{2,1,3,0:T(8,128)} %fusion.68, f32[2,8,128]{2,1,0:T(8,128)S(1)} %add.38, pred[128,2048]{0,1:T(8,128)(4,1)S(1)} %copy-done.5), kind=kOutput, calls=%fused_computation.61 | convolution fusion | flops 1091043328 | bytes 18620416 | tf_op jit(solution)/shard_map/ghij,igha->jga/dot_general | solution.py:128
  211.7 2.3 copy.51
  214.1 2.7 pad_maximum_fusion
  216.8 0.0 reduce-scatter.2.cloned.1.call-update
  216.9 30.8 %all-gather = s32[1,2048]{1,0:T(1,128)S(1)} all-gather(s32[1,128]{1,0:T(1,128)S(1)} %copy-done.7), channel_id=2, replica_groups=mesh['section'=4,'tp'=4,'cp'=16] {'cp'}, dimensions={1}, use_global_device_ids=true | all-gather | bytes 8704 | tf_op jit(solution)/shard_map/all_gather | solution.py:75
  247.6 4.7 %fusion.63 = bf16[2,8,128,128]{2,3,1,0:T(8,128)(2,1)S(1)} fusion(bf16[2048,2,128,1]{0,2,3,1:T(8,128)(2,1)S(1)} %bitcast.160, bf16[2,8,128,2048]{2,3,1,0:T(8,128)(2,1)} %copy-done), kind=kOutput, calls=%fused_computation.65 | convolution fusion | flops 1074266112 | bytes 9961472 | tf_op jit(solution)/shard_map/ghij,jga->igha/dot_general | solution.py:134
  252.3 0.2 copy.52
  252.5 0.0 all-gather.11.cloned.1.call-done
  252.5 37.6 %all-gather.13.cloned.1.call-done = bf16[1,2048,256]{2,1,0:T(8,128)(2,1)} async-done(((bf16[1,128,256]{2,1,0:T(8,128)(2,1)}), bf16[1,2048,256]{2,1,0:T(8,128)(2,1)}) %all-gather.13.cloned.1.call-update) | async-done | bytes 1048592 | tf_op jit(solution)/shard_map/all_gather | solution.py:74
  290.1 28.3 %conditional.2 = (f32[2,8,128]{2,1,0:T(8,128)S(1)}, f32[128,2,8,128]{3,0,2,1:T(8,128)S(1)}) conditional(s32[]{:T(128)} %convert_element_type.32, () %tuple.26, (s32[128]{0:T(128)S(1)}, s32[2048]{0:T(1024)S(1)}, s32[1,128]{1,0:T(1,128)S(1)}, bf16[2048,256]{1,0:T(8,128)(2,1)}, bf16[1,128,2048]{2,1,0:T(8,128)(2,1)S(1)}, ...), branch_computations={%region_0.0_spmd, %region_1.4_spmd} | conditional | flops 2194688000 | bytes 64594988 | solution.py:51
  290.1 0.3 fusion.17
  290.5 1.6 reshape.56
  292.1 0.1 copy.84
  292.2 7.2 %fusion = (f32[2,8,128]{2,1,0:T(8,128)S(1)}, f32[2,2048,128,8]{2,1,3,0:T(8,128)}) fusion(pred[128,2048]{0,1:T(8,128)(4,1)S(1)} %fusion.17, bf16[128,2,8,128]{3,2,1,0:T(8,128)(2,1)S(1)} %bitcast.175, bf16[2048,2,128,1]{2,1,0,3:T(2,128)(2,1)S(1)} %bitcast.170), kind=kOutput, calls=%fused_computation.2 | convolution fusion | flops 1086322688 | bytes 18620416 | tf_op jit(solution)/shard_map/cond/branch_1_fun/igha,jga->ghij/dot_general | solution.py:35
  299.4 1.1 reshape.57
  300.5 8.7 %fusion.11 = f32[128,2,8,128]{3,0,2,1:T(8,128)S(1)} fusion(f32[2,2048,128,8]{2,1,3,0:T(8,128)} %get-tuple-element.68, f32[2,8,128]{2,1,0:T(8,128)S(1)} %compare_select_fusion.1, pred[128,2048]{0,1:T(8,128)(4,1)S(1)} %fusion.17, bf16[2048,2,128,1]{2,1,0,3:T(2,128)(2,1)} %bitcast.171, f32[128,2,8]{0,2,1:T(8,128)S(1)} %fusion.21), kind=kOutput, calls=%fused_computation.10 | convolution fusion | flops 1090781184 | bytes 19152896 | tf_op jit(solution)/shard_map/cond/branch_1_fun/ghij,jga->igha/dot_general | solution.py:45
  309.2 9.2 %fusion.4 = f32[2,8,128]{2,1,0:T(8,128)S(1)} fusion(f32[2,2048,128,8]{2,1,3,0:T(8,128)} %get-tuple-element.68, f32[2,8,128]{2,1,0:T(8,128)S(1)} %compare_select_fusion.1, pred[128,2048]{0,1:T(8,128)(4,1)S(1)} %fusion.17), kind=kLoop, calls=%fused_computation.6 | loop fusion | flops 16775168 | bytes 17055744 | tf_op jit(solution)/shard_map/cond/branch_1_fun/reduce_sum | solution.py:43
  318.4 48.9 %reduce-scatter.2.cloned.1.call-done = bf16[128,512]{1,0:T(8,128)(2,1)} async-done(((bf16[2048,512]{1,0:T(8,128)(2,1)}), bf16[128,512]{1,0:T(8,128)(2,1)}) %reduce-scatter.2.cloned.1.call-update) | async-done | bytes 131088 | tf_op jit(solution)/shard_map/reduce_scatter | solution.py:142
  367.3 0.9 pad_maximum_fusion.1
  368.3 0.6 collective-permute-start.1
  368.9 0.3 divide_convert_fusion
  369.2 0.3 copy.34
  369.6 0.1 copy.97
  369.7 2.8 collective-permute-start
  372.5 6.7 %collective-permute-done = bf16[128,2048]{1,0:T(8,128)(2,1)S(1)} collective-permute-done((bf16[128,2048]{1,0:T(8,128)(2,1)S(1)}, bf16[128,2048]{1,0:T(8,128)(2,1)S(1)}, u32[]{:S(2)}, u32[]{:S(2)}) %collective-permute-start) | collective-permute-done | bytes 524320 | tf_op jit(solution)/shard_map/ppermute | solution.py:14
  379.2 0.9 collective-permute-done.1
  380.1 0.8 slice_bitcast_fusion
  381.0 0.7 slice_bitcast_fusion.1
  381.6 0.8 copy.111
  (17 shorter events, 0.0 us)
Async XLA Ops:
  7.2 143.0 %copy-start.6 = (s32[1,128]{1,0:T(1,128)S(1)}, s32[1,128]{1,0:T(1,128)}, u32[]{:S(2)}) copy-start(s32[1,128]{1,0:T(1,128)} %param.20) | copy-start | bytes 1540
  7.2 73.5 %all-gather.15.cloned.1.call-start = ((), (), s32[]{:S(2)}) async-start(), calls=%async_computation.4 | async-start | bytes 1114112 | tf_op jit(solution)/shard_map/all_gather | solution.py:100
  8.8 141.4 %all-gather.17.cloned.1.call-start = ((), (), s32[]{:S(2)}) async-start(), calls=%async_computation.5 | async-start | bytes 1114112 | tf_op jit(solution)/shard_map/all_gather | solution.py:109
  10.5 242.1 %all-gather.11.cloned.1.call-start = ((), (), s32[]{:S(2)}) async-start(), calls=%async_computation.2 | async-start | bytes 1114112 | tf_op jit(solution)/shard_map/all_gather | solution.py:73
  11.2 278.9 %all-gather.13.cloned.1.call-start = ((), (), s32[]{:S(2)}) async-start(), calls=%async_computation.3 | async-start | bytes 1114112 | tf_op jit(solution)/shard_map/all_gather | solution.py:74
  11.8 355.5 %reduce-scatter.2.cloned.1.call-start = ((), (), s32[]{:S(2)}) async-start(), calls=%async_computation.1 | async-start | bytes 2228224 | tf_op jit(solution)/shard_map/reduce_scatter | solution.py:142
  80.7 69.5 %copy-start.1 = (bf16[1,2048,256]{1,2,0:T(8,128)(2,1)S(1)}, bf16[1,2048,256]{1,2,0:T(8,128)(2,1)}, u32[]{:S(2)}) copy-start(bf16[1,2048,256]{1,2,0:T(8,128)(2,1)} %all-gather.15.cloned.1.call-done) | copy-start | bytes 3145732
  183.6 19.3 %copy-start.5 = (pred[128,2048]{0,1:T(8,128)(4,1)S(1)}, pred[128,2048]{0,1:T(8,128)(4,1)}, u32[]{:S(2)}) copy-start(pred[128,2048]{0,1:T(8,128)(4,1)} %fusion.64) | copy-start | bytes 786436
  195.5 3.2 copy-start
  202.9 11.2 %copy-start.2 = (bf16[2048,256]{1,0:T(8,128)(2,1)S(1)}, bf16[2048,256]{1,0:T(8,128)(2,1)}, u32[]{:S(2)}) copy-start(bf16[2048,256]{1,0:T(8,128)(2,1)} %copy.50) | copy-start | bytes 3145732
  202.9 14.0 %copy-start.7 = (s32[1,128]{1,0:T(1,128)S(1)}, s32[1,128]{1,0:T(1,128)}, u32[]{:S(2)}) copy-start(s32[1,128]{1,0:T(1,128)} %param.16) | copy-start | bytes 1540
  211.7 78.4 %copy-start.4 = (bf16[1,128,2048]{2,1,0:T(8,128)(2,1)S(1)}, bf16[1,128,2048]{2,1,0:T(8,128)(2,1)}, u32[]{:S(2)}) copy-start(bf16[1,128,2048]{2,1,0:T(8,128)(2,1)} %param.13) | copy-start | bytes 1572868
  290.1 9.3 %copy-start.3 = (bf16[2048,256]{1,0:T(8,128)(2,1)S(1)}, bf16[2048,256]{1,0:T(8,128)(2,1)}, u32[]{:S(2)}) copy-start(bf16[2048,256]{1,0:T(8,128)(2,1)} %get-tuple-element.33) | copy-start | bytes 3145732 | tf_op jit(solution)/shard_map/cond
  368.3 11.9 %collective-permute-start.1 = (bf16[128,2560]{1,0:T(8,128)(2,1)S(1)}, bf16[128,2560]{1,0:T(8,128)(2,1)S(1)}, u32[]{:S(2)}, u32[]{:S(2)}) collective-permute-start(bf16[128,2560]{1,0:T(8,128)(2,1)S(1)} %pad_maximum_fusion.1), channel_id=1, source_target_pairs={{64,0},{128,64},{192,128},{0,192},{65,1},{129,65},{193,129},{1,193... | collective-permute-start | bytes 1966088 | tf_op jit(solution)/shard_map/ppermute | solution.py:14
  369.7 9.5 %collective-permute-start = (bf16[128,2048]{1,0:T(8,128)(2,1)S(1)}, bf16[128,2048]{1,0:T(8,128)(2,1)S(1)}, u32[]{:S(2)}, u32[]{:S(2)}) collective-permute-start(bf16[128,2048]{1,0:T(8,128)(2,1)S(1)} %bitcast.174), channel_id=1, source_target_pairs={{192,0},{0,64},{64,128},{128,192},{193,1},{1,65},{65,129},{129,193... | collective-permute-start | bytes 1572872 | tf_op jit(solution)/shard_map/ppermute | solution.py:14
Sparse Core Ops, SparseCore 0:
  10.3 70.3 all-gather.14
  83.0 67.1 all-gather.16
  152.0 67.2 all-gather.10
  220.9 69.1 all-gather.12
  292.5 74.7 reduce-scatter.1
where the time goes:
time: 394 us; the launch traced here: 389 us
  waiting for transfers between devices  186 us (47%)
  matrix products  72.8 us (18%)
  blocking collectives  64.5 us (16%)
  other arithmetic  27.8 us (7%)
  local copies, waits for them, and re-layouts  20.1 us (5%)
  between operations  13.9 us (4%)
    all_gather x1, waiting for transfers between devices, backward_pass(): lax.all_gather(value_backward[0], 'cp', axis=0, tiled=True)  60.1 us
    reduce_scatter x1, waiting for transfers between devices, backward_pass(): lax.psum_scatter(terms.astype(jnp.bfloat16), 'cp', scatter_dimension=0, t...  48.9 us
    all_gather x1, waiting for transfers between devices, forward_pass(): lax.all_gather(value_forward[0], 'cp', axis=0, tiled=True)  37.6 us
    all_gather x1, blocking collectives, backward_pass(): lax.all_gather(segment_bwd[0], 'cp', axis=0, tiled=True)  33.7 us
    all_gather x1, waiting for transfers between devices, backward_pass(): lax.all_gather(key_bwd[0], 'cp', axis=0, tiled=True)  30.8 us
    all_gather x1, blocking collectives, forward_pass(): lax.all_gather(segment_fwd[0], 'cp', axis=0, tiled=True)  30.8 us
    dot_general x2, matrix products, compute(): jnp.einsum('ghij,jga->igha', weights, v_heads, preferred_element_type=jnp...  20.2 us
    reduce_sum x2, other arithmetic, compute(): total = total * factor + jnp.sum(expo, axis=-1)  18.4 us
  transfers between devices with their start and end apart: 7, of which 6 were waited for; matrix products, arithmetic and copies ran while one was open for 29% of the time, Pallas kernels for 0%

commit v1 on v0

v1 whole, which is shorter than its diff:
```python
import math

import jax
import jax.numpy as jnp
from jax import lax
from jax.experimental import pallas as pl
from jax.experimental.pallas import tpu as pltpu
from jax.sharding import PartitionSpec as P

HEAD = 128
ROWS = 128
GROUP = 8
PAIR = 2 * ROWS
HOPS = 4
SLOTS = HOPS + 1
KEYS = SLOTS * PAIR
DOCS = 4
TAIL = 16
HALF = GROUP * HEAD
SCALE = HEAD ** (-0.5)
SCALE2 = SCALE * math.log2(math.e)
F32 = jnp.float32
BF16 = jnp.bfloat16
NT = (((1,), (1,)), ((), ()))
VMEM = pl.BlockSpec(memory_space=pltpu.VMEM)
SMEM = pl.BlockSpec(memory_space=pltpu.SMEM)


def dot(a, b):
    return jnp.dot(a, b, preferred_element_type=F32)


def dot_nt(a, b):
    return lax.dot_general(a, b, NT, preferred_element_type=F32)


def call(kernel, outs, n_in, scratch=(), flops=0, moved_bytes=2**19, name=None):
    return pl.pallas_call(
        kernel,
        out_shape=outs,
        in_specs=[SMEM] + [VMEM] * n_in,
        out_specs=[VMEM] * len(outs),
        scratch_shapes=scratch,
        compiler_params=pltpu.CompilerParams(vmem_limit_bytes=40 * 2**20),
        cost_estimate=pl.CostEstimate(flops=flops, bytes_accessed=moved_bytes, transcendentals=0),
        name=name,
    )


def shape(*dims):
    return jax.ShapeDtypeStruct(dims, BF16)


def split_kernel(where_ref, kb, vb, sb, kf, vf, sf, keep, send):
    side = where_ref[0]
    for at, part in enumerate((kb, vb, kf, vf)):
        cols = pl.ds(at * HEAD, HEAD)
        low, high = part[:, :HEAD], part[:, HEAD:]
        keep[:ROWS, cols] = jnp.where(side == 0, low, high)
        send[:ROWS, cols] = jnp.where(side == 0, high, low)
    for out in (keep, send):
        out[ROWS:, :] = jnp.zeros((TAIL, 4 * HEAD), BF16)
        for at, seg in ((0, sb), (2, sf)):
            row = seg[...].astype(F32).astype(BF16)
            out[ROWS:, at * HEAD : (at + 1) * HEAD] = jnp.broadcast_to(row, (TAIL, ROWS))


def join_kernel(where_ref, keep, got, eb, ef):
    del where_ref
    for at, out in ((0, eb), (2, ef)):
        cols = slice(at * HEAD, (at + 2) * HEAD)
        out[:ROWS, :] = keep[:ROWS, cols]
        out[ROWS:PAIR, :] = got[:ROWS, cols]
        out[PAIR:, :ROWS] = keep[ROWS:, at * HEAD : (at + 1) * HEAD]
        out[PAIR:, ROWS:] = got[ROWS:, at * HEAD : (at + 1) * HEAD]


def other_half_kernel(where_ref, *refs):
    side = where_ref[0]
    start = pl.multiple_of((1 - side) * HALF, HALF)
    out = refs[-1]
    for at, ref in enumerate(refs[:-1]):
        out[:, at * HALF : (at + 1) * HALF] = ref[:, pl.ds(start, HALF)]


def whole_kernel(where_ref, own, cross, out):
    side = where_ref[0]
    out[:, pl.ds(pl.multiple_of(side * HALF, HALF), HALF)] = own[...]
    out[:, pl.ds(pl.multiple_of((1 - side) * HALF, HALF), HALF)] = cross[...]


def fill_cap(where_ref, blocks, cap):
    side, depth = where_ref[0], where_ref[1]
    segs = [b[PAIR : PAIR + 1, :].astype(F32) for b in blocks]
    start = jnp.zeros((1, PAIR), F32)
    for d in range(DOCS):
        first = jnp.sum((segs[0] < d).astype(F32), axis=1, keepdims=True)
        for k in range(1, SLOTS):
            same = jnp.sum((segs[k] == d).astype(F32), axis=1, keepdims=True)
            first = first - jnp.where(depth >= k, same, 0.0)
        start = jnp.where(segs[0] == d, first, start)
    start = start.astype(jnp.int32)
    lane = lax.broadcasted_iota(jnp.int32, (ROWS, PAIR), 1)
    row = jnp.where(lane < ROWS, lane + side * ROWS, lane - side * ROWS)
    for k in range(SLOTS):
        for part in range(2):
            block = side if part == 0 else 1 - side
            key = lax.broadcasted_iota(jnp.int32, (ROWS, PAIR), 0) + (block * ROWS - k * PAIR)
            seen = (key >= start) & (key <= row)
            cap[pl.ds(k * PAIR + part * ROWS, ROWS), :] = jnp.where(seen, 3.0e38, -jnp.inf)


def fill_window(blocks, kwin, vwin):
    for k, b in enumerate(blocks):
        kwin[pl.ds(k * PAIR, PAIR), :] = b[:PAIR, :HEAD]
        vwin[pl.ds(k * PAIR, PAIR), :] = b[:PAIR, HEAD:]


def head_rows(side, own, other, g, base):
    cols = pl.ds(pl.multiple_of(side * HALF + g * HEAD, HEAD), HEAD)
    return jnp.concatenate([own[:, cols], other[:, pl.ds(base + g * HEAD, HEAD)]], axis=0)


def fwd_kernel(where_ref, q_ref, qx_ref, *refs):
    blocks, (own_ref, cross_ref, kwin, vwin, cap, s_ref) = refs[:SLOTS], refs[SLOTS:]
    side = where_ref[0]
    fill_window(blocks, kwin, vwin)
    fill_cap(where_ref, blocks, cap)
    vt = vwin[...].T
    for g in range(GROUP):
        queries = head_rows(side, q_ref, qx_ref, g, 0)
        masked = jnp.minimum(dot_nt(kwin[...], queries), cap[...])
        s_ref[...] = masked
        peak = jnp.max(masked, axis=0, keepdims=True)
        expo = jnp.exp2((s_ref[...] - peak) * SCALE2)
        total = jnp.sum(expo, axis=0, keepdims=True)
        out = (dot(vt, expo.astype(BF16)) / total).T.astype(BF16)
        cols = slice(g * HEAD, (g + 1) * HEAD)
        own_ref[:, cols] = out[:ROWS]
        cross_ref[:, cols] = out[ROWS:]


def bwd_kernel(where_ref, q_ref, d_ref, qdx_ref, *refs):
    blocks = refs[:SLOTS]
    own_ref, cross_ref = refs[SLOTS : SLOTS + 2]
    parts = refs[SLOTS + 2 : 2 * SLOTS + 2]
    kwin, vwin, cap, s_ref, dp_ref, p_ref, ds_ref, qs_ref, gs_ref = refs[2 * SLOTS + 2 :]
    side = where_ref[0]
    fill_window(blocks, kwin, vwin)
    fill_cap(where_ref, blocks, cap)
    kt = kwin[...].T
    for g in range(GROUP):
        cols = pl.ds(g * PAIR, PAIR)
        queries = head_rows(side, q_ref, qdx_ref, g, 0)
        grads = head_rows(side, d_ref, qdx_ref, g, HALF)
        qs_ref[cols, :] = queries
        gs_ref[cols, :] = grads
        masked = jnp.minimum(dot_nt(kwin[...], queries), cap[...])
        s_ref[...] = masked
        peak = jnp.max(masked, axis=0, keepdims=True)
        dp = dot_nt(vwin[...], grads)
        expo = jnp.exp2((s_ref[...] - peak) * SCALE2)
        s_ref[...] = expo
        dp_ref[...] = dp
        inv = 1.0 / jnp.sum(expo, axis=0, keepdims=True)
        delta = jnp.sum(expo * dp, axis=0, keepdims=True) * inv
        prob = s_ref[...] * inv
        p_ref[:, cols] = prob.astype(BF16)
        ds = (prob * (dp_ref[...] - delta)).astype(BF16)
        ds_ref[:, cols] = ds
        dq = (dot(kt, ds) * SCALE).T.astype(BF16)
        at = slice(g * HEAD, (g + 1) * HEAD)
        own_ref[:, at] = dq[:ROWS]
        cross_ref[:, at] = dq[ROWS:]
    for k in range(SLOTS):
        rows = pl.ds(k * PAIR, PAIR)
        parts[k][:, :HEAD] = (dot(ds_ref[rows, :], qs_ref[...]) * SCALE).astype(BF16)
        parts[k][:, HEAD:] = dot(p_ref[rows, :], gs_ref[...]).astype(BF16)


def window_scratch():
    return [
        pltpu.VMEM((KEYS, HEAD), BF16),
        pltpu.VMEM((KEYS, HEAD), BF16),
        pltpu.VMEM((KEYS, PAIR), F32),
        pltpu.VMEM((KEYS, PAIR), F32),
    ]


MATMUL = 2 * GROUP * PAIR * KEYS * HEAD


def run_fwd(where, query, crossed, blocks):
    halves = [shape(ROWS, HALF)] * 2
    return call(fwd_kernel, halves, 2 + SLOTS, window_scratch(), 2 * MATMUL, 2**21, "fwd")(
        where, query, crossed, *blocks
    )


def run_bwd(where, query, grad, crossed, blocks):
    outs = [shape(ROWS, HALF)] * 2 + [shape(PAIR, 2 * HEAD)] * SLOTS
    scratch = window_scratch() + [
        pltpu.VMEM((KEYS, PAIR), F32),
        pltpu.VMEM((KEYS, GROUP * PAIR), BF16),
        pltpu.VMEM((KEYS, GROUP * PAIR), BF16),
        pltpu.VMEM((GROUP * PAIR, HEAD), BF16),
        pltpu.VMEM((GROUP * PAIR, HEAD), BF16),
    ]
    out = call(bwd_kernel, outs, 3 + SLOTS, scratch, 5 * MATMUL, 2**22, "bwd")(
        where, query, grad, crossed, *blocks
    )
    return out[0], out[1], out[2:]


def along_z(block, distance):
    n = lax.axis_size("cp")
    return lax.ppermute(block, "cp", [(i, (i + 2 * distance) % n) for i in range(n)])


def swapped(block):
    return lax.ppermute(block, "cp", [(i, i ^ 1) for i in range(lax.axis_size("cp"))])


def handed(block, distance):
    n = lax.axis_size("section")
    return lax.ppermute(block, "section", [(i, (i + distance) % n) for i in range(n)])


def handed_across(block, distance):
    n, m = lax.axis_size("section"), lax.axis_size("cp")
    route = [
        (s * m + c, (s + distance) % n * m + (c ^ 1)) for s in range(n) for c in range(m)
    ]
    return lax.ppermute(block, ("section", "cp"), route)


def chain(block):
    blocks = [block]
    for _ in range(HOPS):
        blocks.append(along_z(blocks[-1], 1))
    return blocks


def per_device(qf, kf, vf, sf, qb, kb, vb, sb, grad):
    index = lax.axis_index("cp")
    side = index % 2
    where = jnp.stack([side, index // 2]).astype(jnp.int32)
    qf, kf, vf, qb, kb, vb, grad = (a[0] for a in (qf, kf, vf, qb, kb, vb, grad))
    keep, send = call(split_kernel, [shape(ROWS + TAIL, 4 * HEAD)] * 2, 6, name="split")(
        where, kb, vb, sb, kf, vf, sf
    )
    got = swapped(send)
    eb, ef = call(join_kernel, [shape(PAIR + TAIL, 2 * HEAD)] * 2, 2, name="join")(
        where, keep, got
    )
    blocks_b = chain(eb)
    (send_b,) = call(other_half_kernel, [shape(ROWS, 2 * HALF)], 2, name="half_b")(where, qb, grad)
    crossed_b = swapped(send_b)
    blocks_f = chain(ef)
    (send_f,) = call(other_half_kernel, [shape(ROWS, HALF)], 1, name="half_f")(where, qf)
    crossed_f = swapped(send_f)

    dq_own, dq_cross, parts = run_bwd(where, qb, grad, crossed_b, blocks_b)
    whole = [shape(ROWS, 2 * HALF)]
    (grad_query,) = call(whole_kernel, whole, 2, name="whole_dq")(
        where, handed(dq_own, -1), handed_across(dq_cross, -1)
    )
    o_own, o_cross = run_fwd(where, qf, crossed_f, blocks_f)
    (attn_out,) = call(whole_kernel, whole, 2, name="whole_o")(
        where, handed(o_own, 1), handed_across(o_cross, 1)
    )
    running = parts[HOPS]
    for k in range(HOPS - 1, -1, -1):
        total = parts[k].astype(F32) + along_z(running, -1).astype(F32)
        running = total.astype(BF16)
    mine = handed(running[:ROWS], -1)
    theirs = handed_across(running[ROWS:], -1)
    low = jnp.where(side == 0, mine, theirs)
    high = jnp.where(side == 0, theirs, mine)
    grad_key = jnp.concatenate([low[:, :HEAD], high[:, :HEAD]], axis=1)
    grad_value = jnp.concatenate([low[:, HEAD:], high[:, HEAD:]], axis=1)
    return attn_out[None], grad_query[None], grad_key[None], grad_value[None]


def solution(mesh):
    wide = P("section", "cp", "tp")
    flat = P("section", "cp")
    return jax.shard_map(
        per_device,
        mesh=mesh,
        in_specs=(wide, wide, wide, flat, wide, wide, wide, flat, wide),
        out_specs=(wide, wide, wide, wide),
        check_vma=False,
    )
```

time: 394 us -> 96.8 us (0.25)
  the two profiles are of different devices: /device:TPU:56 before, /device:TPU:4 now
where the time goes in v1:
time: 96.8 us; the launch traced here: 96.5 us
  waiting for transfers between devices  37 us (38%)
  starting transfers between devices  27.7 us (29%)
  Pallas kernels  23.7 us (24%)
  local copies, waits for them, and re-layouts  5.81 us (6%)
  other arithmetic  1.5 us (2%)
    ppermute x12, waiting for transfers between devices, along_z(): lax.ppermute(block, 'cp', [(i, (i + 2 * distance) % n) for i in range(n)])  29.8 us
    ppermute x12, starting transfers between devices, along_z(): lax.ppermute(block, 'cp', [(i, (i + 2 * distance) % n) for i in range(n)])  12.9 us
    pallas_call x1, Pallas kernels, run_bwd(): call(bwd_kernel, outs, 3 + SLOTS, scratch, 5 * MATMUL, 2 ** 22, 'bwd')  11.3 us
    ppermute x3, starting transfers between devices, handed(): lax.ppermute(block, 'section', [(i, (i + distance) % n) for i in range(n)])  7.85 us
    pallas_call x1, Pallas kernels, run_fwd(): call(fwd_kernel, halves, 2 + SLOTS, window_scratch(), 2 * MATMUL, 2 ** 21...  7.39 us
    unnamed x20, local copies, waits for them, and re-layouts  5.77 us
    ppermute x3, waiting for transfers between devices, swapped(): lax.ppermute(block, 'cp', [(i, i ^ 1) for i in range(lax.axis_size('cp'))])  4.4 us
    ppermute x3, starting transfers between devices, swapped(): lax.ppermute(block, 'cp', [(i, i ^ 1) for i in range(lax.axis_size('cp'))])  3.85 us
  transfers between devices with their start and end apart: 21, of which 10 were waited for; matrix products, arithmetic and copies ran while one was open for 0% of the time, Pallas kernels for 23%

profile of v1, /device:TPU:4, one launch (start us, length us, event | category | flops | bytes accessed | tf_op | source)
XLA Modules:
  0.0 96.5 jit_solution(4540299404443014194)
XLA Ops:
  0.6 0.0 copy-start
  0.7 0.1 pad_add_fusion.where_ref
  0.7 0.9 copy-done.4
  1.6 0.8 copy-done.5
  2.5 0.8 copy-done.6
  3.3 0.8 copy-done.7
  4.2 0.7 copy-done.8
  4.8 0.7 copy-done.9
  5.5 0.6 split.1
  6.1 1.3 %collective-permute-start.1 = (bf16[144,512]{1,0:T(8,128)(2,1)S(1)}, bf16[144,512]{1,0:T(8,128)(2,1)S(1)}, u32[]{:S(2)}, u32[]{:S(2)}) collective-permute-start(bf16[144,512]{1,0:T(8,128)(2,1)S(1)} %get-tuple-element.18), channel_id=1, source_target_pairs={{0,1},{1,0},{2,3},{3,2},{4,5},{5,4},{6,7},{7,6},{8,9},{9,8},{10,11... | collective-permute-start | bytes 442376 | tf_op jit(solution)/shard_map/ppermute | solution.py:221
  7.3 4.4 %collective-permute-done.1.got = bf16[144,512]{1,0:T(8,128)(2,1)S(1)} collective-permute-done((bf16[144,512]{1,0:T(8,128)(2,1)S(1)}, bf16[144,512]{1,0:T(8,128)(2,1)S(1)}, u32[]{:S(2)}, u32[]{:S(2)}) %collective-permute-start.1) | collective-permute-done | bytes 147488 | tf_op jit(solution)/shard_map/ppermute | solution.py:221
  11.7 0.6 join.1
  12.3 2.0 %collective-permute-start.9 = (bf16[272,256]{1,0:T(8,128)(2,1)S(1)}, bf16[272,256]{1,0:T(8,128)(2,1)S(1)}, u32[]{:S(2)}, u32[]{:S(2)}) collective-permute-start(bf16[272,256]{1,0:T(8,128)(2,1)S(1)} %get-tuple-element.22.refs_0_), channel_id=1, source_target_pairs={{0,2},{1,3},{2,4},{3,5},{4,6},{5,7},{6,8},{7,9},{8,10},{9,11},{10,... | collective-permute-start | bytes 417800 | tf_op jit(solution)/shard_map/ppermute | solution.py:217
  14.3 0.0 copy-done
  14.3 1.0 %copy-done.1 = bf16[1,128,2048]{2,1,0:T(8,128)(2,1)S(1)} copy-done((bf16[1,128,2048]{2,1,0:T(8,128)(2,1)S(1)}, bf16[1,128,2048]{2,1,0:T(8,128)(2,1)}, u32[]{:S(2)}) %copy-start.1) | copy-done | bytes 524312
  15.3 0.6 half_b.1
  15.9 1.3 %collective-permute-start.8 = (bf16[128,2048]{1,0:T(8,128)(2,1)S(1)}, bf16[128,2048]{1,0:T(8,128)(2,1)S(1)}, u32[]{:S(2)}, u32[]{:S(2)}) collective-permute-start(bf16[128,2048]{1,0:T(8,128)(2,1)S(1)} %half_b.1), channel_id=1, source_target_pairs={{0,1},{1,0},{2,3},{3,2},{4,5},{5,4},{6,7},{7,6},{8,9},{9,8},{10,11... | collective-permute-start | bytes 1572872 | tf_op jit(solution)/shard_map/ppermute | solution.py:221
  17.2 4.1 %collective-permute-done.9.refs_1_ = bf16[272,256]{1,0:T(8,128)(2,1)S(1)} collective-permute-done((bf16[272,256]{1,0:T(8,128)(2,1)S(1)}, bf16[272,256]{1,0:T(8,128)(2,1)S(1)}, u32[]{:S(2)}, u32[]{:S(2)}) %collective-permute-start.9) | collective-permute-done | bytes 139296 | tf_op jit(solution)/shard_map/ppermute | solution.py:217
  21.3 0.0 collective-permute-start.10
  21.3 6.3 %collective-permute-done.10.refs_2_ = bf16[272,256]{1,0:T(8,128)(2,1)S(1)} collective-permute-done((bf16[272,256]{1,0:T(8,128)(2,1)S(1)}, bf16[272,256]{1,0:T(8,128)(2,1)S(1)}, u32[]{:S(2)}, u32[]{:S(2)}) %collective-permute-start.10) | collective-permute-done | bytes 139296 | tf_op jit(solution)/shard_map/ppermute | solution.py:217
  27.5 0.0 collective-permute-start.11
  27.5 6.7 %collective-permute-done.11.refs_3_ = bf16[272,256]{1,0:T(8,128)(2,1)S(1)} collective-permute-done((bf16[272,256]{1,0:T(8,128)(2,1)S(1)}, bf16[272,256]{1,0:T(8,128)(2,1)S(1)}, u32[]{:S(2)}, u32[]{:S(2)}) %collective-permute-start.11) | collective-permute-done | bytes 139296 | tf_op jit(solution)/shard_map/ppermute | solution.py:217
  34.2 0.0 collective-permute-start.12
  34.2 0.0 collective-permute-start.2
  34.2 0.0 collective-permute-done.8.qdx_ref
  34.2 6.3 %collective-permute-done.12.refs_4_ = bf16[272,256]{1,0:T(8,128)(2,1)S(1)} collective-permute-done((bf16[272,256]{1,0:T(8,128)(2,1)S(1)}, bf16[272,256]{1,0:T(8,128)(2,1)S(1)}, u32[]{:S(2)}, u32[]{:S(2)}) %collective-permute-start.12) | collective-permute-done | bytes 139296 | tf_op jit(solution)/shard_map/ppermute | solution.py:217
  40.5 0.0 copy-done.2
  40.5 11.3 %bwd.1 = (bf16[128,1024]{1,0:T(8,128)(2,1)S(1)}, bf16[128,1024]{1,0:T(8,128)(2,1)S(1)}, bf16[256,256]{1,0:T(8,128)(2,1)S(1)}, bf16[256,256]{1,0:T(8,128)(2,1)S(1...) custom-call(s32[2]{0:T(128)S(1)} %pad_add_fusion.where_ref, ...), custom_call_target="tpu_custom_call" | custom-call | flops 3355443200 | bytes 4194304 | tf_op jit(solution)/shard_map/bwd/pallas_call | solution.py:209
  51.8 0.0 copy-start.3
  51.8 0.1 collective-permute-start.15
  51.9 0.0 collective-permute-done.2.refs_1_
  51.9 2.0 %collective-permute-start.3 = (bf16[272,256]{1,0:T(8,128)(2,1)S(1)}, bf16[272,256]{1,0:T(8,128)(2,1)S(1)}, u32[]{:S(2)}, u32[]{:S(2)}) collective-permute-start(bf16[272,256]{1,0:T(8,128)(2,1)S(1)} %collective-permute-done.2.refs_1_), channel_id=1, source_target_pairs={{0,2},{1,3},{2,4},{3,5},{4,6},{5,7},{6,8},{7,9},{8,10},{9,11},{10,... | collective-permute-start | bytes 417800 | tf_op jit(solution)/shard_map/ppermute | solution.py:217
  53.9 2.9 %collective-permute-done.15 = bf16[256,256]{1,0:T(8,128)(2,1)S(1)} collective-permute-done((bf16[256,256]{1,0:T(8,128)(2,1)S(1)}, bf16[256,256]{1,0:T(8,128)(2,1)S(1)}, u32[]{:S(2)}, u32[]{:S(2)}) %collective-permute-start.15) | collective-permute-done | bytes 131104 | tf_op jit(solution)/shard_map/ppermute | solution.py:217
  56.9 1.8 %collective-permute-start.16 = (bf16[256,256]{1,0:T(8,128)(2,1)S(1)}, bf16[256,256]{1,0:T(8,128)(2,1)S(1)}, u32[]{:S(2)}, u32[]{:S(2)}) collective-permute-start(bf16[256,256]{1,0:T(8,128)(2,1)S(1)} %add_convert_fusion.3), channel_id=1, source_target_pairs={{0,14},{1,15},{2,0},{3,1},{4,2},{5,3},{6,4},{7,5},{8,6},{9,7},{10,... | collective-permute-start | bytes 393224 | tf_op jit(solution)/shard_map/ppermute | solution.py:217
  58.7 0.1 collective-permute-done.3.refs_2_
  58.7 0.2 collective-permute-start.4
  59.0 2.9 %collective-permute-done.16 = bf16[256,256]{1,0:T(8,128)(2,1)S(1)} collective-permute-done((bf16[256,256]{1,0:T(8,128)(2,1)S(1)}, bf16[256,256]{1,0:T(8,128)(2,1)S(1)}, u32[]{:S(2)}, u32[]{:S(2)}) %collective-permute-start.16) | collective-permute-done | bytes 131104 | tf_op jit(solution)/shard_map/ppermute | solution.py:217
  61.9 3.0 %collective-permute-start.17 = (bf16[256,256]{1,0:T(8,128)(2,1)S(1)}, bf16[256,256]{1,0:T(8,128)(2,1)S(1)}, u32[]{:S(2)}, u32[]{:S(2)}) collective-permute-start(bf16[256,256]{1,0:T(8,128)(2,1)S(1)} %add_convert_fusion.2), channel_id=1, source_target_pairs={{0,14},{1,15},{2,0},{3,1},{4,2},{5,3},{6,4},{7,5},{8,6},{9,7},{10,... | collective-permute-start | bytes 393224 | tf_op jit(solution)/shard_map/ppermute | solution.py:217
  65.0 0.6 half_f.1
  65.5 1.3 %collective-permute-start = (bf16[128,1024]{1,0:T(8,128)(2,1)S(1)}, bf16[128,1024]{1,0:T(8,128)(2,1)S(1)}, u32[]{:S(2)}, u32[]{:S(2)}) collective-permute-start(bf16[128,1024]{1,0:T(8,128)(2,1)S(1)} %half_f.1), channel_id=1, source_target_pairs={{0,1},{1,0},{2,3},{3,2},{4,5},{5,4},{6,7},{7,6},{8,9},{9,8},{10,11... | collective-permute-start | bytes 786440 | tf_op jit(solution)/shard_map/ppermute | solution.py:221
  66.8 0.0 collective-permute-done.4.refs_3_
  66.8 0.0 collective-permute-start.5
  66.8 0.7 collective-permute-done.17
  67.5 3.7 %collective-permute-start.18 = (bf16[256,256]{1,0:T(8,128)(2,1)S(1)}, bf16[256,256]{1,0:T(8,128)(2,1)S(1)}, u32[]{:S(2)}, u32[]{:S(2)}) collective-permute-start(bf16[256,256]{1,0:T(8,128)(2,1)S(1)} %add_convert_fusion.1), channel_id=1, source_target_pairs={{0,14},{1,15},{2,0},{3,1},{4,2},{5,3},{6,4},{7,5},{8,6},{9,7},{10,... | collective-permute-start | bytes 393224 | tf_op jit(solution)/shard_map/ppermute | solution.py:217
  71.2 3.0 %collective-permute-start.13 = (bf16[128,1024]{1,0:T(8,128)(2,1)S(1)}, bf16[128,1024]{1,0:T(8,128)(2,1)S(1)}, u32[]{:S(2)}, u32[]{:S(2)}) collective-permute-start(bf16[128,1024]{1,0:T(8,128)(2,1)S(1)} %get-tuple-element.23), channel_id=1, source_target_pairs={{0,192},{64,0},{128,64},{192,128},{1,193},{65,1},{129,65},{193,129... | collective-permute-start | bytes 786440 | tf_op jit(solution)/shard_map/ppermute | solution.py:226
  74.3 1.4 %collective-permute-start.14 = (bf16[128,1024]{1,0:T(8,128)(2,1)S(1)}, bf16[128,1024]{1,0:T(8,128)(2,1)S(1)}, u32[]{:S(2)}, u32[]{:S(2)}) collective-permute-start(bf16[128,1024]{1,0:T(8,128)(2,1)S(1)} %get-tuple-element.24), channel_id=1, source_target_pairs={{0,193},{1,192},{2,195},{3,194},{4,197},{5,196},{6,199},{7,198},{8... | collective-permute-start | bytes 786440 | tf_op jit(solution)/shard_map/ppermute | solution.py:234
  75.6 0.0 collective-permute-done.qx_ref
  75.6 0.0 collective-permute-done.5.refs_4_
  75.6 7.4 %fwd.1 = (bf16[128,1024]{1,0:T(8,128)(2,1)S(1)}, bf16[128,1024]{1,0:T(8,128)(2,1)S(1)}) custom-call(s32[2]{0:T(128)S(1)} %pad_add_fusion.where_ref, bf16[128,2048]{1,0:T(8,128)(2,1)S(1)} %bitcast.20, bf16[128,1024]{1,0:T(8,128)(2,1)S(1)} %collective-permute-done.qx_ref, bf16[272,256]{1,0:T(8,128)(2,1)S(1)} %get-tuple-element.19.refs_0_, ...), custom_call_target="tpu_custom_call" | custom-call | flops 1342177280 | bytes 2097152 | tf_op jit(solution)/shard_map/fwd/pallas_call | solution.py:195
  83.0 1.6 %collective-permute-start.6 = (bf16[128,1024]{1,0:T(8,128)(2,1)S(1)}, bf16[128,1024]{1,0:T(8,128)(2,1)S(1)}, u32[]{:S(2)}, u32[]{:S(2)}) collective-permute-start(bf16[128,1024]{1,0:T(8,128)(2,1)S(1)} %get-tuple-element.20), channel_id=1, source_target_pairs={{0,64},{64,128},{128,192},{192,0},{1,65},{65,129},{129,193},{193,1... | collective-permute-start | bytes 786440 | tf_op jit(solution)/shard_map/ppermute | solution.py:226
  84.7 0.4 collective-permute-start.7
  85.0 0.0 collective-permute-done.18
  85.1 3.2 %collective-permute-start.19 = (bf16[128,256]{1,0:T(8,128)(2,1)S(1)}, bf16[128,256]{1,0:T(8,128)(2,1)S(1)}, u32[]{:S(2)}, u32[]{:S(2)}) collective-permute-start(bf16[128,256]{1,0:T(8,128)(2,1)S(1)} %get-tuple-element.32), channel_id=1, source_target_pairs={{0,192},{64,0},{128,64},{192,128},{1,193},{65,1},{129,65},{193,129... | collective-permute-start | bytes 196616 | tf_op jit(solution)/shard_map/ppermute | solution.py:226
  88.3 0.0 collective-permute-done.13.own
  88.3 1.4 %collective-permute-start.20 = (bf16[128,256]{1,0:T(8,128)(2,1)S(1)}, bf16[128,256]{1,0:T(8,128)(2,1)S(1)}, u32[]{:S(2)}, u32[]{:S(2)}) collective-permute-start(bf16[128,256]{1,0:T(8,128)(2,1)S(1)} %get-tuple-element.33), channel_id=1, source_target_pairs={{0,193},{1,192},{2,195},{3,194},{4,197},{5,196},{6,199},{7,198},{8... | collective-permute-start | bytes 196616 | tf_op jit(solution)/shard_map/ppermute | solution.py:234
  89.7 0.0 collective-permute-done.14.cross
  89.7 1.4 %whole_dq.1 = bf16[128,2048]{1,0:T(8,128)(2,1)} custom-call(s32[2]{0:T(128)S(1)} %pad_add_fusion.where_ref, bf16[128,1024]{1,0:T(8,128)(2,1)S(1)} %collective-permute-done.13.own, bf16[128,1024]{1,0:T(8,128)(2,1)S(1)} %collective-permute-done.14.cross), custom_call_target="tpu_custom_call" | custom-call | bytes 524288 | tf_op jit(solution)/shard_map/whole_dq/pallas_call | solution.py:265
  91.1 2.7 %collective-permute-done.6.own = bf16[128,1024]{1,0:T(8,128)(2,1)S(1)} collective-permute-done((bf16[128,1024]{1,0:T(8,128)(2,1)S(1)}, bf16[128,1024]{1,0:T(8,128)(2,1)S(1)}, u32[]{:S(2)}, u32[]{:S(2)}) %collective-permute-start.6) | collective-permute-done | bytes 262176 | tf_op jit(solution)/shard_map/ppermute | solution.py:226
  93.8 0.0 collective-permute-done.7.cross
  93.8 1.4 %whole_o.1 = bf16[128,2048]{1,0:T(8,128)(2,1)} custom-call(s32[2]{0:T(128)S(1)} %pad_add_fusion.where_ref, bf16[128,1024]{1,0:T(8,128)(2,1)S(1)} %collective-permute-done.6.own, bf16[128,1024]{1,0:T(8,128)(2,1)S(1)} %collective-permute-done.7.cross), custom_call_target="tpu_custom_call" | custom-call | bytes 524288 | tf_op jit(solution)/shard_map/whole_o/pallas_call | solution.py:269
  95.2 0.0 collective-permute-done.19
  95.2 0.0 collective-permute-done.20
  95.2 0.6 maximum_bitcast_fusion.1
  95.9 0.6 maximum_bitcast_fusion
  (16 shorter events, 0.2 us)
Async XLA Ops:
  0.6 13.7 %copy-start = (bf16[1,128,2048]{2,1,0:T(8,128)(2,1)S(1)}, bf16[1,128,2048]{2,1,0:T(8,128)(2,1)}, u32[]{:S(2)}) copy-start(bf16[1,128,2048]{2,1,0:T(8,128)(2,1)} %param.13) | copy-start | bytes 1572868
  0.7 0.9 copy-start.4
  1.6 0.8 copy-start.5
  2.5 0.8 copy-start.6
  3.3 0.8 copy-start.7
  4.1 0.7 copy-start.8
  4.8 0.7 copy-start.9
  6.1 5.7 %collective-permute-start.1 = (bf16[144,512]{1,0:T(8,128)(2,1)S(1)}, bf16[144,512]{1,0:T(8,128)(2,1)S(1)}, u32[]{:S(2)}, u32[]{:S(2)}) collective-permute-start(bf16[144,512]{1,0:T(8,128)(2,1)S(1)} %get-tuple-element.18), channel_id=1, source_target_pairs={{0,1},{1,0},{2,3},{3,2},{4,5},{5,4},{6,7},{7,6},{8,9},{9,8},{10,11... | collective-permute-start | bytes 442376 | tf_op jit(solution)/shard_map/ppermute | solution.py:221
  12.3 9.0 %collective-permute-start.9 = (bf16[272,256]{1,0:T(8,128)(2,1)S(1)}, bf16[272,256]{1,0:T(8,128)(2,1)S(1)}, u32[]{:S(2)}, u32[]{:S(2)}) collective-permute-start(bf16[272,256]{1,0:T(8,128)(2,1)S(1)} %get-tuple-element.22.refs_0_), channel_id=1, source_target_pairs={{0,2},{1,3},{2,4},{3,5},{4,6},{5,7},{6,8},{7,9},{8,10},{9,11},{10,... | collective-permute-start | bytes 417800 | tf_op jit(solution)/shard_map/ppermute | solution.py:217
  14.3 1.0 %copy-start.1 = (bf16[1,128,2048]{2,1,0:T(8,128)(2,1)S(1)}, bf16[1,128,2048]{2,1,0:T(8,128)(2,1)}, u32[]{:S(2)}) copy-start(bf16[1,128,2048]{2,1,0:T(8,128)(2,1)} %param.17) | copy-start | bytes 1572868
  15.3 25.1 %copy-start.2 = (bf16[1,128,2048]{2,1,0:T(8,128)(2,1)S(1)}, bf16[1,128,2048]{2,1,0:T(8,128)(2,1)}, u32[]{:S(2)}) copy-start(bf16[1,128,2048]{2,1,0:T(8,128)(2,1)} %param.17) | copy-start | bytes 1572868
  15.9 18.3 %collective-permute-start.8 = (bf16[128,2048]{1,0:T(8,128)(2,1)S(1)}, bf16[128,2048]{1,0:T(8,128)(2,1)S(1)}, u32[]{:S(2)}, u32[]{:S(2)}) collective-permute-start(bf16[128,2048]{1,0:T(8,128)(2,1)S(1)} %half_b.1), channel_id=1, source_target_pairs={{0,1},{1,0},{2,3},{3,2},{4,5},{5,4},{6,7},{7,6},{8,9},{9,8},{10,11... | collective-permute-start | bytes 1572872 | tf_op jit(solution)/shard_map/ppermute | solution.py:221
  21.3 6.3 %collective-permute-start.10 = (bf16[272,256]{1,0:T(8,128)(2,1)S(1)}, bf16[272,256]{1,0:T(8,128)(2,1)S(1)}, u32[]{:S(2)}, u32[]{:S(2)}) collective-permute-start(bf16[272,256]{1,0:T(8,128)(2,1)S(1)} %collective-permute-done.9.refs_1_), channel_id=1, source_target_pairs={{0,2},{1,3},{2,4},{3,5},{4,6},{5,7},{6,8},{7,9},{8,10},{9,11},{10,... | collective-permute-start | bytes 417800 | tf_op jit(solution)/shard_map/ppermute | solution.py:217
  27.5 6.7 %collective-permute-start.11 = (bf16[272,256]{1,0:T(8,128)(2,1)S(1)}, bf16[272,256]{1,0:T(8,128)(2,1)S(1)}, u32[]{:S(2)}, u32[]{:S(2)}) collective-permute-start(bf16[272,256]{1,0:T(8,128)(2,1)S(1)} %collective-permute-done.10.refs_2_), channel_id=1, source_target_pairs={{0,2},{1,3},{2,4},{3,5},{4,6},{5,7},{6,8},{7,9},{8,10},{9,11},{10,... | collective-permute-start | bytes 417800 | tf_op jit(solution)/shard_map/ppermute | solution.py:217
  34.2 6.3 %collective-permute-start.12 = (bf16[272,256]{1,0:T(8,128)(2,1)S(1)}, bf16[272,256]{1,0:T(8,128)(2,1)S(1)}, u32[]{:S(2)}, u32[]{:S(2)}) collective-permute-start(bf16[272,256]{1,0:T(8,128)(2,1)S(1)} %collective-permute-done.11.refs_3_), channel_id=1, source_target_pairs={{0,2},{1,3},{2,4},{3,5},{4,6},{5,7},{6,8},{7,9},{8,10},{9,11},{10,... | collective-permute-start | bytes 417800 | tf_op jit(solution)/shard_map/ppermute | solution.py:217
  34.2 17.7 %collective-permute-start.2 = (bf16[272,256]{1,0:T(8,128)(2,1)S(1)}, bf16[272,256]{1,0:T(8,128)(2,1)S(1)}, u32[]{:S(2)}, u32[]{:S(2)}) collective-permute-start(bf16[272,256]{1,0:T(8,128)(2,1)S(1)} %get-tuple-element.19.refs_0_), channel_id=1, source_target_pairs={{0,2},{1,3},{2,4},{3,5},{4,6},{5,7},{6,8},{7,9},{8,10},{9,11},{10,... | collective-permute-start | bytes 417800 | tf_op jit(solution)/shard_map/ppermute | solution.py:217
  51.8 13.2 %copy-start.3 = (bf16[1,128,2048]{2,1,0:T(8,128)(2,1)S(1)}, bf16[1,128,2048]{2,1,0:T(8,128)(2,1)}, u32[]{:S(2)}) copy-start(bf16[1,128,2048]{2,1,0:T(8,128)(2,1)} %param.9) | copy-start | bytes 1572868
  51.8 5.0 %collective-permute-start.15 = (bf16[256,256]{1,0:T(8,128)(2,1)S(1)}, bf16[256,256]{1,0:T(8,128)(2,1)S(1)}, u32[]{:S(2)}, u32[]{:S(2)}) collective-permute-start(bf16[256,256]{1,0:T(8,128)(2,1)S(1)} %get-tuple-element.29), channel_id=1, source_target_pairs={{0,14},{1,15},{2,0},{3,1},{4,2},{5,3},{6,4},{7,5},{8,6},{9,7},{10,... | collective-permute-start | bytes 393224 | tf_op jit(solution)/shard_map/ppermute | solution.py:217
  51.9 6.9 %collective-permute-start.3 = (bf16[272,256]{1,0:T(8,128)(2,1)S(1)}, bf16[272,256]{1,0:T(8,128)(2,1)S(1)}, u32[]{:S(2)}, u32[]{:S(2)}) collective-permute-start(bf16[272,256]{1,0:T(8,128)(2,1)S(1)} %collective-permute-done.2.refs_1_), channel_id=1, source_target_pairs={{0,2},{1,3},{2,4},{3,5},{4,6},{5,7},{6,8},{7,9},{8,10},{9,11},{10,... | collective-permute-start | bytes 417800 | tf_op jit(solution)/shard_map/ppermute | solution.py:217
  56.9 5.0 %collective-permute-start.16 = (bf16[256,256]{1,0:T(8,128)(2,1)S(1)}, bf16[256,256]{1,0:T(8,128)(2,1)S(1)}, u32[]{:S(2)}, u32[]{:S(2)}) collective-permute-start(bf16[256,256]{1,0:T(8,128)(2,1)S(1)} %add_convert_fusion.3), channel_id=1, source_target_pairs={{0,14},{1,15},{2,0},{3,1},{4,2},{5,3},{6,4},{7,5},{8,6},{9,7},{10,... | collective-permute-start | bytes 393224 | tf_op jit(solution)/shard_map/ppermute | solution.py:217
  58.7 8.1 %collective-permute-start.4 = (bf16[272,256]{1,0:T(8,128)(2,1)S(1)}, bf16[272,256]{1,0:T(8,128)(2,1)S(1)}, u32[]{:S(2)}, u32[]{:S(2)}) collective-permute-start(bf16[272,256]{1,0:T(8,128)(2,1)S(1)} %collective-permute-done.3.refs_2_), channel_id=1, source_target_pairs={{0,2},{1,3},{2,4},{3,5},{4,6},{5,7},{6,8},{7,9},{8,10},{9,11},{10,... | collective-permute-start | bytes 417800 | tf_op jit(solution)/shard_map/ppermute | solution.py:217
  61.9 5.5 %collective-permute-start.17 = (bf16[256,256]{1,0:T(8,128)(2,1)S(1)}, bf16[256,256]{1,0:T(8,128)(2,1)S(1)}, u32[]{:S(2)}, u32[]{:S(2)}) collective-permute-start(bf16[256,256]{1,0:T(8,128)(2,1)S(1)} %add_convert_fusion.2), channel_id=1, source_target_pairs={{0,14},{1,15},{2,0},{3,1},{4,2},{5,3},{6,4},{7,5},{8,6},{9,7},{10,... | collective-permute-start | bytes 393224 | tf_op jit(solution)/shard_map/ppermute | solution.py:217
  65.5 10.1 %collective-permute-start = (bf16[128,1024]{1,0:T(8,128)(2,1)S(1)}, bf16[128,1024]{1,0:T(8,128)(2,1)S(1)}, u32[]{:S(2)}, u32[]{:S(2)}) collective-permute-start(bf16[128,1024]{1,0:T(8,128)(2,1)S(1)} %half_f.1), channel_id=1, source_target_pairs={{0,1},{1,0},{2,3},{3,2},{4,5},{5,4},{6,7},{7,6},{8,9},{9,8},{10,11... | collective-permute-start | bytes 786440 | tf_op jit(solution)/shard_map/ppermute | solution.py:221
  66.8 8.8 %collective-permute-start.5 = (bf16[272,256]{1,0:T(8,128)(2,1)S(1)}, bf16[272,256]{1,0:T(8,128)(2,1)S(1)}, u32[]{:S(2)}, u32[]{:S(2)}) collective-permute-start(bf16[272,256]{1,0:T(8,128)(2,1)S(1)} %collective-permute-done.4.refs_3_), channel_id=1, source_target_pairs={{0,2},{1,3},{2,4},{3,5},{4,6},{5,7},{6,8},{7,9},{8,10},{9,11},{10,... | collective-permute-start | bytes 417800 | tf_op jit(solution)/shard_map/ppermute | solution.py:217
  67.5 17.5 %collective-permute-start.18 = (bf16[256,256]{1,0:T(8,128)(2,1)S(1)}, bf16[256,256]{1,0:T(8,128)(2,1)S(1)}, u32[]{:S(2)}, u32[]{:S(2)}) collective-permute-start(bf16[256,256]{1,0:T(8,128)(2,1)S(1)} %add_convert_fusion.1), channel_id=1, source_target_pairs={{0,14},{1,15},{2,0},{3,1},{4,2},{5,3},{6,4},{7,5},{8,6},{9,7},{10,... | collective-permute-start | bytes 393224 | tf_op jit(solution)/shard_map/ppermute | solution.py:217
  71.2 17.1 %collective-permute-start.13 = (bf16[128,1024]{1,0:T(8,128)(2,1)S(1)}, bf16[128,1024]{1,0:T(8,128)(2,1)S(1)}, u32[]{:S(2)}, u32[]{:S(2)}) collective-permute-start(bf16[128,1024]{1,0:T(8,128)(2,1)S(1)} %get-tuple-element.23), channel_id=1, source_target_pairs={{0,192},{64,0},{128,64},{192,128},{1,193},{65,1},{129,65},{193,129... | collective-permute-start | bytes 786440 | tf_op jit(solution)/shard_map/ppermute | solution.py:226
  74.3 15.4 %collective-permute-start.14 = (bf16[128,1024]{1,0:T(8,128)(2,1)S(1)}, bf16[128,1024]{1,0:T(8,128)(2,1)S(1)}, u32[]{:S(2)}, u32[]{:S(2)}) collective-permute-start(bf16[128,1024]{1,0:T(8,128)(2,1)S(1)} %get-tuple-element.24), channel_id=1, source_target_pairs={{0,193},{1,192},{2,195},{3,194},{4,197},{5,196},{6,199},{7,198},{8... | collective-permute-start | bytes 786440 | tf_op jit(solution)/shard_map/ppermute | solution.py:234
  83.0 10.7 %collective-permute-start.6 = (bf16[128,1024]{1,0:T(8,128)(2,1)S(1)}, bf16[128,1024]{1,0:T(8,128)(2,1)S(1)}, u32[]{:S(2)}, u32[]{:S(2)}) collective-permute-start(bf16[128,1024]{1,0:T(8,128)(2,1)S(1)} %get-tuple-element.20), channel_id=1, source_target_pairs={{0,64},{64,128},{128,192},{192,0},{1,65},{65,129},{129,193},{193,1... | collective-permute-start | bytes 786440 | tf_op jit(solution)/shard_map/ppermute | solution.py:226
  84.7 9.1 %collective-permute-start.7 = (bf16[128,1024]{1,0:T(8,128)(2,1)S(1)}, bf16[128,1024]{1,0:T(8,128)(2,1)S(1)}, u32[]{:S(2)}, u32[]{:S(2)}) collective-permute-start(bf16[128,1024]{1,0:T(8,128)(2,1)S(1)} %get-tuple-element.21), channel_id=1, source_target_pairs={{0,65},{1,64},{2,67},{3,66},{4,69},{5,68},{6,71},{7,70},{8,73},{9,... | collective-permute-start | bytes 786440 | tf_op jit(solution)/shard_map/ppermute | solution.py:234
  85.1 10.1 %collective-permute-start.19 = (bf16[128,256]{1,0:T(8,128)(2,1)S(1)}, bf16[128,256]{1,0:T(8,128)(2,1)S(1)}, u32[]{:S(2)}, u32[]{:S(2)}) collective-permute-start(bf16[128,256]{1,0:T(8,128)(2,1)S(1)} %get-tuple-element.32), channel_id=1, source_target_pairs={{0,192},{64,0},{128,64},{192,128},{1,193},{65,1},{129,65},{193,129... | collective-permute-start | bytes 196616 | tf_op jit(solution)/shard_map/ppermute | solution.py:226
  88.3 6.9 %collective-permute-start.20 = (bf16[128,256]{1,0:T(8,128)(2,1)S(1)}, bf16[128,256]{1,0:T(8,128)(2,1)S(1)}, u32[]{:S(2)}, u32[]{:S(2)}) collective-permute-start(bf16[128,256]{1,0:T(8,128)(2,1)S(1)} %get-tuple-element.33), channel_id=1, source_target_pairs={{0,193},{1,192},{2,195},{3,194},{4,197},{5,196},{6,199},{7,198},{8... | collective-permute-start | bytes 196616 | tf_op jit(solution)/shard_map/ppermute | solution.py:234

commit v2 on v1

v2 whole, which is shorter than its diff:
```python
import functools
import math

import jax
import jax.numpy as jnp
from jax import lax
from jax.experimental import pallas as pl
from jax.experimental.pallas import tpu as pltpu
from jax.sharding import PartitionSpec as P

HEAD = 128
ROWS = 128
GROUP = 8
PAIR = 2 * ROWS
SLOTS = 5
KEYS = SLOTS * PAIR
DOCS = 4
TAIL = 16
HALF = GROUP * HEAD
SCALE = HEAD ** (-0.5)
SCALE2 = SCALE * math.log2(math.e)
F32 = jnp.float32
BF16 = jnp.bfloat16
NT = (((1,), (1,)), ((), ()))
VMEM = pl.BlockSpec(memory_space=pltpu.VMEM)
SMEM = pl.BlockSpec(memory_space=pltpu.SMEM)
ANY = pl.BlockSpec(memory_space=pl.ANY)
HBM = pl.BlockSpec(memory_space=pltpu.HBM)


def dot(a, b):
    return jnp.dot(a, b, preferred_element_type=F32)


def dot_nt(a, b):
    return lax.dot_general(a, b, NT, preferred_element_type=F32)


def call(kernel, outs, ins, scratch=(), flops=0, moved_bytes=2**19, name=None, place=VMEM, limit=4):
    return pl.pallas_call(
        kernel,
        out_shape=outs,
        in_specs=[SMEM] + ([VMEM] * ins if isinstance(ins, int) else ins),
        out_specs=[place] * len(outs),
        scratch_shapes=scratch,
        compiler_params=pltpu.CompilerParams(vmem_limit_bytes=limit * 2**20),
        cost_estimate=pl.CostEstimate(flops=flops, bytes_accessed=moved_bytes, transcendentals=0),
        name=name,
    )


def shape(*dims):
    return jax.ShapeDtypeStruct(dims, BF16)


def fetched(copies, sems):
    started = [pltpu.make_async_copy(a, b, sems.at[i]) for i, (a, b) in enumerate(copies)]
    for c in started:
        c.start()
    for c in started:
        c.wait()


def split_kernel(where_ref, *refs):
    side = where_ref[0]
    ins, (keep, send, keys, segs, sems) = refs[:6], refs[6:]
    copies = []
    for i in range(2):
        copies += [(ins[3 * i], keys.at[2 * i]), (ins[3 * i + 1], keys.at[2 * i + 1])]
        copies.append((ins[3 * i + 2], segs.at[i]))
    fetched(copies, sems)
    for at in range(4):
        cols = slice(at * HEAD, (at + 1) * HEAD)
        low, high = keys[at, :, :HEAD], keys[at, :, HEAD:]
        keep[:ROWS, cols] = jnp.where(side == 0, low, high)
        send[:ROWS, cols] = jnp.where(side == 0, high, low)
        row = jnp.broadcast_to(segs[at // 2].astype(F32).astype(BF16), (TAIL, ROWS))
        for out in (keep, send):
            out[ROWS:, cols] = row


def join_kernel(where_ref, keep, got, half_in, eb, ef, half_out):
    del where_ref, half_in, half_out
    for at, out in ((0, eb), (2, ef)):
        cols = slice(at * HEAD, (at + 2) * HEAD)
        one = slice(at * HEAD, (at + 1) * HEAD)
        out[:ROWS, :] = keep[:ROWS, cols]
        out[ROWS:PAIR, :] = got[:ROWS, cols]
        out[PAIR:, :HEAD] = keep[ROWS:, one]
        out[PAIR:, HEAD:] = got[ROWS:, one]


def other_half_kernel(where_ref, *refs, count):
    start = pl.multiple_of((1 - where_ref[0]) * HALF, HALF)
    ins, out, sems = refs[:count], refs[-2], refs[-1]
    fetched(
        [
            (ref.at[:, pl.ds(start, HALF)], out.at[:, at * HALF : (at + 1) * HALF])
            for at, ref in enumerate(ins)
        ],
        sems,
    )


def total_kernel(where_ref, *refs):
    del where_ref
    own, cross = refs[-2:]
    for i, out in enumerate((own, cross)):
        rows = pl.ds(i * ROWS, ROWS)
        out[...] = sum(r[rows, :].astype(F32) for r in refs[:SLOTS]).astype(BF16)


def final_kernel(where_ref, *refs):
    side = where_ref[0]
    ins, (o, dq, dk, dv), sems = refs[:6], refs[6:10], refs[10]
    copies = []
    for i, at in enumerate((side, 1 - side)):
        wide = pl.ds(pl.multiple_of(at * HALF, HALF), HALF)
        head = pl.ds(pl.multiple_of(at * HEAD, HEAD), HEAD)
        copies.append((ins[i], o.at[:, wide]))
        copies.append((ins[2 + i], dq.at[:, wide]))
        copies.append((ins[4 + i].at[:, :HEAD], dk.at[:, head]))
        copies.append((ins[4 + i].at[:, HEAD:], dv.at[:, head]))
    fetched(copies, sems)


def fill_cap(where_ref, blocks, cap):
    side, depth = where_ref[0], where_ref[1]
    segs = [b[PAIR : PAIR + 1, :].astype(F32) for b in blocks]
    start = jnp.zeros((1, PAIR), F32)
    for d in range(DOCS):
        first = jnp.sum((segs[0] < d).astype(F32), axis=1, keepdims=True)
        for k in range(1, SLOTS):
            same = jnp.sum((segs[k] == d).astype(F32), axis=1, keepdims=True)
            first = first - jnp.where(depth >= k, same, 0.0)
        start = jnp.where(segs[0] == d, first, start)
    start = start.astype(jnp.int32)
    lane = lax.broadcasted_iota(jnp.int32, (ROWS, PAIR), 1)
    row = jnp.where(lane < ROWS, lane + side * ROWS, lane - side * ROWS)
    for k in range(SLOTS):
        for part in range(2):
            block = side if part == 0 else 1 - side
            key = lax.broadcasted_iota(jnp.int32, (ROWS, PAIR), 0) + (block * ROWS - k * PAIR)
            seen = (key >= start) & (key <= row)
            cap[pl.ds(k * PAIR + part * ROWS, ROWS), :] = jnp.where(seen, 3.0e38, -jnp.inf)


def slot(k):
    return slice(k * PAIR, (k + 1) * PAIR)


def folded(x, reduce):
    return reduce(x.reshape(PAIR // 8, 8, PAIR), axis=0)


def joined(running, new, op):
    return new if running is None else op(running, new)


def score_slot(k, lanes, keys, turned, cap, s_ref):
    masked = jnp.minimum(dot(keys, turned), cap[slot(k), :])
    s_ref[slot(k), lanes] = masked
    return folded(masked, jnp.max)


def exponentials(k, lanes, s_ref, peak):
    return jnp.exp2((s_ref[slot(k), lanes] - peak) * SCALE2)


def head_rows(own, crossed, g, offset=0):
    at = slice(g * HEAD, (g + 1) * HEAD)
    far = slice(offset + g * HEAD, offset + (g + 1) * HEAD)
    return jnp.concatenate([own[:, at], crossed[:, far]], axis=0)


def put_rows(g, columns, own, crossed):
    rows = columns.T.astype(BF16)
    at = slice(g * HEAD, (g + 1) * HEAD)
    own[:, at] = rows[:ROWS]
    crossed[:, at] = rows[ROWS:]


ALL = slice(0, PAIR)


def fwd_kernel(where_ref, q_hbm, qx_ref, *refs):
    blocks, refs = refs[:SLOTS], refs[SLOTS + 1 :]
    o_own, o_cross, cap, s_ref, e_ref, vt_ref, q_ref, turned, sems = refs
    base = pl.multiple_of(where_ref[0] * HALF, HALF)
    fetch = pltpu.make_async_copy(q_hbm.at[:, pl.ds(base, HALF)], q_ref, sems.at[0])
    fetch.start()
    fill_cap(where_ref, blocks, cap)
    for k, b in enumerate(blocks):
        vt_ref[:, slot(k)] = b[:PAIR, HEAD:].T
    fetch.wait()

    def turn(g):
        turned[g % 2] = head_rows(q_ref, qx_ref, g).T

    peak = None
    turn(0)
    for k in range(SLOTS):
        peak = joined(peak, score_slot(k, ALL, blocks[k][:PAIR, :HEAD], turned[0], cap, s_ref.at[0]), jnp.maximum)
    for g in range(GROUP):
        now, later = g % 2, (g + 1) % 2
        top = jnp.max(peak, axis=0, keepdims=True)
        peak = total = None
        if g + 1 < GROUP:
            turn(g + 1)
        for k in range(SLOTS):
            expo = exponentials(k, ALL, s_ref.at[now], top)
            e_ref[now, slot(k), :] = expo.astype(BF16)
            total = joined(total, folded(expo, jnp.sum), jnp.add)
            if g + 1 < GROUP:
                new = score_slot(k, ALL, blocks[k][:PAIR, :HEAD], turned[later], cap, s_ref.at[later])
                peak = joined(peak, new, jnp.maximum)
        inv = 1.0 / jnp.sum(total, axis=0, keepdims=True)
        put_rows(g, dot(vt_ref[...], e_ref[now]) * inv, o_own, o_cross)


def bwd_kernel(where_ref, q_hbm, d_hbm, qdx_ref, *refs):
    blocks, refs = refs[:SLOTS], refs[SLOTS:]
    dq_own, dq_cross = refs[:2]
    parts, refs = refs[2 : SLOTS + 2], refs[SLOTS + 2 :]
    cap, s_ref, dp_ref, e_ref, ds_ref, qs_ref, gs_ref, acc, kt_ref, qd_ref, turned, sems = refs
    base = pl.multiple_of(where_ref[0] * HALF, HALF)
    fetch = [
        pltpu.make_async_copy(h.at[:, pl.ds(base, HALF)], qd_ref.at[i], sems.at[i])
        for i, h in enumerate((q_hbm, d_hbm))
    ]
    for c in fetch:
        c.start()
    fill_cap(where_ref, blocks, cap)
    for k, b in enumerate(blocks):
        kt_ref[:, slot(k)] = b[:PAIR, :HEAD].T
    for c in fetch:
        c.wait()

    def span_of(g):
        return slice(g * PAIR, (g + 1) * PAIR)

    def key_terms(k, span, last):
        dk = dot(ds_ref[slot(k), span], qs_ref[span, :])
        dv = dot(e_ref[slot(k), span], gs_ref[span, :])
        if last:
            parts[k][:, :HEAD] = ((dk + acc[0, slot(k), :]) * SCALE).astype(BF16)
            parts[k][:, HEAD:] = (dv + acc[1, slot(k), :]).astype(BF16)
        else:
            acc[0, slot(k), :] = dk
            acc[1, slot(k), :] = dv

    def query_terms(g, inv):
        put_rows(g, dot(kt_ref[...], ds_ref[:, span_of(g)]) * (inv * SCALE), dq_own, dq_cross)

    half = GROUP // 2
    first, second = slice(0, half * PAIR), slice(half * PAIR, GROUP * PAIR)

    def turn(g):
        turned[g % 2, 0] = head_rows(qd_ref.at[0], qdx_ref, g).T
        turned[g % 2, 1] = head_rows(qd_ref.at[1], qdx_ref, g, HALF).T

    peak = None
    turn(0)
    for k in range(SLOTS):
        peak = joined(peak, score_slot(k, ALL, blocks[k][:PAIR, :HEAD], turned[0, 0], cap, s_ref.at[0]), jnp.maximum)
    for g in range(GROUP):
        now, later = g % 2, (g + 1) % 2
        cols = span_of(g)
        top = jnp.max(peak, axis=0, keepdims=True)
        peak = total = inner = None
        for k in range(SLOTS):
            expo = exponentials(k, ALL, s_ref.at[now], top)
            dp = dot(blocks[k][:PAIR, HEAD:], turned[now, 1])
            e_ref[slot(k), cols] = expo.astype(BF16)
            dp_ref[now, slot(k), :] = dp
            total = joined(total, folded(expo, jnp.sum), jnp.add)
            inner = joined(inner, folded(expo * dp, jnp.sum), jnp.add)
            if k == 0 and g > 0:
                query_terms(g - 1, inv)
        inv = 1.0 / jnp.sum(total, axis=0, keepdims=True)
        delta = jnp.sum(inner, axis=0, keepdims=True) * inv
        factor = jnp.broadcast_to(inv, (HEAD, PAIR)).T
        qs_ref[cols, :] = (head_rows(qd_ref.at[0], qdx_ref, g).astype(F32) * factor).astype(BF16)
        gs_ref[cols, :] = (head_rows(qd_ref.at[1], qdx_ref, g, HALF).astype(F32) * factor).astype(BF16)
        if g + 1 < GROUP:
            turn(g + 1)
        for k in range(SLOTS):
            ds = (dp_ref[now, slot(k), :] - delta).astype(BF16)
            ds_ref[slot(k), cols] = e_ref[slot(k), cols] * ds
            if g + 1 < GROUP:
                new = score_slot(k, ALL, blocks[k][:PAIR, :HEAD], turned[later, 0], cap, s_ref.at[later])
                peak = joined(peak, new, jnp.maximum)
        if g >= half:
            for k in (2 * (g - half), 2 * (g - half) + 1):
                if k < SLOTS:
                    key_terms(k, first, False)
    query_terms(GROUP - 1, inv)
    for k in range(SLOTS):
        key_terms(k, second, True)


MATMUL = 2 * GROUP * PAIR * KEYS * HEAD


def run_fwd(where, query, crossed, blocks, after):
    scratch = [
        pltpu.VMEM((KEYS, PAIR), F32),
        pltpu.VMEM((2, KEYS, PAIR), F32),
        pltpu.VMEM((2, KEYS, PAIR), BF16),
        pltpu.VMEM((HEAD, KEYS), BF16),
        pltpu.VMEM((ROWS, HALF), BF16),
        pltpu.VMEM((2, HEAD, PAIR), BF16),
        pltpu.SemaphoreType.DMA((1,)),
    ]
    return call(
        fwd_kernel,
        [shape(ROWS, HALF)] * 2,
        [HBM] + [VMEM] * (1 + SLOTS) + [ANY] * 1,
        scratch,
        2 * MATMUL,
        2**21,
        "fwd",
        limit=20,
    )(where, query, crossed, *blocks, *after)


def run_bwd(where, query, grad, crossed, blocks):
    outs = [shape(ROWS, HALF)] * 2 + [shape(PAIR, 2 * HEAD)] * SLOTS
    scratch = [
        pltpu.VMEM((KEYS, PAIR), F32),
        pltpu.VMEM((2, KEYS, PAIR), F32),
        pltpu.VMEM((2, KEYS, PAIR), F32),
        pltpu.VMEM((KEYS, GROUP * PAIR), BF16),
        pltpu.VMEM((KEYS, GROUP * PAIR), BF16),
        pltpu.VMEM((GROUP * PAIR, HEAD), BF16),
        pltpu.VMEM((GROUP * PAIR, HEAD), BF16),
        pltpu.VMEM((2, KEYS, HEAD), F32),
        pltpu.VMEM((HEAD, KEYS), BF16),
        pltpu.VMEM((2, ROWS, HALF), BF16),
        pltpu.VMEM((2, 2, HEAD, PAIR), BF16),
        pltpu.SemaphoreType.DMA((2,)),
    ]
    out = call(
        bwd_kernel,
        outs,
        [HBM] * 2 + [VMEM] * (1 + SLOTS),
        scratch,
        5 * MATMUL,
        2**22,
        "bwd",
        limit=32,
    )(where, query, grad, crossed, *blocks)
    return out[0], out[1], out[2:]


def along_z(block, distance):
    n = lax.axis_size("cp")
    return lax.ppermute(block, "cp", [(i, (i + 2 * distance) % n) for i in range(n)])


def swapped(block):
    return lax.ppermute(block, "cp", [(i, i ^ 1) for i in range(lax.axis_size("cp"))])


def handed(block, distance):
    n = lax.axis_size("section")
    return lax.ppermute(block, "section", [(i, (i + distance) % n) for i in range(n)])


def handed_across(block, distance):
    n, m = lax.axis_size("section"), lax.axis_size("cp")
    route = [
        (s * m + c, (s + distance) % n * m + (c ^ 1)) for s in range(n) for c in range(m)
    ]
    return lax.ppermute(block, ("section", "cp"), route)


def split(where, *arrays):
    scratch = [
        pltpu.VMEM((4, ROWS, 2 * HEAD), BF16),
        pltpu.VMEM((2, 1, ROWS), jnp.int32),
        pltpu.SemaphoreType.DMA((6,)),
    ]
    outs = [shape(ROWS + TAIL, 4 * HEAD)] * 2
    return call(split_kernel, outs, [HBM] * 6, scratch, name="split")(where, *arrays)


def join(where, keep, got, through):
    return pl.pallas_call(
        join_kernel,
        out_shape=[shape(PAIR + TAIL, 2 * HEAD)] * 2 + [shape(*through.shape)],
        in_specs=[SMEM] + [VMEM] * 2 + [ANY],
        out_specs=[VMEM] * 2 + [ANY],
        input_output_aliases={3: 2},
        compiler_params=pltpu.CompilerParams(vmem_limit_bytes=4 * 2**20),
        name="join",
    )(where, keep, got, through)


def tied_kernel(where_ref, held, after, out):
    del where_ref, held, after, out


def tied(where, held, after):
    return pl.pallas_call(
        tied_kernel,
        out_shape=shape(*held.shape),
        in_specs=[SMEM, ANY, ANY],
        out_specs=ANY,
        input_output_aliases={1: 0},
        compiler_params=pltpu.CompilerParams(vmem_limit_bytes=2**20),
        name="tied",
    )(where, held, after)


def other_half(where, arrays, after, name):
    (out,) = call(
        functools.partial(other_half_kernel, count=len(arrays)),
        [shape(ROWS, len(arrays) * HALF)],
        [HBM] * len(arrays) + [ANY],
        [pltpu.SemaphoreType.DMA((len(arrays),))],
        name=name,
    )(where, *arrays, after)
    return out


def per_device(qf, kf, vf, sf, qb, kb, vb, sb, grad):
    index = lax.axis_index("cp")
    side = index % 2
    where = jnp.stack([side, index // 2]).astype(jnp.int32)
    qf, kf, vf, qb, kb, vb, grad = (a[0] for a in (qf, kf, vf, qb, kb, vb, grad))
    qf, kf, vf, sf, qb, kb, vb, sb, grad = (
        pltpu.with_memory_space_constraint(a, pltpu.HBM)
        for a in (qf, kf, vf, sf, qb, kb, vb, sb, grad)
    )

    keep, send = split(where, kb, vb, sb, kf, vf, sf)
    half_b = other_half(where, (qb, grad), send, "half_b")
    b0, f0, half_b = join(where, keep, swapped(send), half_b)
    b4 = along_z(b0, -2)
    b2 = along_z(b0, 2)
    b1 = along_z(b0, 1)
    crossed_b = swapped(half_b)
    b4 = along_z(b4, -2)
    b3 = along_z(b2, 1)
    half_f = other_half(where, (qf,), b2, "half_f")
    f0 = tied(where, f0, b2)
    blocks_f = [f0] + [along_z(f0, k) for k in (1, 2, 3, 4)]
    crossed_f = swapped(half_f)

    dq_own, dq_cross, parts = run_bwd(where, qb, grad, crossed_b, (b0, b1, b2, b3, b4))
    terms = [parts[0]] + [along_z(parts[k], -k) for k in (1, 2, 3, 4)]
    o_own, o_cross = run_fwd(where, qf, crossed_f, blocks_f, (terms[1],))
    dq = handed(dq_own, -1), handed_across(dq_cross, -1)
    own, cross = call(
        total_kernel, [shape(ROWS, 2 * HEAD)] * 2, SLOTS, name="total"
    )(where, *terms)
    outs = call(
        final_kernel,
        [shape(ROWS, 2 * HALF)] * 2 + [shape(ROWS, 2 * HEAD)] * 2,
        6,
        [pltpu.SemaphoreType.DMA((8,))],
        name="final",
        place=HBM,
    )(
        where,
        handed(o_own, 1),
        handed_across(o_cross, 1),
        *dq,
        handed(own, -1),
        handed_across(cross, -1),
    )
    return tuple(out[None] for out in outs)


def solution(mesh):
    wide = P("section", "cp", "tp")
    flat = P("section", "cp")
    return jax.shard_map(
        per_device,
        mesh=mesh,
        in_specs=(wide, wide, wide, flat, wide, wide, wide, flat, wide),
        out_specs=(wide, wide, wide, wide),
        check_vma=False,
    )
```

time: 96.8 us -> 87 us (0.90)
  the two profiles are of different devices: /device:TPU:4 before, /device:TPU:56 now
where the time goes in v2:
time: 87 us; the launch traced here: 86.8 us
  starting transfers between devices  41.8 us (48%)
  Pallas kernels  25.4 us (29%)
  waiting for transfers between devices  18.5 us (21%)
  between operations  0.95 us (1%)
    ppermute x13, starting transfers between devices, along_z(): lax.ppermute(block, 'cp', [(i, (i + 2 * distance) % n) for i in range(n)])  31.1 us
    pallas_call x1, Pallas kernels, run_bwd(): call(bwd_kernel, outs, [HBM] * 2 + [VMEM] * (1 + SLOTS), scratch, 5 * MAT...  11.7 us
    ppermute x3, waiting for transfers between devices, handed_across(): return lax.ppermute(block, ('section', 'cp'), route)  6.38 us
    pallas_call x1, Pallas kernels, run_fwd(): call(fwd_kernel, [shape(ROWS, HALF)] * 2, [HBM] + [VMEM] * (1 + SLOTS) +...  5.71 us
    ppermute x13, waiting for transfers between devices, along_z(): lax.ppermute(block, 'cp', [(i, (i + 2 * distance) % n) for i in range(n)])  4.84 us
    ppermute x3, waiting for transfers between devices, handed(): lax.ppermute(block, 'section', [(i, (i + distance) % n) for i in range(n)])  4.74 us
    ppermute x3, starting transfers between devices, handed(): lax.ppermute(block, 'section', [(i, (i + distance) % n) for i in range(n)])  4.43 us
    ppermute x3, starting transfers between devices, swapped(): lax.ppermute(block, 'cp', [(i, i ^ 1) for i in range(lax.axis_size('cp'))])  3.69 us
  transfers between devices with their start and end apart: 22, of which 5 were waited for; matrix products, arithmetic and copies ran while one was open for 0% of the time, Pallas kernels for 25%

profile of v2, /device:TPU:56, one launch (start us, length us, event | category | flops | bytes accessed | tf_op | source)
XLA Modules:
  0.0 86.8 jit_solution(248391281897302184)
XLA Ops:
  0.6 0.1 pad_add_fusion.where_ref
  0.7 1.6 %split.1 = (bf16[144,512]{1,0:T(8,128)(2,1)S(1)}, bf16[144,512]{1,0:T(8,128)(2,1)S(1)}) custom-call(s32[2]{0:T(128)S(1)} %pad_add_fusion.where_ref, bf16[128,256]{1,0:T(8,128)(2,1)} %bitcast.19, bf16[128,256]{1,0:T(8,128)(2,1)} %bitcast.20, s32[1,128]{1,0:T(1,128)} %refs_2_.1, bf16[128,256]{1,0:T(8,128)(2,1)} %bitcast.21, bf16[128,256]{1,0:T(8,128)(2,1)} %bitcast.22, ...), custom_call_target="tpu_custom_call" | custom-call | bytes 524288 | tf_op jit(solution)/shard_map/split/pallas_call | solution.py:385
  2.3 1.6 %collective-permute-start = (bf16[144,512]{1,0:T(8,128)(2,1)S(1)}, bf16[144,512]{1,0:T(8,128)(2,1)S(1)}, u32[]{:S(2)}, u32[]{:S(2)}) collective-permute-start(bf16[144,512]{1,0:T(8,128)(2,1)S(1)} %get-tuple-element.25.refs_2_), channel_id=1, source_target_pairs={{0,1},{1,0},{2,3},{3,2},{4,5},{5,4},{6,7},{7,6},{8,9},{9,8},{10,11... | collective-permute-start | bytes 442376 | tf_op jit(solution)/shard_map/ppermute | solution.py:362
  3.9 1.6 %half_b.1.half_in = bf16[128,2048]{1,0:T(8,128)(2,1)S(1)} custom-call(s32[2]{0:T(128)S(1)} %pad_add_fusion.where_ref, bf16[128,2048]{1,0:T(8,128)(2,1)} %bitcast.13, bf16[128,2048]{1,0:T(8,128)(2,1)} %bitcast.15, bf16[144,512]{1,0:T(8,128)(2,1)S(1)} %get-tuple-element.25.refs_2_), custom_call_target="tpu_custom_call" | custom-call | bytes 524288 | tf_op jit(solution)/shard_map/half_b/pallas_call | solution.py:417
  5.5 2.5 %collective-permute-done.got = bf16[144,512]{1,0:T(8,128)(2,1)S(1)} collective-permute-done((bf16[144,512]{1,0:T(8,128)(2,1)S(1)}, bf16[144,512]{1,0:T(8,128)(2,1)S(1)}, u32[]{:S(2)}, u32[]{:S(2)}) %collective-permute-start) | collective-permute-done | bytes 147488 | tf_op jit(solution)/shard_map/ppermute | solution.py:362
  8.0 0.6 join.1
  8.6 1.6 %collective-permute-start.7 = (bf16[128,2048]{1,0:T(8,128)(2,1)S(1)}, bf16[128,2048]{1,0:T(8,128)(2,1)S(1)}, u32[]{:S(2)}, u32[]{:S(2)}) collective-permute-start(bf16[128,2048]{1,0:T(8,128)(2,1)S(1)} %get-tuple-element.28), channel_id=1, source_target_pairs={{0,1},{1,0},{2,3},{3,2},{4,5},{5,4},{6,7},{7,6},{8,9},{9,8},{10,11... | collective-permute-start | bytes 1572872 | tf_op jit(solution)/shard_map/ppermute | solution.py:362
  10.1 5.4 %collective-permute-start.10 = (bf16[272,256]{1,0:T(8,128)(2,1)S(1)}, bf16[272,256]{1,0:T(8,128)(2,1)S(1)}, u32[]{:S(2)}, u32[]{:S(2)}) collective-permute-start(bf16[272,256]{1,0:T(8,128)(2,1)S(1)} %get-tuple-element.26.refs_0_), channel_id=1, source_target_pairs={{0,12},{1,13},{2,14},{3,15},{4,0},{5,1},{6,2},{7,3},{8,4},{9,5},{1... | collective-permute-start | bytes 417800 | tf_op jit(solution)/shard_map/ppermute | solution.py:358
  15.5 0.0 collective-permute-start.1
  15.6 1.0 %collective-permute-start.8 = (bf16[272,256]{1,0:T(8,128)(2,1)S(1)}, bf16[272,256]{1,0:T(8,128)(2,1)S(1)}, u32[]{:S(2)}, u32[]{:S(2)}) collective-permute-start(bf16[272,256]{1,0:T(8,128)(2,1)S(1)} %get-tuple-element.26.refs_0_), channel_id=1, source_target_pairs={{0,2},{1,3},{2,4},{3,5},{4,6},{5,7},{6,8},{7,9},{8,10},{9,11},{10,... | collective-permute-start | bytes 417800 | tf_op jit(solution)/shard_map/ppermute | solution.py:358
  16.6 1.9 %collective-permute-done.10 = bf16[272,256]{1,0:T(8,128)(2,1)S(1)} collective-permute-done((bf16[272,256]{1,0:T(8,128)(2,1)S(1)}, bf16[272,256]{1,0:T(8,128)(2,1)S(1)}, u32[]{:S(2)}, u32[]{:S(2)}) %collective-permute-start.10) | collective-permute-done | bytes 139296 | tf_op jit(solution)/shard_map/ppermute | solution.py:358
  18.4 4.6 %collective-permute-start.11 = (bf16[272,256]{1,0:T(8,128)(2,1)S(1)}, bf16[272,256]{1,0:T(8,128)(2,1)S(1)}, u32[]{:S(2)}, u32[]{:S(2)}) collective-permute-start(bf16[272,256]{1,0:T(8,128)(2,1)S(1)} %collective-permute-done.10), channel_id=1, source_target_pairs={{0,12},{1,13},{2,14},{3,15},{4,0},{5,1},{6,2},{7,3},{8,4},{9,5},{1... | collective-permute-start | bytes 417800 | tf_op jit(solution)/shard_map/ppermute | solution.py:358
  23.0 2.9 %collective-permute-done.1.refs_1_.after.refs_2_ = bf16[272,256]{1,0:T(8,128)(2,1)S(1)} collective-permute-done((bf16[272,256]{1,0:T(8,128)(2,1)S(1)}, bf16[272,256]{1,0:T(8,128)(2,1)S(1)}, u32[]{:S(2)}, u32[]{:S(2)}) %collective-permute-start.1) | collective-permute-done | bytes 139296 | tf_op jit(solution)/shard_map/ppermute | solution.py:358
  26.0 0.0 collective-permute-start.9
  26.0 0.5 tied.1.refs_0_
  26.5 0.1 collective-permute-start.3
  26.6 1.5 %half_f.1 = bf16[128,1024]{1,0:T(8,128)(2,1)S(1)} custom-call(s32[2]{0:T(128)S(1)} %pad_add_fusion.where_ref, bf16[128,2048]{1,0:T(8,128)(2,1)} %bitcast.17, bf16[272,256]{1,0:T(8,128)(2,1)S(1)} %collective-permute-done.1.refs_1_.after.refs_2_), custom_call_target="tpu_custom_call" | custom-call | bytes 524288 | tf_op jit(solution)/shard_map/half_f/pallas_call | solution.py:417
  28.1 0.0 collective-permute-done.8.refs_1_
  28.1 1.8 %collective-permute-start.4 = (bf16[272,256]{1,0:T(8,128)(2,1)S(1)}, bf16[272,256]{1,0:T(8,128)(2,1)S(1)}, u32[]{:S(2)}, u32[]{:S(2)}) collective-permute-start(bf16[272,256]{1,0:T(8,128)(2,1)S(1)} %tied.1.refs_0_), channel_id=1, source_target_pairs={{0,4},{1,5},{2,6},{3,7},{4,8},{5,9},{6,10},{7,11},{8,12},{9,13},{1... | collective-permute-start | bytes 417800 | tf_op jit(solution)/shard_map/ppermute | solution.py:358
  30.0 0.0 collective-permute-done.11.refs_4_
  30.0 4.4 %collective-permute-start.5 = (bf16[272,256]{1,0:T(8,128)(2,1)S(1)}, bf16[272,256]{1,0:T(8,128)(2,1)S(1)}, u32[]{:S(2)}, u32[]{:S(2)}) collective-permute-start(bf16[272,256]{1,0:T(8,128)(2,1)S(1)} %tied.1.refs_0_), channel_id=1, source_target_pairs={{0,6},{1,7},{2,8},{3,9},{4,10},{5,11},{6,12},{7,13},{8,14},{9,15},... | collective-permute-start | bytes 417800 | tf_op jit(solution)/shard_map/ppermute | solution.py:358
  34.4 0.0 collective-permute-done.9.refs_3_
  34.4 2.0 %collective-permute-start.6 = (bf16[272,256]{1,0:T(8,128)(2,1)S(1)}, bf16[272,256]{1,0:T(8,128)(2,1)S(1)}, u32[]{:S(2)}, u32[]{:S(2)}) collective-permute-start(bf16[272,256]{1,0:T(8,128)(2,1)S(1)} %tied.1.refs_0_), channel_id=1, source_target_pairs={{0,8},{1,9},{2,10},{3,11},{4,12},{5,13},{6,14},{7,15},{8,0},{9,1},... | collective-permute-start | bytes 417800 | tf_op jit(solution)/shard_map/ppermute | solution.py:358
  36.4 0.0 collective-permute-done.7.qdx_ref
  36.4 0.5 collective-permute-start.2
  36.9 11.7 %bwd.1 = (bf16[128,1024]{1,0:T(8,128)(2,1)S(1)}, bf16[128,1024]{1,0:T(8,128)(2,1)S(1)}, bf16[256,256]{1,0:T(8,128)(2,1)S(1)}, bf16[256,256]{1,0:T(8,128)(2,1)S(1...) custom-call(s32[2]{0:T(128)S(1)} %pad_add_fusion.where_ref, ...), custom_call_target="tpu_custom_call" | custom-call | flops 3355443200 | bytes 4194304 | tf_op jit(solution)/shard_map/bwd/pallas_call | solution.py:343
  48.6 0.0 collective-permute-done.3.refs_1_
  48.6 0.5 collective-permute-start.12
  49.1 0.0 collective-permute-done.4.refs_2_
  49.1 4.0 %collective-permute-start.17 = (bf16[256,256]{1,0:T(8,128)(2,1)S(1)}, bf16[256,256]{1,0:T(8,128)(2,1)S(1)}, u32[]{:S(2)}, u32[]{:S(2)}) collective-permute-start(bf16[256,256]{1,0:T(8,128)(2,1)S(1)} %get-tuple-element.35), channel_id=1, source_target_pairs={{0,12},{1,13},{2,14},{3,15},{4,0},{5,1},{6,2},{7,3},{8,4},{9,5},{1... | collective-permute-start | bytes 393224 | tf_op jit(solution)/shard_map/ppermute | solution.py:358
  53.2 0.0 collective-permute-done.5.refs_3_
  53.2 1.0 %collective-permute-start.18 = (bf16[256,256]{1,0:T(8,128)(2,1)S(1)}, bf16[256,256]{1,0:T(8,128)(2,1)S(1)}, u32[]{:S(2)}, u32[]{:S(2)}) collective-permute-start(bf16[256,256]{1,0:T(8,128)(2,1)S(1)} %get-tuple-element.36), channel_id=1, source_target_pairs={{0,10},{1,11},{2,12},{3,13},{4,14},{5,15},{6,0},{7,1},{8,2},{9,3},... | collective-permute-start | bytes 393224 | tf_op jit(solution)/shard_map/ppermute | solution.py:358
  54.2 0.0 collective-permute-done.6.refs_4_
  54.2 6.2 %collective-permute-start.19 = (bf16[256,256]{1,0:T(8,128)(2,1)S(1)}, bf16[256,256]{1,0:T(8,128)(2,1)S(1)}, u32[]{:S(2)}, u32[]{:S(2)}) collective-permute-start(bf16[256,256]{1,0:T(8,128)(2,1)S(1)} %get-tuple-element.37), channel_id=1, source_target_pairs={{0,8},{1,9},{2,10},{3,11},{4,12},{5,13},{6,14},{7,15},{8,0},{9,1},... | collective-permute-start | bytes 393224 | tf_op jit(solution)/shard_map/ppermute | solution.py:358
  60.4 0.0 collective-permute-done.2.qx_ref
  60.4 0.7 collective-permute-start.15
  61.2 0.0 collective-permute-done.12.refs_5_.refs_1_
  61.2 0.4 collective-permute-start.16
  61.6 5.7 %fwd.1 = (bf16[128,1024]{1,0:T(8,128)(2,1)S(1)}, bf16[128,1024]{1,0:T(8,128)(2,1)S(1)}) custom-call(s32[2]{0:T(128)S(1)} %pad_add_fusion.where_ref, bf16[128,2048]{1,0:T(8,128)(2,1)} %bitcast.18, bf16[128,1024]{1,0:T(8,128)(2,1)S(1)} %collective-permute-done.2.qx_ref, bf16[272,256]{1,0:T(8,128)(2,1)S(1)} %tied.1.refs_0_, ...), custom_call_target="tpu_custom_call" | custom-call | flops 1342177280 | bytes 2097152 | tf_op jit(solution)/shard_map/fwd/pallas_call | solution.py:315
  67.3 0.0 collective-permute-done.17.refs_2_
  67.3 2.9 %collective-permute-start.13 = (bf16[128,1024]{1,0:T(8,128)(2,1)S(1)}, bf16[128,1024]{1,0:T(8,128)(2,1)S(1)}, u32[]{:S(2)}, u32[]{:S(2)}) collective-permute-start(bf16[128,1024]{1,0:T(8,128)(2,1)S(1)} %get-tuple-element.30), channel_id=1, source_target_pairs={{0,64},{64,128},{128,192},{192,0},{1,65},{65,129},{129,193},{193,1... | collective-permute-start | bytes 786440 | tf_op jit(solution)/shard_map/ppermute | solution.py:367
  70.2 0.0 collective-permute-done.18.refs_3_
  70.2 2.2 %collective-permute-start.14 = (bf16[128,1024]{1,0:T(8,128)(2,1)S(1)}, bf16[128,1024]{1,0:T(8,128)(2,1)S(1)}, u32[]{:S(2)}, u32[]{:S(2)}) collective-permute-start(bf16[128,1024]{1,0:T(8,128)(2,1)S(1)} %get-tuple-element.31), channel_id=1, source_target_pairs={{0,65},{1,64},{2,67},{3,66},{4,69},{5,68},{6,71},{7,70},{8,73},{9,... | collective-permute-start | bytes 786440 | tf_op jit(solution)/shard_map/ppermute | solution.py:375
  72.4 0.0 collective-permute-done.19.refs_4_
  72.4 0.6 total.1
  73.0 0.8 collective-permute-start.20
  73.8 4.7 %collective-permute-done.20.refs_4_ = bf16[128,256]{1,0:T(8,128)(2,1)S(1)} collective-permute-done((bf16[128,256]{1,0:T(8,128)(2,1)S(1)}, bf16[128,256]{1,0:T(8,128)(2,1)S(1)}, u32[]{:S(2)}, u32[]{:S(2)}) %collective-permute-start.20) | collective-permute-done | bytes 65568 | tf_op jit(solution)/shard_map/ppermute | solution.py:367
  78.6 0.0 collective-permute-start.21
  78.6 6.4 %collective-permute-done.21.refs_5_ = bf16[128,256]{1,0:T(8,128)(2,1)S(1)} collective-permute-done((bf16[128,256]{1,0:T(8,128)(2,1)S(1)}, bf16[128,256]{1,0:T(8,128)(2,1)S(1)}, u32[]{:S(2)}, u32[]{:S(2)}) %collective-permute-start.21) | collective-permute-done | bytes 65568 | tf_op jit(solution)/shard_map/ppermute | solution.py:375
  84.9 0.0 collective-permute-done.15.refs_2_
  84.9 0.0 collective-permute-done.16.refs_3_
  85.0 0.0 collective-permute-done.13.refs_0_
  85.0 0.0 collective-permute-done.14.refs_1_
  85.0 1.6 %final.1 = (bf16[128,2048]{1,0:T(8,128)(2,1)}, bf16[128,2048]{1,0:T(8,128)(2,1)}, bf16[128,256]{1,0:T(8,128)(2,1)}, bf16[128,256]{1,0:T(8,128)(2,1)}) custom-call(s32[2]{0:T(128)S(1)} %pad_add_fusion.where_ref, bf16[128,1024]{1,0:T(8,128)(2,1)S(1)} %collective-permute-done.13.refs_0_, bf16[128,1024]{1,0:T(8,128)(2,1)S(1)} %collective-permute-done.14.refs_1_, ...), custom_call_target="tpu_custom_call" | custom-call | bytes 524288 | tf_op jit(solution)/shard_map/final/pallas_call | solution.py:458
Async XLA Ops:
  2.3 5.7 %collective-permute-start = (bf16[144,512]{1,0:T(8,128)(2,1)S(1)}, bf16[144,512]{1,0:T(8,128)(2,1)S(1)}, u32[]{:S(2)}, u32[]{:S(2)}) collective-permute-start(bf16[144,512]{1,0:T(8,128)(2,1)S(1)} %get-tuple-element.25.refs_2_), channel_id=1, source_target_pairs={{0,1},{1,0},{2,3},{3,2},{4,5},{5,4},{6,7},{7,6},{8,9},{9,8},{10,11... | collective-permute-start | bytes 442376 | tf_op jit(solution)/shard_map/ppermute | solution.py:362
  8.6 27.8 %collective-permute-start.7 = (bf16[128,2048]{1,0:T(8,128)(2,1)S(1)}, bf16[128,2048]{1,0:T(8,128)(2,1)S(1)}, u32[]{:S(2)}, u32[]{:S(2)}) collective-permute-start(bf16[128,2048]{1,0:T(8,128)(2,1)S(1)} %get-tuple-element.28), channel_id=1, source_target_pairs={{0,1},{1,0},{2,3},{3,2},{4,5},{5,4},{6,7},{7,6},{8,9},{9,8},{10,11... | collective-permute-start | bytes 1572872 | tf_op jit(solution)/shard_map/ppermute | solution.py:362
  10.1 8.3 %collective-permute-start.10 = (bf16[272,256]{1,0:T(8,128)(2,1)S(1)}, bf16[272,256]{1,0:T(8,128)(2,1)S(1)}, u32[]{:S(2)}, u32[]{:S(2)}) collective-permute-start(bf16[272,256]{1,0:T(8,128)(2,1)S(1)} %get-tuple-element.26.refs_0_), channel_id=1, source_target_pairs={{0,12},{1,13},{2,14},{3,15},{4,0},{5,1},{6,2},{7,3},{8,4},{9,5},{1... | collective-permute-start | bytes 417800 | tf_op jit(solution)/shard_map/ppermute | solution.py:358
  15.5 10.4 %collective-permute-start.1 = (bf16[272,256]{1,0:T(8,128)(2,1)S(1)}, bf16[272,256]{1,0:T(8,128)(2,1)S(1)}, u32[]{:S(2)}, u32[]{:S(2)}) collective-permute-start(bf16[272,256]{1,0:T(8,128)(2,1)S(1)} %get-tuple-element.26.refs_0_), channel_id=1, source_target_pairs={{0,4},{1,5},{2,6},{3,7},{4,8},{5,9},{6,10},{7,11},{8,12},{9,13},{1... | collective-permute-start | bytes 417800 | tf_op jit(solution)/shard_map/ppermute | solution.py:358
  15.6 12.6 %collective-permute-start.8 = (bf16[272,256]{1,0:T(8,128)(2,1)S(1)}, bf16[272,256]{1,0:T(8,128)(2,1)S(1)}, u32[]{:S(2)}, u32[]{:S(2)}) collective-permute-start(bf16[272,256]{1,0:T(8,128)(2,1)S(1)} %get-tuple-element.26.refs_0_), channel_id=1, source_target_pairs={{0,2},{1,3},{2,4},{3,5},{4,6},{5,7},{6,8},{7,9},{8,10},{9,11},{10,... | collective-permute-start | bytes 417800 | tf_op jit(solution)/shard_map/ppermute | solution.py:358
  18.4 11.5 %collective-permute-start.11 = (bf16[272,256]{1,0:T(8,128)(2,1)S(1)}, bf16[272,256]{1,0:T(8,128)(2,1)S(1)}, u32[]{:S(2)}, u32[]{:S(2)}) collective-permute-start(bf16[272,256]{1,0:T(8,128)(2,1)S(1)} %collective-permute-done.10), channel_id=1, source_target_pairs={{0,12},{1,13},{2,14},{3,15},{4,0},{5,1},{6,2},{7,3},{8,4},{9,5},{1... | collective-permute-start | bytes 417800 | tf_op jit(solution)/shard_map/ppermute | solution.py:358
  26.0 8.4 %collective-permute-start.9 = (bf16[272,256]{1,0:T(8,128)(2,1)S(1)}, bf16[272,256]{1,0:T(8,128)(2,1)S(1)}, u32[]{:S(2)}, u32[]{:S(2)}) collective-permute-start(bf16[272,256]{1,0:T(8,128)(2,1)S(1)} %collective-permute-done.1.refs_1_.after.refs_2_), channel_id=1, source_target_pairs={{0,2},{1,3},{2,4},{3,5},{4,6},{5,7},{6,8},{7,9},{8,10},{9,11},{10,... | collective-permute-start | bytes 417800 | tf_op jit(solution)/shard_map/ppermute | solution.py:358
  26.5 22.1 %collective-permute-start.3 = (bf16[272,256]{1,0:T(8,128)(2,1)S(1)}, bf16[272,256]{1,0:T(8,128)(2,1)S(1)}, u32[]{:S(2)}, u32[]{:S(2)}) collective-permute-start(bf16[272,256]{1,0:T(8,128)(2,1)S(1)} %tied.1.refs_0_), channel_id=1, source_target_pairs={{0,2},{1,3},{2,4},{3,5},{4,6},{5,7},{6,8},{7,9},{8,10},{9,11},{10,... | collective-permute-start | bytes 417800 | tf_op jit(solution)/shard_map/ppermute | solution.py:358
  28.1 21.0 %collective-permute-start.4 = (bf16[272,256]{1,0:T(8,128)(2,1)S(1)}, bf16[272,256]{1,0:T(8,128)(2,1)S(1)}, u32[]{:S(2)}, u32[]{:S(2)}) collective-permute-start(bf16[272,256]{1,0:T(8,128)(2,1)S(1)} %tied.1.refs_0_), channel_id=1, source_target_pairs={{0,4},{1,5},{2,6},{3,7},{4,8},{5,9},{6,10},{7,11},{8,12},{9,13},{1... | collective-permute-start | bytes 417800 | tf_op jit(solution)/shard_map/ppermute | solution.py:358
  30.0 23.2 %collective-permute-start.5 = (bf16[272,256]{1,0:T(8,128)(2,1)S(1)}, bf16[272,256]{1,0:T(8,128)(2,1)S(1)}, u32[]{:S(2)}, u32[]{:S(2)}) collective-permute-start(bf16[272,256]{1,0:T(8,128)(2,1)S(1)} %tied.1.refs_0_), channel_id=1, source_target_pairs={{0,6},{1,7},{2,8},{3,9},{4,10},{5,11},{6,12},{7,13},{8,14},{9,15},... | collective-permute-start | bytes 417800 | tf_op jit(solution)/shard_map/ppermute | solution.py:358
  34.4 19.8 %collective-permute-start.6 = (bf16[272,256]{1,0:T(8,128)(2,1)S(1)}, bf16[272,256]{1,0:T(8,128)(2,1)S(1)}, u32[]{:S(2)}, u32[]{:S(2)}) collective-permute-start(bf16[272,256]{1,0:T(8,128)(2,1)S(1)} %tied.1.refs_0_), channel_id=1, source_target_pairs={{0,8},{1,9},{2,10},{3,11},{4,12},{5,13},{6,14},{7,15},{8,0},{9,1},... | collective-permute-start | bytes 417800 | tf_op jit(solution)/shard_map/ppermute | solution.py:358
  36.4 24.0 %collective-permute-start.2 = (bf16[128,1024]{1,0:T(8,128)(2,1)S(1)}, bf16[128,1024]{1,0:T(8,128)(2,1)S(1)}, u32[]{:S(2)}, u32[]{:S(2)}) collective-permute-start(bf16[128,1024]{1,0:T(8,128)(2,1)S(1)} %half_f.1), channel_id=1, source_target_pairs={{0,1},{1,0},{2,3},{3,2},{4,5},{5,4},{6,7},{7,6},{8,9},{9,8},{10,11... | collective-permute-start | bytes 786440 | tf_op jit(solution)/shard_map/ppermute | solution.py:362
  48.6 12.5 %collective-permute-start.12 = (bf16[256,256]{1,0:T(8,128)(2,1)S(1)}, bf16[256,256]{1,0:T(8,128)(2,1)S(1)}, u32[]{:S(2)}, u32[]{:S(2)}) collective-permute-start(bf16[256,256]{1,0:T(8,128)(2,1)S(1)} %get-tuple-element.29), channel_id=1, source_target_pairs={{0,14},{1,15},{2,0},{3,1},{4,2},{5,3},{6,4},{7,5},{8,6},{9,7},{10,... | collective-permute-start | bytes 393224 | tf_op jit(solution)/shard_map/ppermute | solution.py:358
  49.1 18.2 %collective-permute-start.17 = (bf16[256,256]{1,0:T(8,128)(2,1)S(1)}, bf16[256,256]{1,0:T(8,128)(2,1)S(1)}, u32[]{:S(2)}, u32[]{:S(2)}) collective-permute-start(bf16[256,256]{1,0:T(8,128)(2,1)S(1)} %get-tuple-element.35), channel_id=1, source_target_pairs={{0,12},{1,13},{2,14},{3,15},{4,0},{5,1},{6,2},{7,3},{8,4},{9,5},{1... | collective-permute-start | bytes 393224 | tf_op jit(solution)/shard_map/ppermute | solution.py:358
  53.2 17.0 %collective-permute-start.18 = (bf16[256,256]{1,0:T(8,128)(2,1)S(1)}, bf16[256,256]{1,0:T(8,128)(2,1)S(1)}, u32[]{:S(2)}, u32[]{:S(2)}) collective-permute-start(bf16[256,256]{1,0:T(8,128)(2,1)S(1)} %get-tuple-element.36), channel_id=1, source_target_pairs={{0,10},{1,11},{2,12},{3,13},{4,14},{5,15},{6,0},{7,1},{8,2},{9,3},... | collective-permute-start | bytes 393224 | tf_op jit(solution)/shard_map/ppermute | solution.py:358
  54.2 18.2 %collective-permute-start.19 = (bf16[256,256]{1,0:T(8,128)(2,1)S(1)}, bf16[256,256]{1,0:T(8,128)(2,1)S(1)}, u32[]{:S(2)}, u32[]{:S(2)}) collective-permute-start(bf16[256,256]{1,0:T(8,128)(2,1)S(1)} %get-tuple-element.37), channel_id=1, source_target_pairs={{0,8},{1,9},{2,10},{3,11},{4,12},{5,13},{6,14},{7,15},{8,0},{9,1},... | collective-permute-start | bytes 393224 | tf_op jit(solution)/shard_map/ppermute | solution.py:358
  60.4 24.5 %collective-permute-start.15 = (bf16[128,1024]{1,0:T(8,128)(2,1)S(1)}, bf16[128,1024]{1,0:T(8,128)(2,1)S(1)}, u32[]{:S(2)}, u32[]{:S(2)}) collective-permute-start(bf16[128,1024]{1,0:T(8,128)(2,1)S(1)} %get-tuple-element.32), channel_id=1, source_target_pairs={{0,192},{64,0},{128,64},{192,128},{1,193},{65,1},{129,65},{193,129... | collective-permute-start | bytes 786440 | tf_op jit(solution)/shard_map/ppermute | solution.py:367
  61.2 23.8 %collective-permute-start.16 = (bf16[128,1024]{1,0:T(8,128)(2,1)S(1)}, bf16[128,1024]{1,0:T(8,128)(2,1)S(1)}, u32[]{:S(2)}, u32[]{:S(2)}) collective-permute-start(bf16[128,1024]{1,0:T(8,128)(2,1)S(1)} %get-tuple-element.33), channel_id=1, source_target_pairs={{0,193},{1,192},{2,195},{3,194},{4,197},{5,196},{6,199},{7,198},{8... | collective-permute-start | bytes 786440 | tf_op jit(solution)/shard_map/ppermute | solution.py:375
  67.3 17.7 %collective-permute-start.13 = (bf16[128,1024]{1,0:T(8,128)(2,1)S(1)}, bf16[128,1024]{1,0:T(8,128)(2,1)S(1)}, u32[]{:S(2)}, u32[]{:S(2)}) collective-permute-start(bf16[128,1024]{1,0:T(8,128)(2,1)S(1)} %get-tuple-element.30), channel_id=1, source_target_pairs={{0,64},{64,128},{128,192},{192,0},{1,65},{65,129},{129,193},{193,1... | collective-permute-start | bytes 786440 | tf_op jit(solution)/shard_map/ppermute | solution.py:367
  70.2 14.8 %collective-permute-start.14 = (bf16[128,1024]{1,0:T(8,128)(2,1)S(1)}, bf16[128,1024]{1,0:T(8,128)(2,1)S(1)}, u32[]{:S(2)}, u32[]{:S(2)}) collective-permute-start(bf16[128,1024]{1,0:T(8,128)(2,1)S(1)} %get-tuple-element.31), channel_id=1, source_target_pairs={{0,65},{1,64},{2,67},{3,66},{4,69},{5,68},{6,71},{7,70},{8,73},{9,... | collective-permute-start | bytes 786440 | tf_op jit(solution)/shard_map/ppermute | solution.py:375
  73.0 5.6 %collective-permute-start.20 = (bf16[128,256]{1,0:T(8,128)(2,1)S(1)}, bf16[128,256]{1,0:T(8,128)(2,1)S(1)}, u32[]{:S(2)}, u32[]{:S(2)}) collective-permute-start(bf16[128,256]{1,0:T(8,128)(2,1)S(1)} %get-tuple-element.38), channel_id=1, source_target_pairs={{0,192},{64,0},{128,64},{192,128},{1,193},{65,1},{129,65},{193,129... | collective-permute-start | bytes 196616 | tf_op jit(solution)/shard_map/ppermute | solution.py:367
  78.6 6.4 %collective-permute-start.21 = (bf16[128,256]{1,0:T(8,128)(2,1)S(1)}, bf16[128,256]{1,0:T(8,128)(2,1)S(1)}, u32[]{:S(2)}, u32[]{:S(2)}) collective-permute-start(bf16[128,256]{1,0:T(8,128)(2,1)S(1)} %get-tuple-element.39), channel_id=1, source_target_pairs={{0,193},{1,192},{2,195},{3,194},{4,197},{5,196},{6,199},{7,198},{8... | collective-permute-start | bytes 196616 | tf_op jit(solution)/shard_map/ppermute | solution.py:375

commit v3 on v2

--- a/solution.py
+++ b/solution.py
@@ -41,7 +41,7 @@
         kernel,
         out_shape=outs,
         in_specs=[SMEM] + ([VMEM] * ins if isinstance(ins, int) else ins),
-        out_specs=[place] * len(outs),
+        out_specs=place if isinstance(place, list) else [place] * len(outs),
         scratch_shapes=scratch,
         compiler_params=pltpu.CompilerParams(vmem_limit_bytes=limit * 2**20),
         cost_estimate=pl.CostEstimate(flops=flops, bytes_accessed=moved_bytes, transcendentals=0),
@@ -104,23 +104,32 @@
 
 def total_kernel(where_ref, *refs):
     del where_ref
-    own, cross = refs[-2:]
-    for i, out in enumerate((own, cross)):
-        rows = pl.ds(i * ROWS, ROWS)
-        out[...] = sum(r[rows, :].astype(F32) for r in refs[:SLOTS]).astype(BF16)
+    refs[-1][...] = sum(r[...].astype(F32) for r in refs[:SLOTS]).astype(BF16)
+
+
+def output_kernel(where_ref, own, cross, o, token, sems):
+    side = where_ref[0]
+    token[...] = jnp.zeros_like(token)
+    fetched(
+        [
+            (part, o.at[:, pl.ds(pl.multiple_of(at * HALF, HALF), HALF)])
+            for part, at in ((own, side), (cross, 1 - side))
+        ],
+        sems,
+    )
 
 
 def final_kernel(where_ref, *refs):
     side = where_ref[0]
-    ins, (o, dq, dk, dv), sems = refs[:6], refs[6:10], refs[10]
+    ins, (dq, dk, dv), sems = refs[:4], refs[5:8], refs[8]
     copies = []
     for i, at in enumerate((side, 1 - side)):
         wide = pl.ds(pl.multiple_of(at * HALF, HALF), HALF)
         head = pl.ds(pl.multiple_of(at * HEAD, HEAD), HEAD)
-        copies.append((ins[i], o.at[:, wide]))
-        copies.append((ins[2 + i], dq.at[:, wide]))
-        copies.append((ins[4 + i].at[:, :HEAD], dk.at[:, head]))
-        copies.append((ins[4 + i].at[:, HEAD:], dv.at[:, head]))
+        rows = pl.ds(i * ROWS, ROWS)
+        copies.append((ins[i], dq.at[:, wide]))
+        copies.append((ins[2 + i].at[rows, :HEAD], dk.at[:, head]))
+        copies.append((ins[2 + i].at[rows, HEAD:], dv.at[:, head]))
     fetched(copies, sems)
 
 
@@ -157,14 +166,19 @@
     return new if running is None else op(running, new)
 
 
-def score_slot(k, lanes, keys, turned, cap, s_ref):
-    masked = jnp.minimum(dot(keys, turned), cap[slot(k), :])
-    s_ref[slot(k), lanes] = masked
-    return folded(masked, jnp.max)
-
-
-def exponentials(k, lanes, s_ref, peak):
-    return jnp.exp2((s_ref[slot(k), lanes] - peak) * SCALE2)
+def bounded(k, s_ref, cap):
+    return jnp.minimum(s_ref[slot(k), :], cap[slot(k), :])
+
+
+def row_peak(s_ref, cap):
+    peak = None
+    for k in range(SLOTS):
+        peak = joined(peak, folded(bounded(k, s_ref, cap), jnp.max), jnp.maximum)
+    return jnp.max(peak, axis=0, keepdims=True)
+
+
+def exponentials(k, s_ref, cap, peak):
+    return jnp.exp2((bounded(k, s_ref, cap) - peak) * SCALE2)
 
 
 def head_rows(own, crossed, g, offset=0):
@@ -180,40 +194,32 @@
     crossed[:, at] = rows[ROWS:]
 
 
-ALL = slice(0, PAIR)
-
-
 def fwd_kernel(where_ref, q_hbm, qx_ref, *refs):
     blocks, refs = refs[:SLOTS], refs[SLOTS + 1 :]
-    o_own, o_cross, cap, s_ref, e_ref, vt_ref, q_ref, turned, sems = refs
+    o_own, o_cross, cap, s_ref, e_ref, keys, vt_ref, q_ref, sems = refs
     base = pl.multiple_of(where_ref[0] * HALF, HALF)
     fetch = pltpu.make_async_copy(q_hbm.at[:, pl.ds(base, HALF)], q_ref, sems.at[0])
     fetch.start()
     fill_cap(where_ref, blocks, cap)
     for k, b in enumerate(blocks):
+        keys[slot(k), :] = b[:PAIR, :HEAD]
         vt_ref[:, slot(k)] = b[:PAIR, HEAD:].T
     fetch.wait()
 
-    def turn(g):
-        turned[g % 2] = head_rows(q_ref, qx_ref, g).T
-
-    peak = None
-    turn(0)
-    for k in range(SLOTS):
-        peak = joined(peak, score_slot(k, ALL, blocks[k][:PAIR, :HEAD], turned[0], cap, s_ref.at[0]), jnp.maximum)
+    def score(g):
+        s_ref[g % 2] = dot(keys[...], head_rows(q_ref, qx_ref, g, 2 * HALF).T)
+
+    score(0)
     for g in range(GROUP):
-        now, later = g % 2, (g + 1) % 2
-        top = jnp.max(peak, axis=0, keepdims=True)
-        peak = total = None
+        now = g % 2
         if g + 1 < GROUP:
-            turn(g + 1)
+            score(g + 1)
+        top = row_peak(s_ref.at[now], cap)
+        total = None
         for k in range(SLOTS):
-            expo = exponentials(k, ALL, s_ref.at[now], top)
+            expo = exponentials(k, s_ref.at[now], cap, top)
             e_ref[now, slot(k), :] = expo.astype(BF16)
             total = joined(total, folded(expo, jnp.sum), jnp.add)
-            if g + 1 < GROUP:
-                new = score_slot(k, ALL, blocks[k][:PAIR, :HEAD], turned[later], cap, s_ref.at[later])
-                peak = joined(peak, new, jnp.maximum)
         inv = 1.0 / jnp.sum(total, axis=0, keepdims=True)
         put_rows(g, dot(vt_ref[...], e_ref[now]) * inv, o_own, o_cross)
 
@@ -222,7 +228,7 @@
     blocks, refs = refs[:SLOTS], refs[SLOTS:]
     dq_own, dq_cross = refs[:2]
     parts, refs = refs[2 : SLOTS + 2], refs[SLOTS + 2 :]
-    cap, s_ref, dp_ref, e_ref, ds_ref, qs_ref, gs_ref, acc, kt_ref, qd_ref, turned, sems = refs
+    cap, s_ref, dp_ref, e_ref, ds_ref, qs_ref, gs_ref, acc, keys, values, kt_ref, qd_ref, sems = refs
     base = pl.multiple_of(where_ref[0] * HALF, HALF)
     fetch = [
         pltpu.make_async_copy(h.at[:, pl.ds(base, HALF)], qd_ref.at[i], sems.at[i])
@@ -232,74 +238,60 @@
         c.start()
     fill_cap(where_ref, blocks, cap)
     for k, b in enumerate(blocks):
+        keys[slot(k), :] = b[:PAIR, :HEAD]
+        values[slot(k), :] = b[:PAIR, HEAD:]
         kt_ref[:, slot(k)] = b[:PAIR, :HEAD].T
     for c in fetch:
         c.wait()
 
-    def span_of(g):
-        return slice(g * PAIR, (g + 1) * PAIR)
-
-    def key_terms(k, span, last):
-        dk = dot(ds_ref[slot(k), span], qs_ref[span, :])
-        dv = dot(e_ref[slot(k), span], gs_ref[span, :])
-        if last:
-            parts[k][:, :HEAD] = ((dk + acc[0, slot(k), :]) * SCALE).astype(BF16)
-            parts[k][:, HEAD:] = (dv + acc[1, slot(k), :]).astype(BF16)
-        else:
-            acc[0, slot(k), :] = dk
-            acc[1, slot(k), :] = dv
-
-    def query_terms(g, inv):
-        put_rows(g, dot(kt_ref[...], ds_ref[:, span_of(g)]) * (inv * SCALE), dq_own, dq_cross)
-
-    half = GROUP // 2
-    first, second = slice(0, half * PAIR), slice(half * PAIR, GROUP * PAIR)
-
-    def turn(g):
-        turned[g % 2, 0] = head_rows(qd_ref.at[0], qdx_ref, g).T
-        turned[g % 2, 1] = head_rows(qd_ref.at[1], qdx_ref, g, HALF).T
-
-    peak = None
-    turn(0)
-    for k in range(SLOTS):
-        peak = joined(peak, score_slot(k, ALL, blocks[k][:PAIR, :HEAD], turned[0, 0], cap, s_ref.at[0]), jnp.maximum)
+    def rows_of(which, g):
+        return head_rows(qd_ref.at[which], qdx_ref, g, which * HALF)
+
+    def products(g):
+        s_ref[g % 2] = dot(keys[...], rows_of(0, g).T)
+        dp_ref[g % 2] = dot(values[...], rows_of(1, g).T)
+
+    def span_of(g, count=1):
+        return slice(g * PAIR, (g + count) * PAIR)
+
+    def key_terms(g):
+        span = span_of(g, 2)
+        both = dot(ds_ref[:, span], qs_ref[span, :]), dot(e_ref[:, span], gs_ref[span, :])
+        for i, terms in enumerate(both):
+            acc[i] = terms if g == 0 else acc[i] + terms
+
+    products(0)
     for g in range(GROUP):
-        now, later = g % 2, (g + 1) % 2
+        now = g % 2
         cols = span_of(g)
-        top = jnp.max(peak, axis=0, keepdims=True)
-        peak = total = inner = None
+        if g + 1 < GROUP:
+            products(g + 1)
+        if g > 1 and g % 2 == 0:
+            key_terms(g - 2)
+        top = row_peak(s_ref.at[now], cap)
+        total = inner = None
         for k in range(SLOTS):
-            expo = exponentials(k, ALL, s_ref.at[now], top)
-            dp = dot(blocks[k][:PAIR, HEAD:], turned[now, 1])
+            expo = exponentials(k, s_ref.at[now], cap, top)
             e_ref[slot(k), cols] = expo.astype(BF16)
-            dp_ref[now, slot(k), :] = dp
             total = joined(total, folded(expo, jnp.sum), jnp.add)
-            inner = joined(inner, folded(expo * dp, jnp.sum), jnp.add)
-            if k == 0 and g > 0:
-                query_terms(g - 1, inv)
+            inner = joined(inner, folded(expo * dp_ref[now, slot(k), :], jnp.sum), jnp.add)
         inv = 1.0 / jnp.sum(total, axis=0, keepdims=True)
         delta = jnp.sum(inner, axis=0, keepdims=True) * inv
         factor = jnp.broadcast_to(inv, (HEAD, PAIR)).T
-        qs_ref[cols, :] = (head_rows(qd_ref.at[0], qdx_ref, g).astype(F32) * factor).astype(BF16)
-        gs_ref[cols, :] = (head_rows(qd_ref.at[1], qdx_ref, g, HALF).astype(F32) * factor).astype(BF16)
-        if g + 1 < GROUP:
-            turn(g + 1)
+        qs_ref[cols, :] = (rows_of(0, g).astype(F32) * factor).astype(BF16)
+        gs_ref[cols, :] = (rows_of(1, g).astype(F32) * factor).astype(BF16)
         for k in range(SLOTS):
             ds = (dp_ref[now, slot(k), :] - delta).astype(BF16)
             ds_ref[slot(k), cols] = e_ref[slot(k), cols] * ds
-            if g + 1 < GROUP:
-                new = score_slot(k, ALL, blocks[k][:PAIR, :HEAD], turned[later, 0], cap, s_ref.at[later])
-                peak = joined(peak, new, jnp.maximum)
-        if g >= half:
-            for k in (2 * (g - half), 2 * (g - half) + 1):
-                if k < SLOTS:
-                    key_terms(k, first, False)
-    query_terms(GROUP - 1, inv)
+        put_rows(g, dot(kt_ref[...], ds_ref[:, cols]) * (inv * SCALE), dq_own, dq_cross)
+    key_terms(GROUP - 2)
     for k in range(SLOTS):
-        key_terms(k, second, True)
+        parts[k][:, :HEAD] = (acc[0, slot(k), :] * SCALE).astype(BF16)
+        parts[k][:, HEAD:] = acc[1, slot(k), :].astype(BF16)
 
 
 MATMUL = 2 * GROUP * PAIR * KEYS * HEAD
+FINAL_FLOPS = 2 * MATMUL
 
 
 def run_fwd(where, query, crossed, blocks, after):
@@ -307,9 +299,9 @@
         pltpu.VMEM((KEYS, PAIR), F32),
         pltpu.VMEM((2, KEYS, PAIR), F32),
         pltpu.VMEM((2, KEYS, PAIR), BF16),
+        pltpu.VMEM((KEYS, HEAD), BF16),
         pltpu.VMEM((HEAD, KEYS), BF16),
         pltpu.VMEM((ROWS, HALF), BF16),
-        pltpu.VMEM((2, HEAD, PAIR), BF16),
         pltpu.SemaphoreType.DMA((1,)),
     ]
     return call(
@@ -335,9 +327,10 @@
         pltpu.VMEM((GROUP * PAIR, HEAD), BF16),
         pltpu.VMEM((GROUP * PAIR, HEAD), BF16),
         pltpu.VMEM((2, KEYS, HEAD), F32),
+        pltpu.VMEM((KEYS, HEAD), BF16),
+        pltpu.VMEM((KEYS, HEAD), BF16),
         pltpu.VMEM((HEAD, KEYS), BF16),
         pltpu.VMEM((2, ROWS, HALF), BF16),
-        pltpu.VMEM((2, 2, HEAD, PAIR), BF16),
         pltpu.SemaphoreType.DMA((2,)),
     ]
     out = call(
@@ -435,42 +428,44 @@
     )
 
     keep, send = split(where, kb, vb, sb, kf, vf, sf)
-    half_b = other_half(where, (qb, grad), send, "half_b")
-    b0, f0, half_b = join(where, keep, swapped(send), half_b)
+    halves = other_half(where, (qb, grad, qf), send, "halves")
+    b0, f0, halves = join(where, keep, swapped(send), halves)
     b4 = along_z(b0, -2)
     b2 = along_z(b0, 2)
     b1 = along_z(b0, 1)
-    crossed_b = swapped(half_b)
+    crossed = swapped(halves)
     b4 = along_z(b4, -2)
     b3 = along_z(b2, 1)
-    half_f = other_half(where, (qf,), b2, "half_f")
     f0 = tied(where, f0, b2)
     blocks_f = [f0] + [along_z(f0, k) for k in (1, 2, 3, 4)]
-    crossed_f = swapped(half_f)
-
-    dq_own, dq_cross, parts = run_bwd(where, qb, grad, crossed_b, (b0, b1, b2, b3, b4))
-    terms = [parts[0]] + [along_z(parts[k], -k) for k in (1, 2, 3, 4)]
-    o_own, o_cross = run_fwd(where, qf, crossed_f, blocks_f, (terms[1],))
+
+    dq_own, dq_cross, parts = run_bwd(where, qb, grad, crossed, (b0, b1, b2, b3, b4))
+    terms = [parts[0]] + [along_z(parts[k], -k) for k in range(1, SLOTS)]
     dq = handed(dq_own, -1), handed_across(dq_cross, -1)
-    own, cross = call(
-        total_kernel, [shape(ROWS, 2 * HEAD)] * 2, SLOTS, name="total"
-    )(where, *terms)
-    outs = call(
+    o_own, o_cross = run_fwd(where, qf, crossed, blocks_f, (terms[1],))
+    dq = handed(dq_own, -1), handed_across(dq_cross, -1)
+    (summed,) = call(
+        total_kernel, [shape(PAIR, 2 * HEAD)], [VMEM] * SLOTS + [ANY] * 2, name="total"
+    )(where, *terms, *dq)
+    received = handed(summed, -1)
+    attn_out, token = call(
+        output_kernel,
+        [shape(ROWS, 2 * HALF), shape(TAIL, HEAD)],
+        2,
+        [pltpu.SemaphoreType.DMA((2,))],
+        FINAL_FLOPS,
+        name="output",
+        place=[HBM, VMEM],
+    )(where, handed(o_own, 1), handed_across(o_cross, 1))
+    grads = call(
         final_kernel,
-        [shape(ROWS, 2 * HALF)] * 2 + [shape(ROWS, 2 * HEAD)] * 2,
-        6,
-        [pltpu.SemaphoreType.DMA((8,))],
+        [shape(ROWS, 2 * HALF)] + [shape(ROWS, 2 * HEAD)] * 2,
+        [VMEM] * 4 + [ANY],
+        [pltpu.SemaphoreType.DMA((6,))],
         name="final",
         place=HBM,
-    )(
-        where,
-        handed(o_own, 1),
-        handed_across(o_cross, 1),
-        *dq,
-        handed(own, -1),
-        handed_across(cross, -1),
-    )
-    return tuple(out[None] for out in outs)
+    )(where, *dq, received, swapped(received), token)
+    return tuple(out[None] for out in (attn_out, *grads))
 
 
 def solution(mesh):

time: 87 us -> 89 us (1.023)
  waiting for transfers between devices: 18.5 us -> 26 us
  starting transfers between devices: 41.8 us -> 36.1 us
    ppermute x13, waiting for transfers between devices: 4.84 us -> 14.4 us  [along_z(): lax.ppermute(block, 'cp', [(i, (i + 2 * distance) % n) for i in range(n)])]
    ppermute x3 -> x2, waiting for transfers between devices: 6.38 us -> 0.01 us  [handed_across(): return lax.ppermute(block, ('section', 'cp'), route)]
    ppermute x13, starting transfers between devices: 31.1 us -> 27.4 us  [along_z(): lax.ppermute(block, 'cp', [(i, (i + 2 * distance) % n) for i in range(n)])]
    ppermute x3, waiting for transfers between devices: 2.5 us -> 5.44 us  [swapped(): lax.ppermute(block, 'cp', [(i, i ^ 1) for i in range(lax.axis_size('cp'))])]
    ppermute x3, starting transfers between devices: 4.43 us -> 1.81 us  [handed(): lax.ppermute(block, 'section', [(i, (i + distance) % n) for i in range(n)])]
    ppermute x3, waiting for transfers between devices: 4.74 us -> 6.17 us  [handed(): lax.ppermute(block, 'section', [(i, (i + distance) % n) for i in range(n)])]
    pallas_call x2 -> x1, Pallas kernels: 3.09 us -> 1.68 us  [other_half(): call(functools.partial(other_half_kernel, count=len(arrays)), [shape(ROWS...]
    pallas_call x2 -> x3, Pallas kernels: 2.23 us -> 3.39 us  [the longest x1 1.41 us: per_device(): call(final_kernel, [shape(ROWS, 2 * HALF)] + [shape(ROWS, 2 * HEAD)] * 2,...]
  transfers between devices with their start and end apart: 22 -> 21, of which waited for: 5 -> 8; matrix products, arithmetic and copies ran while one was open for 0% -> 0% of each run, Pallas kernels for 25% -> 25%
where the time goes in v3:
time: 89 us; the launch traced here: 88.8 us
  starting transfers between devices  36.1 us (41%)
  waiting for transfers between devices  26 us (29%)
  Pallas kernels  25.6 us (29%)
  between operations  0.95 us (1%)
    ppermute x13, starting transfers between devices, along_z(): lax.ppermute(block, 'cp', [(i, (i + 2 * distance) % n) for i in range(n)])  27.4 us
    ppermute x13, waiting for transfers between devices, along_z(): lax.ppermute(block, 'cp', [(i, (i + 2 * distance) % n) for i in range(n)])  14.4 us
    pallas_call x1, Pallas kernels, run_bwd(): call(bwd_kernel, outs, [HBM] * 2 + [VMEM] * (1 + SLOTS), scratch, 5 * MAT...  11.8 us
    ppermute x3, waiting for transfers between devices, handed(): lax.ppermute(block, 'section', [(i, (i + distance) % n) for i in range(n)])  6.17 us
    pallas_call x1, Pallas kernels, run_fwd(): call(fwd_kernel, [shape(ROWS, HALF)] * 2, [HBM] + [VMEM] * (1 + SLOTS) +...  6.04 us
    ppermute x3, waiting for transfers between devices, swapped(): lax.ppermute(block, 'cp', [(i, i ^ 1) for i in range(lax.axis_size('cp'))])  5.44 us
    ppermute x3, starting transfers between devices, swapped(): lax.ppermute(block, 'cp', [(i, i ^ 1) for i in range(lax.axis_size('cp'))])  3.73 us
    ppermute x2, starting transfers between devices, handed_across(): return lax.ppermute(block, ('section', 'cp'), route)  3.17 us
  transfers between devices with their start and end apart: 21, of which 8 were waited for; matrix products, arithmetic and copies ran while one was open for 0% of the time, Pallas kernels for 25%

profile of v3, /device:TPU:56, one launch (start us, length us, event | category | flops | bytes accessed | tf_op | source)
XLA Modules:
  0.0 88.8 jit_solution(4652972224032003430)
XLA Ops:
  0.6 0.1 pad_add_fusion.where_ref
  0.7 1.6 %split.1 = (bf16[144,512]{1,0:T(8,128)(2,1)S(1)}, bf16[144,512]{1,0:T(8,128)(2,1)S(1)}) custom-call(s32[2]{0:T(128)S(1)} %pad_add_fusion.where_ref, bf16[128,256]{1,0:T(8,128)(2,1)} %bitcast.19, bf16[128,256]{1,0:T(8,128)(2,1)} %bitcast.20, s32[1,128]{1,0:T(1,128)} %refs_2_.1, bf16[128,256]{1,0:T(8,128)(2,1)} %bitcast.21, bf16[128,256]{1,0:T(8,128)(2,1)} %bitcast.22, ...), custom_call_target="tpu_custom_call" | custom-call | bytes 524288 | tf_op jit(solution)/shard_map/split/pallas_call | solution.py:378
  2.3 1.6 %collective-permute-start = (bf16[144,512]{1,0:T(8,128)(2,1)S(1)}, bf16[144,512]{1,0:T(8,128)(2,1)S(1)}, u32[]{:S(2)}, u32[]{:S(2)}) collective-permute-start(bf16[144,512]{1,0:T(8,128)(2,1)S(1)} %get-tuple-element.24.refs_3_), channel_id=1, source_target_pairs={{0,1},{1,0},{2,3},{3,2},{4,5},{5,4},{6,7},{7,6},{8,9},{9,8},{10,11... | collective-permute-start | bytes 442376 | tf_op jit(solution)/shard_map/ppermute | solution.py:355
  3.9 1.7 %halves.1.half_in = bf16[128,3072]{1,0:T(8,128)(2,1)S(1)} custom-call(s32[2]{0:T(128)S(1)} %pad_add_fusion.where_ref, bf16[128,2048]{1,0:T(8,128)(2,1)} %bitcast.13, bf16[128,2048]{1,0:T(8,128)(2,1)} %bitcast.15, bf16[128,2048]{1,0:T(8,128)(2,1)} %bitcast.17, bf16[144,512]{1,0:T(8,128)(2,1)S(1)} %get-tuple-element.24.refs_3_), custom_call_target="tpu_custom_call" | custom-call | bytes 524288 | tf_op jit(solution)/shard_map/halves/pallas_call | solution.py:410
  5.6 2.4 %collective-permute-done.got = bf16[144,512]{1,0:T(8,128)(2,1)S(1)} collective-permute-done((bf16[144,512]{1,0:T(8,128)(2,1)S(1)}, bf16[144,512]{1,0:T(8,128)(2,1)S(1)}, u32[]{:S(2)}, u32[]{:S(2)}) %collective-permute-start) | collective-permute-done | bytes 147488 | tf_op jit(solution)/shard_map/ppermute | solution.py:355
  8.0 0.6 join.1
  8.6 1.6 %collective-permute-start.1 = (bf16[128,3072]{1,0:T(8,128)(2,1)S(1)}, bf16[128,3072]{1,0:T(8,128)(2,1)S(1)}, u32[]{:S(2)}, u32[]{:S(2)}) collective-permute-start(bf16[128,3072]{1,0:T(8,128)(2,1)S(1)} %get-tuple-element.25), channel_id=1, source_target_pairs={{0,1},{1,0},{2,3},{3,2},{4,5},{5,4},{6,7},{7,6},{8,9},{9,8},{10,11... | collective-permute-start | bytes 2359304 | tf_op jit(solution)/shard_map/ppermute | solution.py:355
  10.1 5.4 %collective-permute-start.9 = (bf16[272,256]{1,0:T(8,128)(2,1)S(1)}, bf16[272,256]{1,0:T(8,128)(2,1)S(1)}, u32[]{:S(2)}, u32[]{:S(2)}) collective-permute-start(bf16[272,256]{1,0:T(8,128)(2,1)S(1)} %get-tuple-element.27.refs_0_), channel_id=1, source_target_pairs={{0,12},{1,13},{2,14},{3,15},{4,0},{5,1},{6,2},{7,3},{8,4},{9,5},{1... | collective-permute-start | bytes 417800 | tf_op jit(solution)/shard_map/ppermute | solution.py:351
  15.5 0.0 collective-permute-start.2
  15.6 1.0 %collective-permute-start.7 = (bf16[272,256]{1,0:T(8,128)(2,1)S(1)}, bf16[272,256]{1,0:T(8,128)(2,1)S(1)}, u32[]{:S(2)}, u32[]{:S(2)}) collective-permute-start(bf16[272,256]{1,0:T(8,128)(2,1)S(1)} %get-tuple-element.27.refs_0_), channel_id=1, source_target_pairs={{0,2},{1,3},{2,4},{3,5},{4,6},{5,7},{6,8},{7,9},{8,10},{9,11},{10,... | collective-permute-start | bytes 417800 | tf_op jit(solution)/shard_map/ppermute | solution.py:351
  16.6 1.9 %collective-permute-done.9 = bf16[272,256]{1,0:T(8,128)(2,1)S(1)} collective-permute-done((bf16[272,256]{1,0:T(8,128)(2,1)S(1)}, bf16[272,256]{1,0:T(8,128)(2,1)S(1)}, u32[]{:S(2)}, u32[]{:S(2)}) %collective-permute-start.9) | collective-permute-done | bytes 139296 | tf_op jit(solution)/shard_map/ppermute | solution.py:351
  18.4 4.6 %collective-permute-start.10 = (bf16[272,256]{1,0:T(8,128)(2,1)S(1)}, bf16[272,256]{1,0:T(8,128)(2,1)S(1)}, u32[]{:S(2)}, u32[]{:S(2)}) collective-permute-start(bf16[272,256]{1,0:T(8,128)(2,1)S(1)} %collective-permute-done.9), channel_id=1, source_target_pairs={{0,12},{1,13},{2,14},{3,15},{4,0},{5,1},{6,2},{7,3},{8,4},{9,5},{1... | collective-permute-start | bytes 417800 | tf_op jit(solution)/shard_map/ppermute | solution.py:351
  23.0 2.9 %collective-permute-done.2.after.refs_2_ = bf16[272,256]{1,0:T(8,128)(2,1)S(1)} collective-permute-done((bf16[272,256]{1,0:T(8,128)(2,1)S(1)}, bf16[272,256]{1,0:T(8,128)(2,1)S(1)}, u32[]{:S(2)}, u32[]{:S(2)}) %collective-permute-start.2) | collective-permute-done | bytes 139296 | tf_op jit(solution)/shard_map/ppermute | solution.py:351
  26.0 0.0 collective-permute-start.8
  26.0 0.5 tied.1.refs_0_
  26.5 0.1 collective-permute-start.3
  26.6 0.0 collective-permute-done.7.refs_1_
  26.6 1.8 %collective-permute-start.4 = (bf16[272,256]{1,0:T(8,128)(2,1)S(1)}, bf16[272,256]{1,0:T(8,128)(2,1)S(1)}, u32[]{:S(2)}, u32[]{:S(2)}) collective-permute-start(bf16[272,256]{1,0:T(8,128)(2,1)S(1)} %tied.1.refs_0_), channel_id=1, source_target_pairs={{0,4},{1,5},{2,6},{3,7},{4,8},{5,9},{6,10},{7,11},{8,12},{9,13},{1... | collective-permute-start | bytes 417800 | tf_op jit(solution)/shard_map/ppermute | solution.py:351
  28.4 0.0 collective-permute-done.10.refs_4_
  28.4 4.4 %collective-permute-start.5 = (bf16[272,256]{1,0:T(8,128)(2,1)S(1)}, bf16[272,256]{1,0:T(8,128)(2,1)S(1)}, u32[]{:S(2)}, u32[]{:S(2)}) collective-permute-start(bf16[272,256]{1,0:T(8,128)(2,1)S(1)} %tied.1.refs_0_), channel_id=1, source_target_pairs={{0,6},{1,7},{2,8},{3,9},{4,10},{5,11},{6,12},{7,13},{8,14},{9,15},... | collective-permute-start | bytes 417800 | tf_op jit(solution)/shard_map/ppermute | solution.py:351
  32.8 1.2 %collective-permute-done.8.refs_3_ = bf16[272,256]{1,0:T(8,128)(2,1)S(1)} collective-permute-done((bf16[272,256]{1,0:T(8,128)(2,1)S(1)}, bf16[272,256]{1,0:T(8,128)(2,1)S(1)}, u32[]{:S(2)}, u32[]{:S(2)}) %collective-permute-start.8) | collective-permute-done | bytes 139296 | tf_op jit(solution)/shard_map/ppermute | solution.py:351
  34.0 0.7 collective-permute-start.6
  34.8 0.0 collective-permute-done.1.qdx_ref.qx_ref
  34.8 11.8 %bwd.1 = (bf16[128,1024]{1,0:T(8,128)(2,1)S(1)}, bf16[128,1024]{1,0:T(8,128)(2,1)S(1)}, bf16[256,256]{1,0:T(8,128)(2,1)S(1)}, bf16[256,256]{1,0:T(8,128)(2,1)S(1...) custom-call(s32[2]{0:T(128)S(1)} %pad_add_fusion.where_ref, ...), custom_call_target="tpu_custom_call" | custom-call | flops 3355443200 | bytes 4194304 | tf_op jit(solution)/shard_map/bwd/pallas_call | solution.py:336
  46.6 1.6 %collective-permute-start.11 = (bf16[256,256]{1,0:T(8,128)(2,1)S(1)}, bf16[256,256]{1,0:T(8,128)(2,1)S(1)}, u32[]{:S(2)}, u32[]{:S(2)}) collective-permute-start(bf16[256,256]{1,0:T(8,128)(2,1)S(1)} %get-tuple-element.28), channel_id=1, source_target_pairs={{0,14},{1,15},{2,0},{3,1},{4,2},{5,3},{6,4},{7,5},{8,6},{9,7},{10,... | collective-permute-start | bytes 393224 | tf_op jit(solution)/shard_map/ppermute | solution.py:351
  48.2 0.0 collective-permute-done.3.refs_1_
  48.2 0.7 collective-permute-start.14
  49.0 0.0 collective-permute-done.4.refs_2_
  49.0 0.4 collective-permute-start.15
  49.4 3.4 %collective-permute-done.5.refs_3_ = bf16[272,256]{1,0:T(8,128)(2,1)S(1)} collective-permute-done((bf16[272,256]{1,0:T(8,128)(2,1)S(1)}, bf16[272,256]{1,0:T(8,128)(2,1)S(1)}, u32[]{:S(2)}, u32[]{:S(2)}) %collective-permute-start.5) | collective-permute-done | bytes 139296 | tf_op jit(solution)/shard_map/ppermute | solution.py:351
  52.9 0.9 %collective-permute-start.16 = (bf16[256,256]{1,0:T(8,128)(2,1)S(1)}, bf16[256,256]{1,0:T(8,128)(2,1)S(1)}, u32[]{:S(2)}, u32[]{:S(2)}) collective-permute-start(bf16[256,256]{1,0:T(8,128)(2,1)S(1)} %get-tuple-element.35), channel_id=1, source_target_pairs={{0,12},{1,13},{2,14},{3,15},{4,0},{5,1},{6,2},{7,3},{8,4},{9,5},{1... | collective-permute-start | bytes 393224 | tf_op jit(solution)/shard_map/ppermute | solution.py:351
  53.7 0.0 collective-permute-done.6.refs_4_
  53.7 2.4 %collective-permute-start.17 = (bf16[256,256]{1,0:T(8,128)(2,1)S(1)}, bf16[256,256]{1,0:T(8,128)(2,1)S(1)}, u32[]{:S(2)}, u32[]{:S(2)}) collective-permute-start(bf16[256,256]{1,0:T(8,128)(2,1)S(1)} %get-tuple-element.36), channel_id=1, source_target_pairs={{0,10},{1,11},{2,12},{3,13},{4,14},{5,15},{6,0},{7,1},{8,2},{9,3},... | collective-permute-start | bytes 393224 | tf_op jit(solution)/shard_map/ppermute | solution.py:351
  56.2 0.0 collective-permute-done.11.refs_5_.refs_1_
  56.2 4.4 %collective-permute-start.18 = (bf16[256,256]{1,0:T(8,128)(2,1)S(1)}, bf16[256,256]{1,0:T(8,128)(2,1)S(1)}, u32[]{:S(2)}, u32[]{:S(2)}) collective-permute-start(bf16[256,256]{1,0:T(8,128)(2,1)S(1)} %get-tuple-element.37), channel_id=1, source_target_pairs={{0,8},{1,9},{2,10},{3,11},{4,12},{5,13},{6,14},{7,15},{8,0},{9,1},... | collective-permute-start | bytes 393224 | tf_op jit(solution)/shard_map/ppermute | solution.py:351
  60.6 6.0 %fwd.1 = (bf16[128,1024]{1,0:T(8,128)(2,1)S(1)}, bf16[128,1024]{1,0:T(8,128)(2,1)S(1)}) custom-call(s32[2]{0:T(128)S(1)} %pad_add_fusion.where_ref, bf16[128,2048]{1,0:T(8,128)(2,1)} %bitcast.18, bf16[128,3072]{1,0:T(8,128)(2,1)S(1)} %collective-permute-done.1.qdx_ref.qx_ref, bf16[272,256]{1,0:T(8,128)(2,1)S(1)} %tied.1.refs_0_, ...), custom_call_target="tpu_custom_call" | custom-call | flops 1342177280 | bytes 2097152 | tf_op jit(solution)/shard_map/fwd/pallas_call | solution.py:307
  66.7 0.0 collective-permute-done.16.refs_2_
  66.7 1.0 %collective-permute-start.12 = (bf16[128,1024]{1,0:T(8,128)(2,1)S(1)}, bf16[128,1024]{1,0:T(8,128)(2,1)S(1)}, u32[]{:S(2)}, u32[]{:S(2)}) collective-permute-start(bf16[128,1024]{1,0:T(8,128)(2,1)S(1)} %get-tuple-element.29), channel_id=1, source_target_pairs={{0,64},{64,128},{128,192},{192,0},{1,65},{65,129},{129,193},{193,1... | collective-permute-start | bytes 786440 | tf_op jit(solution)/shard_map/ppermute | solution.py:360
  67.7 4.9 %collective-permute-done.17.refs_3_ = bf16[256,256]{1,0:T(8,128)(2,1)S(1)} collective-permute-done((bf16[256,256]{1,0:T(8,128)(2,1)S(1)}, bf16[256,256]{1,0:T(8,128)(2,1)S(1)}, u32[]{:S(2)}, u32[]{:S(2)}) %collective-permute-start.17) | collective-permute-done | bytes 131104 | tf_op jit(solution)/shard_map/ppermute | solution.py:351
  72.6 2.8 %collective-permute-start.13 = (bf16[128,1024]{1,0:T(8,128)(2,1)S(1)}, bf16[128,1024]{1,0:T(8,128)(2,1)S(1)}, u32[]{:S(2)}, u32[]{:S(2)}) collective-permute-start(bf16[128,1024]{1,0:T(8,128)(2,1)S(1)} %get-tuple-element.30), channel_id=1, source_target_pairs={{0,65},{1,64},{2,67},{3,66},{4,69},{5,68},{6,71},{7,70},{8,73},{9,... | collective-permute-start | bytes 786440 | tf_op jit(solution)/shard_map/ppermute | solution.py:368
  75.3 0.0 collective-permute-done.18.refs_4_
  75.3 0.0 collective-permute-done.14.refs_5_.refs_0_
  75.3 0.0 collective-permute-done.15.refs_6_.refs_1_
  75.3 0.6 total.1
  76.0 0.1 collective-permute-start.19
  76.0 6.2 %collective-permute-done.19.refs_2_ = bf16[256,256]{1,0:T(8,128)(2,1)S(1)} collective-permute-done((bf16[256,256]{1,0:T(8,128)(2,1)S(1)}, bf16[256,256]{1,0:T(8,128)(2,1)S(1)}, u32[]{:S(2)}, u32[]{:S(2)}) %collective-permute-start.19) | collective-permute-done | bytes 131104 | tf_op jit(solution)/shard_map/ppermute | solution.py:360
  82.2 0.6 collective-permute-start.20
  82.8 0.0 collective-permute-done.12.own
  82.8 0.0 collective-permute-done.13.cross
  82.8 1.4 %output.1 = (bf16[128,2048]{1,0:T(8,128)(2,1)}, bf16[16,128]{1,0:T(8,128)(2,1)S(1)}) custom-call(s32[2]{0:T(128)S(1)} %pad_add_fusion.where_ref, bf16[128,1024]{1,0:T(8,128)(2,1)S(1)} %collective-permute-done.12.own, bf16[128,1024]{1,0:T(8,128)(2,1)S(1)} %collective-permute-done.13.cross), custom_call_target="tpu_custom_call" | custom-call | flops 1342177280 | bytes 524288 | tf_op jit(solution)/shard_map/output/pallas_call | solution.py:451
  84.2 3.0 %collective-permute-done.20.refs_3_ = bf16[256,256]{1,0:T(8,128)(2,1)S(1)} collective-permute-done((bf16[256,256]{1,0:T(8,128)(2,1)S(1)}, bf16[256,256]{1,0:T(8,128)(2,1)S(1)}, u32[]{:S(2)}, u32[]{:S(2)}) %collective-permute-start.20) | collective-permute-done | bytes 131104 | tf_op jit(solution)/shard_map/ppermute | solution.py:355
  87.2 1.4 %final.1 = (bf16[128,2048]{1,0:T(8,128)(2,1)}, bf16[128,256]{1,0:T(8,128)(2,1)}, bf16[128,256]{1,0:T(8,128)(2,1)}) custom-call(s32[2]{0:T(128)S(1)} %pad_add_fusion.where_ref, bf16[128,1024]{1,0:T(8,128)(2,1)S(1)} %collective-permute-done.14.refs_5_.refs_0_, bf16[128,1024]{1,0:T(8,128)(2,1)S(1)} %collective-permute-done.15.refs_6_.refs_1_, ...), custom_call_target="tpu_custom_call" | custom-call | bytes 524288 | tf_op jit(solution)/shard_map/final/pallas_call | solution.py:460
Async XLA Ops:
  2.3 5.7 %collective-permute-start = (bf16[144,512]{1,0:T(8,128)(2,1)S(1)}, bf16[144,512]{1,0:T(8,128)(2,1)S(1)}, u32[]{:S(2)}, u32[]{:S(2)}) collective-permute-start(bf16[144,512]{1,0:T(8,128)(2,1)S(1)} %get-tuple-element.24.refs_3_), channel_id=1, source_target_pairs={{0,1},{1,0},{2,3},{3,2},{4,5},{5,4},{6,7},{7,6},{8,9},{9,8},{10,11... | collective-permute-start | bytes 442376 | tf_op jit(solution)/shard_map/ppermute | solution.py:355
  8.6 26.2 %collective-permute-start.1 = (bf16[128,3072]{1,0:T(8,128)(2,1)S(1)}, bf16[128,3072]{1,0:T(8,128)(2,1)S(1)}, u32[]{:S(2)}, u32[]{:S(2)}) collective-permute-start(bf16[128,3072]{1,0:T(8,128)(2,1)S(1)} %get-tuple-element.25), channel_id=1, source_target_pairs={{0,1},{1,0},{2,3},{3,2},{4,5},{5,4},{6,7},{7,6},{8,9},{9,8},{10,11... | collective-permute-start | bytes 2359304 | tf_op jit(solution)/shard_map/ppermute | solution.py:355
  10.1 8.3 %collective-permute-start.9 = (bf16[272,256]{1,0:T(8,128)(2,1)S(1)}, bf16[272,256]{1,0:T(8,128)(2,1)S(1)}, u32[]{:S(2)}, u32[]{:S(2)}) collective-permute-start(bf16[272,256]{1,0:T(8,128)(2,1)S(1)} %get-tuple-element.27.refs_0_), channel_id=1, source_target_pairs={{0,12},{1,13},{2,14},{3,15},{4,0},{5,1},{6,2},{7,3},{8,4},{9,5},{1... | collective-permute-start | bytes 417800 | tf_op jit(solution)/shard_map/ppermute | solution.py:351
  15.5 10.4 %collective-permute-start.2 = (bf16[272,256]{1,0:T(8,128)(2,1)S(1)}, bf16[272,256]{1,0:T(8,128)(2,1)S(1)}, u32[]{:S(2)}, u32[]{:S(2)}) collective-permute-start(bf16[272,256]{1,0:T(8,128)(2,1)S(1)} %get-tuple-element.27.refs_0_), channel_id=1, source_target_pairs={{0,4},{1,5},{2,6},{3,7},{4,8},{5,9},{6,10},{7,11},{8,12},{9,13},{1... | collective-permute-start | bytes 417800 | tf_op jit(solution)/shard_map/ppermute | solution.py:351
  15.6 11.0 %collective-permute-start.7 = (bf16[272,256]{1,0:T(8,128)(2,1)S(1)}, bf16[272,256]{1,0:T(8,128)(2,1)S(1)}, u32[]{:S(2)}, u32[]{:S(2)}) collective-permute-start(bf16[272,256]{1,0:T(8,128)(2,1)S(1)} %get-tuple-element.27.refs_0_), channel_id=1, source_target_pairs={{0,2},{1,3},{2,4},{3,5},{4,6},{5,7},{6,8},{7,9},{8,10},{9,11},{10,... | collective-permute-start | bytes 417800 | tf_op jit(solution)/shard_map/ppermute | solution.py:351
  18.4 9.9 %collective-permute-start.10 = (bf16[272,256]{1,0:T(8,128)(2,1)S(1)}, bf16[272,256]{1,0:T(8,128)(2,1)S(1)}, u32[]{:S(2)}, u32[]{:S(2)}) collective-permute-start(bf16[272,256]{1,0:T(8,128)(2,1)S(1)} %collective-permute-done.9), channel_id=1, source_target_pairs={{0,12},{1,13},{2,14},{3,15},{4,0},{5,1},{6,2},{7,3},{8,4},{9,5},{1... | collective-permute-start | bytes 417800 | tf_op jit(solution)/shard_map/ppermute | solution.py:351
  26.0 8.1 %collective-permute-start.8 = (bf16[272,256]{1,0:T(8,128)(2,1)S(1)}, bf16[272,256]{1,0:T(8,128)(2,1)S(1)}, u32[]{:S(2)}, u32[]{:S(2)}) collective-permute-start(bf16[272,256]{1,0:T(8,128)(2,1)S(1)} %collective-permute-done.2.after.refs_2_), channel_id=1, source_target_pairs={{0,2},{1,3},{2,4},{3,5},{4,6},{5,7},{6,8},{7,9},{8,10},{9,11},{10,... | collective-permute-start | bytes 417800 | tf_op jit(solution)/shard_map/ppermute | solution.py:351
  26.5 21.7 %collective-permute-start.3 = (bf16[272,256]{1,0:T(8,128)(2,1)S(1)}, bf16[272,256]{1,0:T(8,128)(2,1)S(1)}, u32[]{:S(2)}, u32[]{:S(2)}) collective-permute-start(bf16[272,256]{1,0:T(8,128)(2,1)S(1)} %tied.1.refs_0_), channel_id=1, source_target_pairs={{0,2},{1,3},{2,4},{3,5},{4,6},{5,7},{6,8},{7,9},{8,10},{9,11},{10,... | collective-permute-start | bytes 417800 | tf_op jit(solution)/shard_map/ppermute | solution.py:351
  26.6 22.4 %collective-permute-start.4 = (bf16[272,256]{1,0:T(8,128)(2,1)S(1)}, bf16[272,256]{1,0:T(8,128)(2,1)S(1)}, u32[]{:S(2)}, u32[]{:S(2)}) collective-permute-start(bf16[272,256]{1,0:T(8,128)(2,1)S(1)} %tied.1.refs_0_), channel_id=1, source_target_pairs={{0,4},{1,5},{2,6},{3,7},{4,8},{5,9},{6,10},{7,11},{8,12},{9,13},{1... | collective-permute-start | bytes 417800 | tf_op jit(solution)/shard_map/ppermute | solution.py:351
  28.4 24.5 %collective-permute-start.5 = (bf16[272,256]{1,0:T(8,128)(2,1)S(1)}, bf16[272,256]{1,0:T(8,128)(2,1)S(1)}, u32[]{:S(2)}, u32[]{:S(2)}) collective-permute-start(bf16[272,256]{1,0:T(8,128)(2,1)S(1)} %tied.1.refs_0_), channel_id=1, source_target_pairs={{0,6},{1,7},{2,8},{3,9},{4,10},{5,11},{6,12},{7,13},{8,14},{9,15},... | collective-permute-start | bytes 417800 | tf_op jit(solution)/shard_map/ppermute | solution.py:351
  34.0 19.7 %collective-permute-start.6 = (bf16[272,256]{1,0:T(8,128)(2,1)S(1)}, bf16[272,256]{1,0:T(8,128)(2,1)S(1)}, u32[]{:S(2)}, u32[]{:S(2)}) collective-permute-start(bf16[272,256]{1,0:T(8,128)(2,1)S(1)} %tied.1.refs_0_), channel_id=1, source_target_pairs={{0,8},{1,9},{2,10},{3,11},{4,12},{5,13},{6,14},{7,15},{8,0},{9,1},... | collective-permute-start | bytes 417800 | tf_op jit(solution)/shard_map/ppermute | solution.py:351
  46.6 9.6 %collective-permute-start.11 = (bf16[256,256]{1,0:T(8,128)(2,1)S(1)}, bf16[256,256]{1,0:T(8,128)(2,1)S(1)}, u32[]{:S(2)}, u32[]{:S(2)}) collective-permute-start(bf16[256,256]{1,0:T(8,128)(2,1)S(1)} %get-tuple-element.28), channel_id=1, source_target_pairs={{0,14},{1,15},{2,0},{3,1},{4,2},{5,3},{6,4},{7,5},{8,6},{9,7},{10,... | collective-permute-start | bytes 393224 | tf_op jit(solution)/shard_map/ppermute | solution.py:351
  48.2 27.1 %collective-permute-start.14 = (bf16[128,1024]{1,0:T(8,128)(2,1)S(1)}, bf16[128,1024]{1,0:T(8,128)(2,1)S(1)}, u32[]{:S(2)}, u32[]{:S(2)}) collective-permute-start(bf16[128,1024]{1,0:T(8,128)(2,1)S(1)} %get-tuple-element.32), channel_id=1, source_target_pairs={{0,192},{64,0},{128,64},{192,128},{1,193},{65,1},{129,65},{193,129... | collective-permute-start | bytes 786440 | tf_op jit(solution)/shard_map/ppermute | solution.py:360
  49.0 26.3 %collective-permute-start.15 = (bf16[128,1024]{1,0:T(8,128)(2,1)S(1)}, bf16[128,1024]{1,0:T(8,128)(2,1)S(1)}, u32[]{:S(2)}, u32[]{:S(2)}) collective-permute-start(bf16[128,1024]{1,0:T(8,128)(2,1)S(1)} %get-tuple-element.33), channel_id=1, source_target_pairs={{0,193},{1,192},{2,195},{3,194},{4,197},{5,196},{6,199},{7,198},{8... | collective-permute-start | bytes 786440 | tf_op jit(solution)/shard_map/ppermute | solution.py:368
  52.9 13.8 %collective-permute-start.16 = (bf16[256,256]{1,0:T(8,128)(2,1)S(1)}, bf16[256,256]{1,0:T(8,128)(2,1)S(1)}, u32[]{:S(2)}, u32[]{:S(2)}) collective-permute-start(bf16[256,256]{1,0:T(8,128)(2,1)S(1)} %get-tuple-element.35), channel_id=1, source_target_pairs={{0,12},{1,13},{2,14},{3,15},{4,0},{5,1},{6,2},{7,3},{8,4},{9,5},{1... | collective-permute-start | bytes 393224 | tf_op jit(solution)/shard_map/ppermute | solution.py:351
  53.7 18.8 %collective-permute-start.17 = (bf16[256,256]{1,0:T(8,128)(2,1)S(1)}, bf16[256,256]{1,0:T(8,128)(2,1)S(1)}, u32[]{:S(2)}, u32[]{:S(2)}) collective-permute-start(bf16[256,256]{1,0:T(8,128)(2,1)S(1)} %get-tuple-element.36), channel_id=1, source_target_pairs={{0,10},{1,11},{2,12},{3,13},{4,14},{5,15},{6,0},{7,1},{8,2},{9,3},... | collective-permute-start | bytes 393224 | tf_op jit(solution)/shard_map/ppermute | solution.py:351
  56.2 19.1 %collective-permute-start.18 = (bf16[256,256]{1,0:T(8,128)(2,1)S(1)}, bf16[256,256]{1,0:T(8,128)(2,1)S(1)}, u32[]{:S(2)}, u32[]{:S(2)}) collective-permute-start(bf16[256,256]{1,0:T(8,128)(2,1)S(1)} %get-tuple-element.37), channel_id=1, source_target_pairs={{0,8},{1,9},{2,10},{3,11},{4,12},{5,13},{6,14},{7,15},{8,0},{9,1},... | collective-permute-start | bytes 393224 | tf_op jit(solution)/shard_map/ppermute | solution.py:351
  66.7 16.1 %collective-permute-start.12 = (bf16[128,1024]{1,0:T(8,128)(2,1)S(1)}, bf16[128,1024]{1,0:T(8,128)(2,1)S(1)}, u32[]{:S(2)}, u32[]{:S(2)}) collective-permute-start(bf16[128,1024]{1,0:T(8,128)(2,1)S(1)} %get-tuple-element.29), channel_id=1, source_target_pairs={{0,64},{64,128},{128,192},{192,0},{1,65},{65,129},{129,193},{193,1... | collective-permute-start | bytes 786440 | tf_op jit(solution)/shard_map/ppermute | solution.py:360
  72.6 10.2 %collective-permute-start.13 = (bf16[128,1024]{1,0:T(8,128)(2,1)S(1)}, bf16[128,1024]{1,0:T(8,128)(2,1)S(1)}, u32[]{:S(2)}, u32[]{:S(2)}) collective-permute-start(bf16[128,1024]{1,0:T(8,128)(2,1)S(1)} %get-tuple-element.30), channel_id=1, source_target_pairs={{0,65},{1,64},{2,67},{3,66},{4,69},{5,68},{6,71},{7,70},{8,73},{9,... | collective-permute-start | bytes 786440 | tf_op jit(solution)/shard_map/ppermute | solution.py:368
  76.0 6.3 %collective-permute-start.19 = (bf16[256,256]{1,0:T(8,128)(2,1)S(1)}, bf16[256,256]{1,0:T(8,128)(2,1)S(1)}, u32[]{:S(2)}, u32[]{:S(2)}) collective-permute-start(bf16[256,256]{1,0:T(8,128)(2,1)S(1)} %total.1), channel_id=1, source_target_pairs={{0,192},{64,0},{128,64},{192,128},{1,193},{65,1},{129,65},{193,129... | collective-permute-start | bytes 393224 | tf_op jit(solution)/shard_map/ppermute | solution.py:360
  82.2 5.0 %collective-permute-start.20 = (bf16[256,256]{1,0:T(8,128)(2,1)S(1)}, bf16[256,256]{1,0:T(8,128)(2,1)S(1)}, u32[]{:S(2)}, u32[]{:S(2)}) collective-permute-start(bf16[256,256]{1,0:T(8,128)(2,1)S(1)} %collective-permute-done.19.refs_2_), channel_id=1, source_target_pairs={{0,1},{1,0},{2,3},{3,2},{4,5},{5,4},{6,7},{7,6},{8,9},{9,8},{10,11... | collective-permute-start | bytes 393224 | tf_op jit(solution)/shard_map/ppermute | solution.py:355

commit v4 on v3

--- a/solution.py
+++ b/solution.py
@@ -90,16 +90,15 @@
         out[PAIR:, HEAD:] = got[ROWS:, one]
 
 
-def other_half_kernel(where_ref, *refs, count):
-    start = pl.multiple_of((1 - where_ref[0]) * HALF, HALF)
-    ins, out, sems = refs[:count], refs[-2], refs[-1]
-    fetched(
-        [
-            (ref.at[:, pl.ds(start, HALF)], out.at[:, at * HALF : (at + 1) * HALF])
-            for at, ref in enumerate(ins)
-        ],
-        sems,
-    )
+def halves_kernel(where_ref, *refs):
+    ins, (mine, theirs, sems) = refs[:3], refs[4:]
+    copies = []
+    for i, ref in enumerate(ins):
+        cols = slice(i * HALF, (i + 1) * HALF)
+        for side, out in ((where_ref[0], mine), (1 - where_ref[0], theirs)):
+            start = pl.multiple_of(side * HALF, HALF)
+            copies.append((ref.at[:, pl.ds(start, HALF)], out.at[:, cols]))
+    fetched(copies, sems)
 
 
 def total_kernel(where_ref, *refs):
@@ -126,10 +125,9 @@
     for i, at in enumerate((side, 1 - side)):
         wide = pl.ds(pl.multiple_of(at * HALF, HALF), HALF)
         head = pl.ds(pl.multiple_of(at * HEAD, HEAD), HEAD)
-        rows = pl.ds(i * ROWS, ROWS)
         copies.append((ins[i], dq.at[:, wide]))
-        copies.append((ins[2 + i].at[rows, :HEAD], dk.at[:, head]))
-        copies.append((ins[2 + i].at[rows, HEAD:], dv.at[:, head]))
+        copies.append((ins[2 + i].at[:ROWS, :HEAD], dk.at[:, head]))
+        copies.append((ins[2 + i].at[:ROWS, HEAD:], dv.at[:, head]))
     fetched(copies, sems)
 
 
@@ -182,9 +180,8 @@
 
 
 def head_rows(own, crossed, g, offset=0):
-    at = slice(g * HEAD, (g + 1) * HEAD)
-    far = slice(offset + g * HEAD, offset + (g + 1) * HEAD)
-    return jnp.concatenate([own[:, at], crossed[:, far]], axis=0)
+    at = slice(offset + g * HEAD, offset + (g + 1) * HEAD)
+    return jnp.concatenate([own[:, at], crossed[:, at]], axis=0)
 
 
 def put_rows(g, columns, own, crossed):
@@ -194,17 +191,13 @@
     crossed[:, at] = rows[ROWS:]
 
 
-def fwd_kernel(where_ref, q_hbm, qx_ref, *refs):
+def fwd_kernel(where_ref, q_ref, qx_ref, *refs):
     blocks, refs = refs[:SLOTS], refs[SLOTS + 1 :]
-    o_own, o_cross, cap, s_ref, e_ref, keys, vt_ref, q_ref, sems = refs
-    base = pl.multiple_of(where_ref[0] * HALF, HALF)
-    fetch = pltpu.make_async_copy(q_hbm.at[:, pl.ds(base, HALF)], q_ref, sems.at[0])
-    fetch.start()
+    o_own, o_cross, cap, s_ref, e_ref, keys, vt_ref = refs
     fill_cap(where_ref, blocks, cap)
     for k, b in enumerate(blocks):
         keys[slot(k), :] = b[:PAIR, :HEAD]
         vt_ref[:, slot(k)] = b[:PAIR, HEAD:].T
-    fetch.wait()
 
     def score(g):
         s_ref[g % 2] = dot(keys[...], head_rows(q_ref, qx_ref, g, 2 * HALF).T)
@@ -224,39 +217,31 @@
         put_rows(g, dot(vt_ref[...], e_ref[now]) * inv, o_own, o_cross)
 
 
-def bwd_kernel(where_ref, q_hbm, d_hbm, qdx_ref, *refs):
+def bwd_kernel(where_ref, qd_ref, qdx_ref, *refs):
     blocks, refs = refs[:SLOTS], refs[SLOTS:]
     dq_own, dq_cross = refs[:2]
     parts, refs = refs[2 : SLOTS + 2], refs[SLOTS + 2 :]
-    cap, s_ref, dp_ref, e_ref, ds_ref, qs_ref, gs_ref, acc, keys, values, kt_ref, qd_ref, sems = refs
-    base = pl.multiple_of(where_ref[0] * HALF, HALF)
-    fetch = [
-        pltpu.make_async_copy(h.at[:, pl.ds(base, HALF)], qd_ref.at[i], sems.at[i])
-        for i, h in enumerate((q_hbm, d_hbm))
-    ]
-    for c in fetch:
-        c.start()
+    cap, s_ref, dp_ref, e_ref, ds_ref, qs_ref, gs_ref, acc, keys, values, kt_ref, turned = refs
     fill_cap(where_ref, blocks, cap)
     for k, b in enumerate(blocks):
         keys[slot(k), :] = b[:PAIR, :HEAD]
         values[slot(k), :] = b[:PAIR, HEAD:]
         kt_ref[:, slot(k)] = b[:PAIR, :HEAD].T
-    for c in fetch:
-        c.wait()
 
     def rows_of(which, g):
-        return head_rows(qd_ref.at[which], qdx_ref, g, which * HALF)
+        return head_rows(qd_ref, qdx_ref, g, which * HALF)
 
     def products(g):
-        s_ref[g % 2] = dot(keys[...], rows_of(0, g).T)
-        dp_ref[g % 2] = dot(values[...], rows_of(1, g).T)
+        for i, (block, out) in enumerate(((keys, s_ref), (values, dp_ref))):
+            turned[g % 2, i] = rows_of(i, g).T
+            out[g % 2] = dot(block[...], turned[g % 2, i])
 
     def span_of(g, count=1):
         return slice(g * PAIR, (g + count) * PAIR)
 
     def key_terms(g):
         span = span_of(g, 2)
-        both = dot(ds_ref[:, span], qs_ref[span, :]), dot(e_ref[:, span], gs_ref[span, :])
+        both = dot_nt(qs_ref[:, span], ds_ref[:, span]), dot_nt(gs_ref[:, span], e_ref[:, span])
         for i, terms in enumerate(both):
             acc[i] = terms if g == 0 else acc[i] + terms
 
@@ -277,46 +262,43 @@
             inner = joined(inner, folded(expo * dp_ref[now, slot(k), :], jnp.sum), jnp.add)
         inv = 1.0 / jnp.sum(total, axis=0, keepdims=True)
         delta = jnp.sum(inner, axis=0, keepdims=True) * inv
-        factor = jnp.broadcast_to(inv, (HEAD, PAIR)).T
-        qs_ref[cols, :] = (rows_of(0, g).astype(F32) * factor).astype(BF16)
-        gs_ref[cols, :] = (rows_of(1, g).astype(F32) * factor).astype(BF16)
+        qs_ref[:, cols] = (turned[now, 0].astype(F32) * inv).astype(BF16)
+        gs_ref[:, cols] = (turned[now, 1].astype(F32) * inv).astype(BF16)
         for k in range(SLOTS):
             ds = (dp_ref[now, slot(k), :] - delta).astype(BF16)
             ds_ref[slot(k), cols] = e_ref[slot(k), cols] * ds
         put_rows(g, dot(kt_ref[...], ds_ref[:, cols]) * (inv * SCALE), dq_own, dq_cross)
     key_terms(GROUP - 2)
     for k in range(SLOTS):
-        parts[k][:, :HEAD] = (acc[0, slot(k), :] * SCALE).astype(BF16)
-        parts[k][:, HEAD:] = acc[1, slot(k), :].astype(BF16)
+        parts[k][:, :HEAD] = (acc[0, :, slot(k)] * SCALE).T.astype(BF16)
+        parts[k][:, HEAD:] = acc[1, :, slot(k)].T.astype(BF16)
 
 
 MATMUL = 2 * GROUP * PAIR * KEYS * HEAD
 FINAL_FLOPS = 2 * MATMUL
 
 
-def run_fwd(where, query, crossed, blocks, after):
+def run_fwd(where, own, crossed, blocks, after):
     scratch = [
         pltpu.VMEM((KEYS, PAIR), F32),
         pltpu.VMEM((2, KEYS, PAIR), F32),
         pltpu.VMEM((2, KEYS, PAIR), BF16),
         pltpu.VMEM((KEYS, HEAD), BF16),
         pltpu.VMEM((HEAD, KEYS), BF16),
-        pltpu.VMEM((ROWS, HALF), BF16),
-        pltpu.SemaphoreType.DMA((1,)),
     ]
     return call(
         fwd_kernel,
         [shape(ROWS, HALF)] * 2,
-        [HBM] + [VMEM] * (1 + SLOTS) + [ANY] * 1,
+        [VMEM] * (2 + SLOTS) + [ANY] * 1,
         scratch,
         2 * MATMUL,
         2**21,
         "fwd",
         limit=20,
-    )(where, query, crossed, *blocks, *after)
-
-
-def run_bwd(where, query, grad, crossed, blocks):
+    )(where, own, crossed, *blocks, *after)
+
+
+def run_bwd(where, own, crossed, blocks):
     outs = [shape(ROWS, HALF)] * 2 + [shape(PAIR, 2 * HEAD)] * SLOTS
     scratch = [
         pltpu.VMEM((KEYS, PAIR), F32),
@@ -324,25 +306,24 @@
         pltpu.VMEM((2, KEYS, PAIR), F32),
         pltpu.VMEM((KEYS, GROUP * PAIR), BF16),
         pltpu.VMEM((KEYS, GROUP * PAIR), BF16),
-        pltpu.VMEM((GROUP * PAIR, HEAD), BF16),
-        pltpu.VMEM((GROUP * PAIR, HEAD), BF16),
-        pltpu.VMEM((2, KEYS, HEAD), F32),
+        pltpu.VMEM((HEAD, GROUP * PAIR), BF16),
+        pltpu.VMEM((HEAD, GROUP * PAIR), BF16),
+        pltpu.VMEM((2, HEAD, KEYS), F32),
         pltpu.VMEM((KEYS, HEAD), BF16),
         pltpu.VMEM((KEYS, HEAD), BF16),
         pltpu.VMEM((HEAD, KEYS), BF16),
-        pltpu.VMEM((2, ROWS, HALF), BF16),
-        pltpu.SemaphoreType.DMA((2,)),
+        pltpu.VMEM((2, 2, HEAD, PAIR), BF16),
     ]
     out = call(
         bwd_kernel,
         outs,
-        [HBM] * 2 + [VMEM] * (1 + SLOTS),
+        2 + SLOTS,
         scratch,
         5 * MATMUL,
         2**22,
         "bwd",
         limit=32,
-    )(where, query, grad, crossed, *blocks)
+    )(where, own, crossed, *blocks)
     return out[0], out[1], out[2:]
 
 
@@ -406,17 +387,6 @@
     )(where, held, after)
 
 
-def other_half(where, arrays, after, name):
-    (out,) = call(
-        functools.partial(other_half_kernel, count=len(arrays)),
-        [shape(ROWS, len(arrays) * HALF)],
-        [HBM] * len(arrays) + [ANY],
-        [pltpu.SemaphoreType.DMA((len(arrays),))],
-        name=name,
-    )(where, *arrays, after)
-    return out
-
-
 def per_device(qf, kf, vf, sf, qb, kb, vb, sb, grad):
     index = lax.axis_index("cp")
     side = index % 2
@@ -428,7 +398,13 @@
     )
 
     keep, send = split(where, kb, vb, sb, kf, vf, sf)
-    halves = other_half(where, (qb, grad, qf), send, "halves")
+    own, halves = call(
+        halves_kernel,
+        [shape(ROWS, 3 * HALF)] * 2,
+        [HBM] * 3 + [ANY],
+        [pltpu.SemaphoreType.DMA((6,))],
+        name="halves",
+    )(where, qb, grad, qf, send)
     b0, f0, halves = join(where, keep, swapped(send), halves)
     b4 = along_z(b0, -2)
     b2 = along_z(b0, 2)
@@ -439,10 +415,10 @@
     f0 = tied(where, f0, b2)
     blocks_f = [f0] + [along_z(f0, k) for k in (1, 2, 3, 4)]
 
-    dq_own, dq_cross, parts = run_bwd(where, qb, grad, crossed, (b0, b1, b2, b3, b4))
+    dq_own, dq_cross, parts = run_bwd(where, own, crossed, (b0, b1, b2, b3, b4))
     terms = [parts[0]] + [along_z(parts[k], -k) for k in range(1, SLOTS)]
     dq = handed(dq_own, -1), handed_across(dq_cross, -1)
-    o_own, o_cross = run_fwd(where, qf, crossed, blocks_f, (terms[1],))
+    o_own, o_cross = run_fwd(where, own, crossed, blocks_f, (terms[1],))
     dq = handed(dq_own, -1), handed_across(dq_cross, -1)
     (summed,) = call(
         total_kernel, [shape(PAIR, 2 * HEAD)], [VMEM] * SLOTS + [ANY] * 2, name="total"
@@ -464,7 +440,7 @@
         [pltpu.SemaphoreType.DMA((6,))],
         name="final",
         place=HBM,
-    )(where, *dq, received, swapped(received), token)
+    )(where, *dq, received, swapped(received[ROWS:]), token)
     return tuple(out[None] for out in (attn_out, *grads))
 
 

time: 89 us -> 87.2 us (0.980)
  Pallas kernels: 25.6 us -> 23.5 us
  waiting for transfers between devices: 26 us -> 27.9 us
  starting transfers between devices: 36.1 us -> 34.7 us
    ppermute x13, waiting for transfers between devices: 14.4 us -> 17.3 us  [along_z(): lax.ppermute(block, 'cp', [(i, (i + 2 * distance) % n) for i in range(n)])]
    pallas_call x3, Pallas kernels: 19.5 us -> 17.4 us  [the longest x1 10.5 us: run_bwd(): call(bwd_kernel, outs, 2 + SLOTS, scratch, 5 * MATMUL, 2 ** 22, 'bwd', li...]
    ppermute x3, waiting for transfers between devices: 5.44 us -> 4.4 us  [swapped(): lax.ppermute(block, 'cp', [(i, i ^ 1) for i in range(lax.axis_size('cp'))])]
  transfers between devices with their start and end apart: 21 -> 21, of which waited for: 8 -> 8; matrix products, arithmetic and copies ran while one was open for 0% -> 0% of each run, Pallas kernels for 25% -> 23%
where the time goes in v4:
time: 87.2 us; the launch traced here: 87.1 us
  starting transfers between devices  34.7 us (40%)
  waiting for transfers between devices  27.9 us (32%)
  Pallas kernels  23.5 us (27%)
  between operations  0.93 us (1%)
    ppermute x13, starting transfers between devices, along_z(): lax.ppermute(block, 'cp', [(i, (i + 2 * distance) % n) for i in range(n)])  27.3 us
    ppermute x13, waiting for transfers between devices, along_z(): lax.ppermute(block, 'cp', [(i, (i + 2 * distance) % n) for i in range(n)])  17.3 us
    pallas_call x1, Pallas kernels, run_bwd(): call(bwd_kernel, outs, 2 + SLOTS, scratch, 5 * MATMUL, 2 ** 22, 'bwd', li...  10.5 us
    ppermute x3, waiting for transfers between devices, handed(): lax.ppermute(block, 'section', [(i, (i + distance) % n) for i in range(n)])  6.13 us
    pallas_call x1, Pallas kernels, run_fwd(): call(fwd_kernel, [shape(ROWS, HALF)] * 2, [VMEM] * (2 + SLOTS) + [ANY] *...  4.97 us
    ppermute x3, waiting for transfers between devices, swapped(): lax.ppermute(block, 'cp', [(i, i ^ 1) for i in range(lax.axis_size('cp'))])  4.4 us
    ppermute x3, starting transfers between devices, swapped(): lax.ppermute(block, 'cp', [(i, i ^ 1) for i in range(lax.axis_size('cp'))])  3.8 us
    ppermute x2, starting transfers between devices, handed_across(): return lax.ppermute(block, ('section', 'cp'), route)  2.39 us
  transfers between devices with their start and end apart: 21, of which 8 were waited for; matrix products, arithmetic and copies ran while one was open for 0% of the time, Pallas kernels for 23%

profile of v4, /device:TPU:56, one launch (start us, length us, event | category | flops | bytes accessed | tf_op | source)
XLA Modules:
  0.0 87.1 jit_solution(5226751720495549704)
XLA Ops:
  0.6 0.1 pad_add_fusion.where_ref
  0.7 1.6 %split.1 = (bf16[144,512]{1,0:T(8,128)(2,1)S(1)}, bf16[144,512]{1,0:T(8,128)(2,1)S(1)}) custom-call(s32[2]{0:T(128)S(1)} %pad_add_fusion.where_ref, bf16[128,256]{1,0:T(8,128)(2,1)} %bitcast.16, bf16[128,256]{1,0:T(8,128)(2,1)} %bitcast.17, s32[1,128]{1,0:T(1,128)} %refs_2_.1, bf16[128,256]{1,0:T(8,128)(2,1)} %bitcast.18, bf16[128,256]{1,0:T(8,128)(2,1)} %bitcast.19, ...), custom_call_target="tpu_custom_call" | custom-call | bytes 524288 | tf_op jit(solution)/shard_map/split/pallas_call | solution.py:359
  2.3 1.6 %collective-permute-start = (bf16[144,512]{1,0:T(8,128)(2,1)S(1)}, bf16[144,512]{1,0:T(8,128)(2,1)S(1)}, u32[]{:S(2)}, u32[]{:S(2)}) collective-permute-start(bf16[144,512]{1,0:T(8,128)(2,1)S(1)} %get-tuple-element.25.refs_3_), channel_id=1, source_target_pairs={{0,1},{1,0},{2,3},{3,2},{4,5},{5,4},{6,7},{7,6},{8,9},{9,8},{10,11... | collective-permute-start | bytes 442376 | tf_op jit(solution)/shard_map/ppermute | solution.py:336
  3.9 1.9 %halves.1 = (bf16[128,3072]{1,0:T(8,128)(2,1)S(1)}, bf16[128,3072]{1,0:T(8,128)(2,1)S(1)}) custom-call(s32[2]{0:T(128)S(1)} %pad_add_fusion.where_ref, bf16[128,2048]{1,0:T(8,128)(2,1)} %bitcast.13, bf16[128,2048]{1,0:T(8,128)(2,1)} %bitcast.14, bf16[128,2048]{1,0:T(8,128)(2,1)} %bitcast.15, bf16[144,512]{1,0:T(8,128)(2,1)S(1)} %get-tuple-element.25.refs_3_), custom_call_target="tpu_custom_call" | custom-call | bytes 524288 | tf_op jit(solution)/shard_map/halves/pallas_call | solution.py:401
  5.9 2.1 %collective-permute-done.got = bf16[144,512]{1,0:T(8,128)(2,1)S(1)} collective-permute-done((bf16[144,512]{1,0:T(8,128)(2,1)S(1)}, bf16[144,512]{1,0:T(8,128)(2,1)S(1)}, u32[]{:S(2)}, u32[]{:S(2)}) %collective-permute-start) | collective-permute-done | bytes 147488 | tf_op jit(solution)/shard_map/ppermute | solution.py:336
  8.0 0.6 join.1
  8.6 1.6 %collective-permute-start.1 = (bf16[128,3072]{1,0:T(8,128)(2,1)S(1)}, bf16[128,3072]{1,0:T(8,128)(2,1)S(1)}, u32[]{:S(2)}, u32[]{:S(2)}) collective-permute-start(bf16[128,3072]{1,0:T(8,128)(2,1)S(1)} %get-tuple-element.29), channel_id=1, source_target_pairs={{0,1},{1,0},{2,3},{3,2},{4,5},{5,4},{6,7},{7,6},{8,9},{9,8},{10,11... | collective-permute-start | bytes 2359304 | tf_op jit(solution)/shard_map/ppermute | solution.py:336
  10.1 5.4 %collective-permute-start.9 = (bf16[272,256]{1,0:T(8,128)(2,1)S(1)}, bf16[272,256]{1,0:T(8,128)(2,1)S(1)}, u32[]{:S(2)}, u32[]{:S(2)}) collective-permute-start(bf16[272,256]{1,0:T(8,128)(2,1)S(1)} %get-tuple-element.31.refs_0_), channel_id=1, source_target_pairs={{0,12},{1,13},{2,14},{3,15},{4,0},{5,1},{6,2},{7,3},{8,4},{9,5},{1... | collective-permute-start | bytes 417800 | tf_op jit(solution)/shard_map/ppermute | solution.py:332
  15.5 0.0 collective-permute-start.2
  15.6 1.0 %collective-permute-start.7 = (bf16[272,256]{1,0:T(8,128)(2,1)S(1)}, bf16[272,256]{1,0:T(8,128)(2,1)S(1)}, u32[]{:S(2)}, u32[]{:S(2)}) collective-permute-start(bf16[272,256]{1,0:T(8,128)(2,1)S(1)} %get-tuple-element.31.refs_0_), channel_id=1, source_target_pairs={{0,2},{1,3},{2,4},{3,5},{4,6},{5,7},{6,8},{7,9},{8,10},{9,11},{10,... | collective-permute-start | bytes 417800 | tf_op jit(solution)/shard_map/ppermute | solution.py:332
  16.6 1.9 %collective-permute-done.9 = bf16[272,256]{1,0:T(8,128)(2,1)S(1)} collective-permute-done((bf16[272,256]{1,0:T(8,128)(2,1)S(1)}, bf16[272,256]{1,0:T(8,128)(2,1)S(1)}, u32[]{:S(2)}, u32[]{:S(2)}) %collective-permute-start.9) | collective-permute-done | bytes 139296 | tf_op jit(solution)/shard_map/ppermute | solution.py:332
  18.4 4.6 %collective-permute-start.10 = (bf16[272,256]{1,0:T(8,128)(2,1)S(1)}, bf16[272,256]{1,0:T(8,128)(2,1)S(1)}, u32[]{:S(2)}, u32[]{:S(2)}) collective-permute-start(bf16[272,256]{1,0:T(8,128)(2,1)S(1)} %collective-permute-done.9), channel_id=1, source_target_pairs={{0,12},{1,13},{2,14},{3,15},{4,0},{5,1},{6,2},{7,3},{8,4},{9,5},{1... | collective-permute-start | bytes 417800 | tf_op jit(solution)/shard_map/ppermute | solution.py:332
  23.0 2.9 %collective-permute-done.2.after.refs_2_ = bf16[272,256]{1,0:T(8,128)(2,1)S(1)} collective-permute-done((bf16[272,256]{1,0:T(8,128)(2,1)S(1)}, bf16[272,256]{1,0:T(8,128)(2,1)S(1)}, u32[]{:S(2)}, u32[]{:S(2)}) %collective-permute-start.2) | collective-permute-done | bytes 139296 | tf_op jit(solution)/shard_map/ppermute | solution.py:332
  26.0 0.0 collective-permute-start.8
  26.0 0.5 tied.1.refs_0_
  26.5 0.1 collective-permute-start.3
  26.6 0.0 collective-permute-done.7.refs_1_
  26.6 1.8 %collective-permute-start.4 = (bf16[272,256]{1,0:T(8,128)(2,1)S(1)}, bf16[272,256]{1,0:T(8,128)(2,1)S(1)}, u32[]{:S(2)}, u32[]{:S(2)}) collective-permute-start(bf16[272,256]{1,0:T(8,128)(2,1)S(1)} %tied.1.refs_0_), channel_id=1, source_target_pairs={{0,4},{1,5},{2,6},{3,7},{4,8},{5,9},{6,10},{7,11},{8,12},{9,13},{1... | collective-permute-start | bytes 417800 | tf_op jit(solution)/shard_map/ppermute | solution.py:332
  28.4 0.0 collective-permute-done.10.refs_4_
  28.4 4.4 %collective-permute-start.5 = (bf16[272,256]{1,0:T(8,128)(2,1)S(1)}, bf16[272,256]{1,0:T(8,128)(2,1)S(1)}, u32[]{:S(2)}, u32[]{:S(2)}) collective-permute-start(bf16[272,256]{1,0:T(8,128)(2,1)S(1)} %tied.1.refs_0_), channel_id=1, source_target_pairs={{0,6},{1,7},{2,8},{3,9},{4,10},{5,11},{6,12},{7,13},{8,14},{9,15},... | collective-permute-start | bytes 417800 | tf_op jit(solution)/shard_map/ppermute | solution.py:332
  32.8 1.2 %collective-permute-done.8.refs_3_ = bf16[272,256]{1,0:T(8,128)(2,1)S(1)} collective-permute-done((bf16[272,256]{1,0:T(8,128)(2,1)S(1)}, bf16[272,256]{1,0:T(8,128)(2,1)S(1)}, u32[]{:S(2)}, u32[]{:S(2)}) %collective-permute-start.8) | collective-permute-done | bytes 139296 | tf_op jit(solution)/shard_map/ppermute | solution.py:332
  34.0 0.7 collective-permute-start.6
  34.8 0.0 collective-permute-done.1.qdx_ref.qx_ref
  34.8 10.5 %bwd.1 = (bf16[128,1024]{1,0:T(8,128)(2,1)S(1)}, bf16[128,1024]{1,0:T(8,128)(2,1)S(1)}, bf16[256,256]{1,0:T(8,128)(2,1)S(1)}, bf16[256,256]{1,0:T(8,128)(2,1)S(1...) custom-call(s32[2]{0:T(128)S(1)} %pad_add_fusion.where_ref, ...), custom_call_target="tpu_custom_call" | custom-call | flops 3355443200 | bytes 4194304 | tf_op jit(solution)/shard_map/bwd/pallas_call | solution.py:317
  45.2 1.6 %collective-permute-start.11 = (bf16[256,256]{1,0:T(8,128)(2,1)S(1)}, bf16[256,256]{1,0:T(8,128)(2,1)S(1)}, u32[]{:S(2)}, u32[]{:S(2)}) collective-permute-start(bf16[256,256]{1,0:T(8,128)(2,1)S(1)} %get-tuple-element.32), channel_id=1, source_target_pairs={{0,14},{1,15},{2,0},{3,1},{4,2},{5,3},{6,4},{7,5},{8,6},{9,7},{10,... | collective-permute-start | bytes 393224 | tf_op jit(solution)/shard_map/ppermute | solution.py:332
  46.9 0.0 collective-permute-done.3.refs_1_
  46.9 0.7 collective-permute-start.14
  47.6 0.0 collective-permute-done.4.refs_2_
  47.6 0.4 collective-permute-start.15
  48.0 4.8 %collective-permute-done.5.refs_3_ = bf16[272,256]{1,0:T(8,128)(2,1)S(1)} collective-permute-done((bf16[272,256]{1,0:T(8,128)(2,1)S(1)}, bf16[272,256]{1,0:T(8,128)(2,1)S(1)}, u32[]{:S(2)}, u32[]{:S(2)}) %collective-permute-start.5) | collective-permute-done | bytes 139296 | tf_op jit(solution)/shard_map/ppermute | solution.py:332
  52.9 0.0 collective-permute-start.16
  52.9 0.0 collective-permute-done.6.refs_4_
  52.9 3.4 %collective-permute-start.17 = (bf16[256,256]{1,0:T(8,128)(2,1)S(1)}, bf16[256,256]{1,0:T(8,128)(2,1)S(1)}, u32[]{:S(2)}, u32[]{:S(2)}) collective-permute-start(bf16[256,256]{1,0:T(8,128)(2,1)S(1)} %get-tuple-element.40), channel_id=1, source_target_pairs={{0,10},{1,11},{2,12},{3,13},{4,14},{5,15},{6,0},{7,1},{8,2},{9,3},... | collective-permute-start | bytes 393224 | tf_op jit(solution)/shard_map/ppermute | solution.py:332
  56.2 0.0 collective-permute-done.11.refs_5_.refs_1_
  56.2 4.3 %collective-permute-start.18 = (bf16[256,256]{1,0:T(8,128)(2,1)S(1)}, bf16[256,256]{1,0:T(8,128)(2,1)S(1)}, u32[]{:S(2)}, u32[]{:S(2)}) collective-permute-start(bf16[256,256]{1,0:T(8,128)(2,1)S(1)} %get-tuple-element.41), channel_id=1, source_target_pairs={{0,8},{1,9},{2,10},{3,11},{4,12},{5,13},{6,14},{7,15},{8,0},{9,1},... | collective-permute-start | bytes 393224 | tf_op jit(solution)/shard_map/ppermute | solution.py:332
  60.5 5.0 %fwd.1 = (bf16[128,1024]{1,0:T(8,128)(2,1)S(1)}, bf16[128,1024]{1,0:T(8,128)(2,1)S(1)}) custom-call(s32[2]{0:T(128)S(1)} %pad_add_fusion.where_ref, bf16[128,3072]{1,0:T(8,128)(2,1)S(1)} %get-tuple-element.26.qd_ref.q_ref, bf16[128,3072]{1,0:T(8,128)(2,1)S(1)} %collective-permute-done.1.qdx_ref.qx_ref, bf16[272,256]{1,0:T(8,128)(2,1)S(1)} %tied.1.refs_0_, ...), custom_call_target="tpu_custom_call" | custom-call | flops 1342177280 | bytes 2097152 | tf_op jit(solution)/shard_map/fwd/pallas_call | solution.py:289
  65.5 0.0 collective-permute-done.16.refs_2_
  65.5 0.4 collective-permute-start.12
  65.9 6.4 %collective-permute-done.17.refs_3_ = bf16[256,256]{1,0:T(8,128)(2,1)S(1)} collective-permute-done((bf16[256,256]{1,0:T(8,128)(2,1)S(1)}, bf16[256,256]{1,0:T(8,128)(2,1)S(1)}, u32[]{:S(2)}, u32[]{:S(2)}) %collective-permute-start.17) | collective-permute-done | bytes 131104 | tf_op jit(solution)/shard_map/ppermute | solution.py:332
  72.3 2.0 %collective-permute-start.13 = (bf16[128,1024]{1,0:T(8,128)(2,1)S(1)}, bf16[128,1024]{1,0:T(8,128)(2,1)S(1)}, u32[]{:S(2)}, u32[]{:S(2)}) collective-permute-start(bf16[128,1024]{1,0:T(8,128)(2,1)S(1)} %get-tuple-element.34), channel_id=1, source_target_pairs={{0,65},{1,64},{2,67},{3,66},{4,69},{5,68},{6,71},{7,70},{8,73},{9,... | collective-permute-start | bytes 786440 | tf_op jit(solution)/shard_map/ppermute | solution.py:349
  74.3 0.0 collective-permute-done.18.refs_4_
  74.3 0.0 collective-permute-done.14.refs_5_.refs_0_
  74.3 0.0 collective-permute-done.15.refs_6_.refs_1_
  74.3 0.6 total.1
  74.9 0.1 collective-permute-start.19
  75.1 6.1 %collective-permute-done.19.refs_2_ = bf16[256,256]{1,0:T(8,128)(2,1)S(1)} collective-permute-done((bf16[256,256]{1,0:T(8,128)(2,1)S(1)}, bf16[256,256]{1,0:T(8,128)(2,1)S(1)}, u32[]{:S(2)}, u32[]{:S(2)}) %collective-permute-start.19) | collective-permute-done | bytes 131104 | tf_op jit(solution)/shard_map/ppermute | solution.py:341
  81.2 0.6 collective-permute-start.20
  81.8 0.0 collective-permute-done.12.own
  81.8 0.0 collective-permute-done.13.cross
  81.8 1.4 %output.1 = (bf16[128,2048]{1,0:T(8,128)(2,1)}, bf16[16,128]{1,0:T(8,128)(2,1)S(1)}) custom-call(s32[2]{0:T(128)S(1)} %pad_add_fusion.where_ref, bf16[128,1024]{1,0:T(8,128)(2,1)S(1)} %collective-permute-done.12.own, bf16[128,1024]{1,0:T(8,128)(2,1)S(1)} %collective-permute-done.13.cross), custom_call_target="tpu_custom_call" | custom-call | flops 1342177280 | bytes 524288 | tf_op jit(solution)/shard_map/output/pallas_call | solution.py:427
  83.2 2.3 %collective-permute-done.20.refs_3_ = bf16[128,256]{1,0:T(8,128)(2,1)S(1)} collective-permute-done((bf16[128,256]{1,0:T(8,128)(2,1)S(1)}, bf16[128,256]{1,0:T(8,128)(2,1)S(1)}, u32[]{:S(2)}, u32[]{:S(2)}) %collective-permute-start.20) | collective-permute-done | bytes 65568 | tf_op jit(solution)/shard_map/ppermute | solution.py:336
  85.5 1.4 %final.1 = (bf16[128,2048]{1,0:T(8,128)(2,1)}, bf16[128,256]{1,0:T(8,128)(2,1)}, bf16[128,256]{1,0:T(8,128)(2,1)}) custom-call(s32[2]{0:T(128)S(1)} %pad_add_fusion.where_ref, bf16[128,1024]{1,0:T(8,128)(2,1)S(1)} %collective-permute-done.14.refs_5_.refs_0_, bf16[128,1024]{1,0:T(8,128)(2,1)S(1)} %collective-permute-done.15.refs_6_.refs_1_, ...), custom_call_target="tpu_custom_call" | custom-call | bytes 524288 | tf_op jit(solution)/shard_map/final/pallas_call | solution.py:436
  (1 shorter events, 0.0 us)
Async XLA Ops:
  2.3 5.7 %collective-permute-start = (bf16[144,512]{1,0:T(8,128)(2,1)S(1)}, bf16[144,512]{1,0:T(8,128)(2,1)S(1)}, u32[]{:S(2)}, u32[]{:S(2)}) collective-permute-start(bf16[144,512]{1,0:T(8,128)(2,1)S(1)} %get-tuple-element.25.refs_3_), channel_id=1, source_target_pairs={{0,1},{1,0},{2,3},{3,2},{4,5},{5,4},{6,7},{7,6},{8,9},{9,8},{10,11... | collective-permute-start | bytes 442376 | tf_op jit(solution)/shard_map/ppermute | solution.py:336
  8.6 26.2 %collective-permute-start.1 = (bf16[128,3072]{1,0:T(8,128)(2,1)S(1)}, bf16[128,3072]{1,0:T(8,128)(2,1)S(1)}, u32[]{:S(2)}, u32[]{:S(2)}) collective-permute-start(bf16[128,3072]{1,0:T(8,128)(2,1)S(1)} %get-tuple-element.29), channel_id=1, source_target_pairs={{0,1},{1,0},{2,3},{3,2},{4,5},{5,4},{6,7},{7,6},{8,9},{9,8},{10,11... | collective-permute-start | bytes 2359304 | tf_op jit(solution)/shard_map/ppermute | solution.py:336
  10.1 8.3 %collective-permute-start.9 = (bf16[272,256]{1,0:T(8,128)(2,1)S(1)}, bf16[272,256]{1,0:T(8,128)(2,1)S(1)}, u32[]{:S(2)}, u32[]{:S(2)}) collective-permute-start(bf16[272,256]{1,0:T(8,128)(2,1)S(1)} %get-tuple-element.31.refs_0_), channel_id=1, source_target_pairs={{0,12},{1,13},{2,14},{3,15},{4,0},{5,1},{6,2},{7,3},{8,4},{9,5},{1... | collective-permute-start | bytes 417800 | tf_op jit(solution)/shard_map/ppermute | solution.py:332
  15.5 10.4 %collective-permute-start.2 = (bf16[272,256]{1,0:T(8,128)(2,1)S(1)}, bf16[272,256]{1,0:T(8,128)(2,1)S(1)}, u32[]{:S(2)}, u32[]{:S(2)}) collective-permute-start(bf16[272,256]{1,0:T(8,128)(2,1)S(1)} %get-tuple-element.31.refs_0_), channel_id=1, source_target_pairs={{0,4},{1,5},{2,6},{3,7},{4,8},{5,9},{6,10},{7,11},{8,12},{9,13},{1... | collective-permute-start | bytes 417800 | tf_op jit(solution)/shard_map/ppermute | solution.py:332
  15.6 11.0 %collective-permute-start.7 = (bf16[272,256]{1,0:T(8,128)(2,1)S(1)}, bf16[272,256]{1,0:T(8,128)(2,1)S(1)}, u32[]{:S(2)}, u32[]{:S(2)}) collective-permute-start(bf16[272,256]{1,0:T(8,128)(2,1)S(1)} %get-tuple-element.31.refs_0_), channel_id=1, source_target_pairs={{0,2},{1,3},{2,4},{3,5},{4,6},{5,7},{6,8},{7,9},{8,10},{9,11},{10,... | collective-permute-start | bytes 417800 | tf_op jit(solution)/shard_map/ppermute | solution.py:332
  18.4 9.9 %collective-permute-start.10 = (bf16[272,256]{1,0:T(8,128)(2,1)S(1)}, bf16[272,256]{1,0:T(8,128)(2,1)S(1)}, u32[]{:S(2)}, u32[]{:S(2)}) collective-permute-start(bf16[272,256]{1,0:T(8,128)(2,1)S(1)} %collective-permute-done.9), channel_id=1, source_target_pairs={{0,12},{1,13},{2,14},{3,15},{4,0},{5,1},{6,2},{7,3},{8,4},{9,5},{1... | collective-permute-start | bytes 417800 | tf_op jit(solution)/shard_map/ppermute | solution.py:332
  26.0 8.1 %collective-permute-start.8 = (bf16[272,256]{1,0:T(8,128)(2,1)S(1)}, bf16[272,256]{1,0:T(8,128)(2,1)S(1)}, u32[]{:S(2)}, u32[]{:S(2)}) collective-permute-start(bf16[272,256]{1,0:T(8,128)(2,1)S(1)} %collective-permute-done.2.after.refs_2_), channel_id=1, source_target_pairs={{0,2},{1,3},{2,4},{3,5},{4,6},{5,7},{6,8},{7,9},{8,10},{9,11},{10,... | collective-permute-start | bytes 417800 | tf_op jit(solution)/shard_map/ppermute | solution.py:332
  26.5 20.4 %collective-permute-start.3 = (bf16[272,256]{1,0:T(8,128)(2,1)S(1)}, bf16[272,256]{1,0:T(8,128)(2,1)S(1)}, u32[]{:S(2)}, u32[]{:S(2)}) collective-permute-start(bf16[272,256]{1,0:T(8,128)(2,1)S(1)} %tied.1.refs_0_), channel_id=1, source_target_pairs={{0,2},{1,3},{2,4},{3,5},{4,6},{5,7},{6,8},{7,9},{8,10},{9,11},{10,... | collective-permute-start | bytes 417800 | tf_op jit(solution)/shard_map/ppermute | solution.py:332
  26.6 21.0 %collective-permute-start.4 = (bf16[272,256]{1,0:T(8,128)(2,1)S(1)}, bf16[272,256]{1,0:T(8,128)(2,1)S(1)}, u32[]{:S(2)}, u32[]{:S(2)}) collective-permute-start(bf16[272,256]{1,0:T(8,128)(2,1)S(1)} %tied.1.refs_0_), channel_id=1, source_target_pairs={{0,4},{1,5},{2,6},{3,7},{4,8},{5,9},{6,10},{7,11},{8,12},{9,13},{1... | collective-permute-start | bytes 417800 | tf_op jit(solution)/shard_map/ppermute | solution.py:332
  28.4 24.5 %collective-permute-start.5 = (bf16[272,256]{1,0:T(8,128)(2,1)S(1)}, bf16[272,256]{1,0:T(8,128)(2,1)S(1)}, u32[]{:S(2)}, u32[]{:S(2)}) collective-permute-start(bf16[272,256]{1,0:T(8,128)(2,1)S(1)} %tied.1.refs_0_), channel_id=1, source_target_pairs={{0,6},{1,7},{2,8},{3,9},{4,10},{5,11},{6,12},{7,13},{8,14},{9,15},... | collective-permute-start | bytes 417800 | tf_op jit(solution)/shard_map/ppermute | solution.py:332
  34.0 18.8 %collective-permute-start.6 = (bf16[272,256]{1,0:T(8,128)(2,1)S(1)}, bf16[272,256]{1,0:T(8,128)(2,1)S(1)}, u32[]{:S(2)}, u32[]{:S(2)}) collective-permute-start(bf16[272,256]{1,0:T(8,128)(2,1)S(1)} %tied.1.refs_0_), channel_id=1, source_target_pairs={{0,8},{1,9},{2,10},{3,11},{4,12},{5,13},{6,14},{7,15},{8,0},{9,1},... | collective-permute-start | bytes 417800 | tf_op jit(solution)/shard_map/ppermute | solution.py:332
  45.2 11.0 %collective-permute-start.11 = (bf16[256,256]{1,0:T(8,128)(2,1)S(1)}, bf16[256,256]{1,0:T(8,128)(2,1)S(1)}, u32[]{:S(2)}, u32[]{:S(2)}) collective-permute-start(bf16[256,256]{1,0:T(8,128)(2,1)S(1)} %get-tuple-element.32), channel_id=1, source_target_pairs={{0,14},{1,15},{2,0},{3,1},{4,2},{5,3},{6,4},{7,5},{8,6},{9,7},{10,... | collective-permute-start | bytes 393224 | tf_op jit(solution)/shard_map/ppermute | solution.py:332
  46.9 27.4 %collective-permute-start.14 = (bf16[128,1024]{1,0:T(8,128)(2,1)S(1)}, bf16[128,1024]{1,0:T(8,128)(2,1)S(1)}, u32[]{:S(2)}, u32[]{:S(2)}) collective-permute-start(bf16[128,1024]{1,0:T(8,128)(2,1)S(1)} %get-tuple-element.36), channel_id=1, source_target_pairs={{0,192},{64,0},{128,64},{192,128},{1,193},{65,1},{129,65},{193,129... | collective-permute-start | bytes 786440 | tf_op jit(solution)/shard_map/ppermute | solution.py:341
  47.6 26.7 %collective-permute-start.15 = (bf16[128,1024]{1,0:T(8,128)(2,1)S(1)}, bf16[128,1024]{1,0:T(8,128)(2,1)S(1)}, u32[]{:S(2)}, u32[]{:S(2)}) collective-permute-start(bf16[128,1024]{1,0:T(8,128)(2,1)S(1)} %get-tuple-element.37), channel_id=1, source_target_pairs={{0,193},{1,192},{2,195},{3,194},{4,197},{5,196},{6,199},{7,198},{8... | collective-permute-start | bytes 786440 | tf_op jit(solution)/shard_map/ppermute | solution.py:349
  52.9 12.6 %collective-permute-start.16 = (bf16[256,256]{1,0:T(8,128)(2,1)S(1)}, bf16[256,256]{1,0:T(8,128)(2,1)S(1)}, u32[]{:S(2)}, u32[]{:S(2)}) collective-permute-start(bf16[256,256]{1,0:T(8,128)(2,1)S(1)} %get-tuple-element.39), channel_id=1, source_target_pairs={{0,12},{1,13},{2,14},{3,15},{4,0},{5,1},{6,2},{7,3},{8,4},{9,5},{1... | collective-permute-start | bytes 393224 | tf_op jit(solution)/shard_map/ppermute | solution.py:332
  52.9 19.4 %collective-permute-start.17 = (bf16[256,256]{1,0:T(8,128)(2,1)S(1)}, bf16[256,256]{1,0:T(8,128)(2,1)S(1)}, u32[]{:S(2)}, u32[]{:S(2)}) collective-permute-start(bf16[256,256]{1,0:T(8,128)(2,1)S(1)} %get-tuple-element.40), channel_id=1, source_target_pairs={{0,10},{1,11},{2,12},{3,13},{4,14},{5,15},{6,0},{7,1},{8,2},{9,3},... | collective-permute-start | bytes 393224 | tf_op jit(solution)/shard_map/ppermute | solution.py:332
  56.2 18.0 %collective-permute-start.18 = (bf16[256,256]{1,0:T(8,128)(2,1)S(1)}, bf16[256,256]{1,0:T(8,128)(2,1)S(1)}, u32[]{:S(2)}, u32[]{:S(2)}) collective-permute-start(bf16[256,256]{1,0:T(8,128)(2,1)S(1)} %get-tuple-element.41), channel_id=1, source_target_pairs={{0,8},{1,9},{2,10},{3,11},{4,12},{5,13},{6,14},{7,15},{8,0},{9,1},... | collective-permute-start | bytes 393224 | tf_op jit(solution)/shard_map/ppermute | solution.py:332
  65.5 16.3 %collective-permute-start.12 = (bf16[128,1024]{1,0:T(8,128)(2,1)S(1)}, bf16[128,1024]{1,0:T(8,128)(2,1)S(1)}, u32[]{:S(2)}, u32[]{:S(2)}) collective-permute-start(bf16[128,1024]{1,0:T(8,128)(2,1)S(1)} %get-tuple-element.33), channel_id=1, source_target_pairs={{0,64},{64,128},{128,192},{192,0},{1,65},{65,129},{129,193},{193,1... | collective-permute-start | bytes 786440 | tf_op jit(solution)/shard_map/ppermute | solution.py:341
  72.3 9.5 %collective-permute-start.13 = (bf16[128,1024]{1,0:T(8,128)(2,1)S(1)}, bf16[128,1024]{1,0:T(8,128)(2,1)S(1)}, u32[]{:S(2)}, u32[]{:S(2)}) collective-permute-start(bf16[128,1024]{1,0:T(8,128)(2,1)S(1)} %get-tuple-element.34), channel_id=1, source_target_pairs={{0,65},{1,64},{2,67},{3,66},{4,69},{5,68},{6,71},{7,70},{8,73},{9,... | collective-permute-start | bytes 786440 | tf_op jit(solution)/shard_map/ppermute | solution.py:349
  74.9 6.3 %collective-permute-start.19 = (bf16[256,256]{1,0:T(8,128)(2,1)S(1)}, bf16[256,256]{1,0:T(8,128)(2,1)S(1)}, u32[]{:S(2)}, u32[]{:S(2)}) collective-permute-start(bf16[256,256]{1,0:T(8,128)(2,1)S(1)} %total.1), channel_id=1, source_target_pairs={{0,192},{64,0},{128,64},{192,128},{1,193},{65,1},{129,65},{193,129... | collective-permute-start | bytes 393224 | tf_op jit(solution)/shard_map/ppermute | solution.py:341
  81.2 4.3 %collective-permute-start.20 = (bf16[128,256]{1,0:T(8,128)(2,1)S(1)}, bf16[128,256]{1,0:T(8,128)(2,1)S(1)}, u32[]{:S(2)}, u32[]{:S(2)}) collective-permute-start(bf16[128,256]{1,0:T(8,128)(2,1)S(1)} %slice.4), channel_id=1, source_target_pairs={{0,1},{1,0},{2,3},{3,2},{4,5},{5,4},{6,7},{7,6},{8,9},{9,8},{10,11... | collective-permute-start | bytes 196616 | tf_op jit(solution)/shard_map/ppermute | solution.py:336

commit v5 on v4

--- a/solution.py
+++ b/solution.py
@@ -416,7 +416,8 @@
     blocks_f = [f0] + [along_z(f0, k) for k in (1, 2, 3, 4)]
 
     dq_own, dq_cross, parts = run_bwd(where, own, crossed, (b0, b1, b2, b3, b4))
-    terms = [parts[0]] + [along_z(parts[k], -k) for k in range(1, SLOTS)]
+    four = along_z(parts[4], 2)
+    terms = [parts[0]] + [along_z(parts[k], -k) for k in (1, 2, 3)] + [along_z(four, 2)]
     dq = handed(dq_own, -1), handed_across(dq_cross, -1)
     o_own, o_cross = run_fwd(where, own, crossed, blocks_f, (terms[1],))
     dq = handed(dq_own, -1), handed_across(dq_cross, -1)

time: 87.2 us -> 86.6 us (level)
  starting transfers between devices: 34.7 us -> 31 us
  waiting for transfers between devices: 27.9 us -> 30.5 us
    ppermute x13 -> x14, starting transfers between devices: 27.3 us -> 23.5 us  [along_z(): lax.ppermute(block, 'cp', [(i, (i + 2 * distance) % n) for i in range(n)])]
    ppermute x13 -> x14, waiting for transfers between devices: 17.3 us -> 20.8 us  [along_z(): lax.ppermute(block, 'cp', [(i, (i + 2 * distance) % n) for i in range(n)])]
  transfers between devices with their start and end apart: 21 -> 22, of which waited for: 8 -> 9; matrix products, arithmetic and copies ran while one was open for 0% -> 0% of each run, Pallas kernels for 23% -> 23%
where the time goes in v5:
time: 86.6 us; the launch traced here: 86 us
  starting transfers between devices  31 us (36%)
  waiting for transfers between devices  30.5 us (35%)
  Pallas kernels  23.4 us (27%)
  between operations  0.94 us (1%)
    ppermute x14, starting transfers between devices, along_z(): lax.ppermute(block, 'cp', [(i, (i + 2 * distance) % n) for i in range(n)])  23.5 us
    ppermute x14, waiting for transfers between devices, along_z(): lax.ppermute(block, 'cp', [(i, (i + 2 * distance) % n) for i in range(n)])  20.8 us
    pallas_call x1, Pallas kernels, run_bwd(): call(bwd_kernel, outs, 2 + SLOTS, scratch, 5 * MATMUL, 2 ** 22, 'bwd', li...  10.5 us
    ppermute x3, waiting for transfers between devices, handed(): lax.ppermute(block, 'section', [(i, (i + distance) % n) for i in range(n)])  6.17 us
    pallas_call x1, Pallas kernels, run_fwd(): call(fwd_kernel, [shape(ROWS, HALF)] * 2, [VMEM] * (2 + SLOTS) + [ANY] *...  4.97 us
    ppermute x3, starting transfers between devices, swapped(): lax.ppermute(block, 'cp', [(i, i ^ 1) for i in range(lax.axis_size('cp'))])  4.65 us
    ppermute x3, waiting for transfers between devices, swapped(): lax.ppermute(block, 'cp', [(i, i ^ 1) for i in range(lax.axis_size('cp'))])  3.56 us
    pallas_call x1, Pallas kernels, per_device(): call(halves_kernel, [shape(ROWS, 3 * HALF)] * 2, [HBM] * 3 + [ANY], [pltp...  1.94 us
  transfers between devices with their start and end apart: 22, of which 9 were waited for; matrix products, arithmetic and copies ran while one was open for 0% of the time, Pallas kernels for 23%

profile of v5, /device:TPU:56, one launch (start us, length us, event | category | flops | bytes accessed | tf_op | source)
XLA Modules:
  0.0 86.0 jit_solution(8239910288390816285)
XLA Ops:
  0.6 0.1 pad_add_fusion.where_ref
  0.7 1.6 %split.1 = (bf16[144,512]{1,0:T(8,128)(2,1)S(1)}, bf16[144,512]{1,0:T(8,128)(2,1)S(1)}) custom-call(s32[2]{0:T(128)S(1)} %pad_add_fusion.where_ref, bf16[128,256]{1,0:T(8,128)(2,1)} %bitcast.16, bf16[128,256]{1,0:T(8,128)(2,1)} %bitcast.17, s32[1,128]{1,0:T(1,128)} %refs_2_.1, bf16[128,256]{1,0:T(8,128)(2,1)} %bitcast.18, bf16[128,256]{1,0:T(8,128)(2,1)} %bitcast.19, ...), custom_call_target="tpu_custom_call" | custom-call | bytes 524288 | tf_op jit(solution)/shard_map/split/pallas_call | solution.py:359
  2.3 1.6 %collective-permute-start = (bf16[144,512]{1,0:T(8,128)(2,1)S(1)}, bf16[144,512]{1,0:T(8,128)(2,1)S(1)}, u32[]{:S(2)}, u32[]{:S(2)}) collective-permute-start(bf16[144,512]{1,0:T(8,128)(2,1)S(1)} %get-tuple-element.25.refs_3_), channel_id=1, source_target_pairs={{0,1},{1,0},{2,3},{3,2},{4,5},{5,4},{6,7},{7,6},{8,9},{9,8},{10,11... | collective-permute-start | bytes 442376 | tf_op jit(solution)/shard_map/ppermute | solution.py:336
  3.9 1.9 %halves.1 = (bf16[128,3072]{1,0:T(8,128)(2,1)S(1)}, bf16[128,3072]{1,0:T(8,128)(2,1)S(1)}) custom-call(s32[2]{0:T(128)S(1)} %pad_add_fusion.where_ref, bf16[128,2048]{1,0:T(8,128)(2,1)} %bitcast.13, bf16[128,2048]{1,0:T(8,128)(2,1)} %bitcast.14, bf16[128,2048]{1,0:T(8,128)(2,1)} %bitcast.15, bf16[144,512]{1,0:T(8,128)(2,1)S(1)} %get-tuple-element.25.refs_3_), custom_call_target="tpu_custom_call" | custom-call | bytes 524288 | tf_op jit(solution)/shard_map/halves/pallas_call | solution.py:401
  5.9 2.1 %collective-permute-done.got = bf16[144,512]{1,0:T(8,128)(2,1)S(1)} collective-permute-done((bf16[144,512]{1,0:T(8,128)(2,1)S(1)}, bf16[144,512]{1,0:T(8,128)(2,1)S(1)}, u32[]{:S(2)}, u32[]{:S(2)}) %collective-permute-start) | collective-permute-done | bytes 147488 | tf_op jit(solution)/shard_map/ppermute | solution.py:336
  8.0 0.6 join.1
  8.6 1.6 %collective-permute-start.1 = (bf16[128,3072]{1,0:T(8,128)(2,1)S(1)}, bf16[128,3072]{1,0:T(8,128)(2,1)S(1)}, u32[]{:S(2)}, u32[]{:S(2)}) collective-permute-start(bf16[128,3072]{1,0:T(8,128)(2,1)S(1)} %get-tuple-element.29), channel_id=1, source_target_pairs={{0,1},{1,0},{2,3},{3,2},{4,5},{5,4},{6,7},{7,6},{8,9},{9,8},{10,11... | collective-permute-start | bytes 2359304 | tf_op jit(solution)/shard_map/ppermute | solution.py:336
  10.1 5.4 %collective-permute-start.9 = (bf16[272,256]{1,0:T(8,128)(2,1)S(1)}, bf16[272,256]{1,0:T(8,128)(2,1)S(1)}, u32[]{:S(2)}, u32[]{:S(2)}) collective-permute-start(bf16[272,256]{1,0:T(8,128)(2,1)S(1)} %get-tuple-element.31.refs_0_), channel_id=1, source_target_pairs={{0,12},{1,13},{2,14},{3,15},{4,0},{5,1},{6,2},{7,3},{8,4},{9,5},{1... | collective-permute-start | bytes 417800 | tf_op jit(solution)/shard_map/ppermute | solution.py:332
  15.5 0.0 collective-permute-start.2
  15.6 1.0 %collective-permute-start.7 = (bf16[272,256]{1,0:T(8,128)(2,1)S(1)}, bf16[272,256]{1,0:T(8,128)(2,1)S(1)}, u32[]{:S(2)}, u32[]{:S(2)}) collective-permute-start(bf16[272,256]{1,0:T(8,128)(2,1)S(1)} %get-tuple-element.31.refs_0_), channel_id=1, source_target_pairs={{0,2},{1,3},{2,4},{3,5},{4,6},{5,7},{6,8},{7,9},{8,10},{9,11},{10,... | collective-permute-start | bytes 417800 | tf_op jit(solution)/shard_map/ppermute | solution.py:332
  16.6 1.9 %collective-permute-done.9 = bf16[272,256]{1,0:T(8,128)(2,1)S(1)} collective-permute-done((bf16[272,256]{1,0:T(8,128)(2,1)S(1)}, bf16[272,256]{1,0:T(8,128)(2,1)S(1)}, u32[]{:S(2)}, u32[]{:S(2)}) %collective-permute-start.9) | collective-permute-done | bytes 139296 | tf_op jit(solution)/shard_map/ppermute | solution.py:332
  18.4 4.6 %collective-permute-start.10 = (bf16[272,256]{1,0:T(8,128)(2,1)S(1)}, bf16[272,256]{1,0:T(8,128)(2,1)S(1)}, u32[]{:S(2)}, u32[]{:S(2)}) collective-permute-start(bf16[272,256]{1,0:T(8,128)(2,1)S(1)} %collective-permute-done.9), channel_id=1, source_target_pairs={{0,12},{1,13},{2,14},{3,15},{4,0},{5,1},{6,2},{7,3},{8,4},{9,5},{1... | collective-permute-start | bytes 417800 | tf_op jit(solution)/shard_map/ppermute | solution.py:332
  23.0 2.9 %collective-permute-done.2.after.refs_2_ = bf16[272,256]{1,0:T(8,128)(2,1)S(1)} collective-permute-done((bf16[272,256]{1,0:T(8,128)(2,1)S(1)}, bf16[272,256]{1,0:T(8,128)(2,1)S(1)}, u32[]{:S(2)}, u32[]{:S(2)}) %collective-permute-start.2) | collective-permute-done | bytes 139296 | tf_op jit(solution)/shard_map/ppermute | solution.py:332
  26.0 0.0 collective-permute-start.8
  26.0 0.5 tied.1.refs_0_
  26.5 0.1 collective-permute-start.3
  26.6 0.0 collective-permute-done.7.refs_1_
  26.6 1.8 %collective-permute-start.4 = (bf16[272,256]{1,0:T(8,128)(2,1)S(1)}, bf16[272,256]{1,0:T(8,128)(2,1)S(1)}, u32[]{:S(2)}, u32[]{:S(2)}) collective-permute-start(bf16[272,256]{1,0:T(8,128)(2,1)S(1)} %tied.1.refs_0_), channel_id=1, source_target_pairs={{0,4},{1,5},{2,6},{3,7},{4,8},{5,9},{6,10},{7,11},{8,12},{9,13},{1... | collective-permute-start | bytes 417800 | tf_op jit(solution)/shard_map/ppermute | solution.py:332
  28.4 0.0 collective-permute-done.10.refs_4_
  28.4 4.4 %collective-permute-start.5 = (bf16[272,256]{1,0:T(8,128)(2,1)S(1)}, bf16[272,256]{1,0:T(8,128)(2,1)S(1)}, u32[]{:S(2)}, u32[]{:S(2)}) collective-permute-start(bf16[272,256]{1,0:T(8,128)(2,1)S(1)} %tied.1.refs_0_), channel_id=1, source_target_pairs={{0,6},{1,7},{2,8},{3,9},{4,10},{5,11},{6,12},{7,13},{8,14},{9,15},... | collective-permute-start | bytes 417800 | tf_op jit(solution)/shard_map/ppermute | solution.py:332
  32.8 1.2 %collective-permute-done.8.refs_3_ = bf16[272,256]{1,0:T(8,128)(2,1)S(1)} collective-permute-done((bf16[272,256]{1,0:T(8,128)(2,1)S(1)}, bf16[272,256]{1,0:T(8,128)(2,1)S(1)}, u32[]{:S(2)}, u32[]{:S(2)}) %collective-permute-start.8) | collective-permute-done | bytes 139296 | tf_op jit(solution)/shard_map/ppermute | solution.py:332
  34.0 0.7 collective-permute-start.6
  34.8 0.0 collective-permute-done.1.qdx_ref.qx_ref
  34.8 10.5 %bwd.1 = (bf16[128,1024]{1,0:T(8,128)(2,1)S(1)}, bf16[128,1024]{1,0:T(8,128)(2,1)S(1)}, bf16[256,256]{1,0:T(8,128)(2,1)S(1)}, bf16[256,256]{1,0:T(8,128)(2,1)S(1...) custom-call(s32[2]{0:T(128)S(1)} %pad_add_fusion.where_ref, ...), custom_call_target="tpu_custom_call" | custom-call | flops 3355443200 | bytes 4194304 | tf_op jit(solution)/shard_map/bwd/pallas_call | solution.py:317
  45.2 1.5 %collective-permute-start.18 = (bf16[256,256]{1,0:T(8,128)(2,1)S(1)}, bf16[256,256]{1,0:T(8,128)(2,1)S(1)}, u32[]{:S(2)}, u32[]{:S(2)}) collective-permute-start(bf16[256,256]{1,0:T(8,128)(2,1)S(1)} %get-tuple-element.41), channel_id=1, source_target_pairs={{0,4},{1,5},{2,6},{3,7},{4,8},{5,9},{6,10},{7,11},{8,12},{9,13},{1... | collective-permute-start | bytes 393224 | tf_op jit(solution)/shard_map/ppermute | solution.py:332
  46.7 0.0 collective-permute-done.3.refs_1_
  46.7 0.9 %collective-permute-start.11 = (bf16[256,256]{1,0:T(8,128)(2,1)S(1)}, bf16[256,256]{1,0:T(8,128)(2,1)S(1)}, u32[]{:S(2)}, u32[]{:S(2)}) collective-permute-start(bf16[256,256]{1,0:T(8,128)(2,1)S(1)} %get-tuple-element.32), channel_id=1, source_target_pairs={{0,14},{1,15},{2,0},{3,1},{4,2},{5,3},{6,4},{7,5},{8,6},{9,7},{10,... | collective-permute-start | bytes 393224 | tf_op jit(solution)/shard_map/ppermute | solution.py:332
  47.6 0.0 collective-permute-done.4.refs_2_
  47.6 0.7 collective-permute-start.14
  48.4 3.1 %collective-permute-done.5.refs_3_ = bf16[272,256]{1,0:T(8,128)(2,1)S(1)} collective-permute-done((bf16[272,256]{1,0:T(8,128)(2,1)S(1)}, bf16[272,256]{1,0:T(8,128)(2,1)S(1)}, u32[]{:S(2)}, u32[]{:S(2)}) %collective-permute-start.5) | collective-permute-done | bytes 139296 | tf_op jit(solution)/shard_map/ppermute | solution.py:332
  51.5 0.7 collective-permute-start.15
  52.2 0.0 collective-permute-done.6.refs_4_
  52.2 0.3 collective-permute-start.16
  52.5 7.6 %collective-permute-done.18 = bf16[256,256]{1,0:T(8,128)(2,1)S(1)} collective-permute-done((bf16[256,256]{1,0:T(8,128)(2,1)S(1)}, bf16[256,256]{1,0:T(8,128)(2,1)S(1)}, u32[]{:S(2)}, u32[]{:S(2)}) %collective-permute-start.18) | collective-permute-done | bytes 131104 | tf_op jit(solution)/shard_map/ppermute | solution.py:332
  60.1 0.0 collective-permute-start.17
  60.1 0.0 collective-permute-done.11.refs_5_.refs_1_
  60.1 2.8 %collective-permute-start.19 = (bf16[256,256]{1,0:T(8,128)(2,1)S(1)}, bf16[256,256]{1,0:T(8,128)(2,1)S(1)}, u32[]{:S(2)}, u32[]{:S(2)}) collective-permute-start(bf16[256,256]{1,0:T(8,128)(2,1)S(1)} %collective-permute-done.18), channel_id=1, source_target_pairs={{0,4},{1,5},{2,6},{3,7},{4,8},{5,9},{6,10},{7,11},{8,12},{9,13},{1... | collective-permute-start | bytes 393224 | tf_op jit(solution)/shard_map/ppermute | solution.py:332
  62.9 5.0 %fwd.1 = (bf16[128,1024]{1,0:T(8,128)(2,1)S(1)}, bf16[128,1024]{1,0:T(8,128)(2,1)S(1)}) custom-call(s32[2]{0:T(128)S(1)} %pad_add_fusion.where_ref, bf16[128,3072]{1,0:T(8,128)(2,1)S(1)} %get-tuple-element.26.qd_ref.q_ref, bf16[128,3072]{1,0:T(8,128)(2,1)S(1)} %collective-permute-done.1.qdx_ref.qx_ref, bf16[272,256]{1,0:T(8,128)(2,1)S(1)} %tied.1.refs_0_, ...), custom_call_target="tpu_custom_call" | custom-call | flops 1342177280 | bytes 2097152 | tf_op jit(solution)/shard_map/fwd/pallas_call | solution.py:289
  67.9 0.0 collective-permute-done.16.refs_2_
  67.9 0.3 collective-permute-start.12
  68.2 4.0 %collective-permute-done.17.refs_3_ = bf16[256,256]{1,0:T(8,128)(2,1)S(1)} collective-permute-done((bf16[256,256]{1,0:T(8,128)(2,1)S(1)}, bf16[256,256]{1,0:T(8,128)(2,1)S(1)}, u32[]{:S(2)}, u32[]{:S(2)}) %collective-permute-start.17) | collective-permute-done | bytes 131104 | tf_op jit(solution)/shard_map/ppermute | solution.py:332
  72.2 1.0 %collective-permute-start.13 = (bf16[128,1024]{1,0:T(8,128)(2,1)S(1)}, bf16[128,1024]{1,0:T(8,128)(2,1)S(1)}, u32[]{:S(2)}, u32[]{:S(2)}) collective-permute-start(bf16[128,1024]{1,0:T(8,128)(2,1)S(1)} %get-tuple-element.34), channel_id=1, source_target_pairs={{0,65},{1,64},{2,67},{3,66},{4,69},{5,68},{6,71},{7,70},{8,73},{9,... | collective-permute-start | bytes 786440 | tf_op jit(solution)/shard_map/ppermute | solution.py:349
  73.3 0.0 collective-permute-done.19.refs_4_
  73.3 0.0 collective-permute-done.14.refs_5_.refs_0_
  73.3 0.0 collective-permute-done.15.refs_6_.refs_1_
  73.3 0.6 total.1
  73.9 0.1 collective-permute-start.20
  74.0 6.2 %collective-permute-done.20.refs_2_ = bf16[256,256]{1,0:T(8,128)(2,1)S(1)} collective-permute-done((bf16[256,256]{1,0:T(8,128)(2,1)S(1)}, bf16[256,256]{1,0:T(8,128)(2,1)S(1)}, u32[]{:S(2)}, u32[]{:S(2)}) %collective-permute-start.20) | collective-permute-done | bytes 131104 | tf_op jit(solution)/shard_map/ppermute | solution.py:341
  80.2 1.5 %collective-permute-start.21 = (bf16[128,256]{1,0:T(8,128)(2,1)S(1)}, bf16[128,256]{1,0:T(8,128)(2,1)S(1)}, u32[]{:S(2)}, u32[]{:S(2)}) collective-permute-start(bf16[128,256]{1,0:T(8,128)(2,1)S(1)} %slice.4), channel_id=1, source_target_pairs={{0,1},{1,0},{2,3},{3,2},{4,5},{5,4},{6,7},{7,6},{8,9},{9,8},{10,11... | collective-permute-start | bytes 196616 | tf_op jit(solution)/shard_map/ppermute | solution.py:336
  81.7 0.0 collective-permute-done.12.own
  81.7 0.0 collective-permute-done.13.cross
  81.7 1.4 %output.1 = (bf16[128,2048]{1,0:T(8,128)(2,1)}, bf16[16,128]{1,0:T(8,128)(2,1)S(1)}) custom-call(s32[2]{0:T(128)S(1)} %pad_add_fusion.where_ref, bf16[128,1024]{1,0:T(8,128)(2,1)S(1)} %collective-permute-done.12.own, bf16[128,1024]{1,0:T(8,128)(2,1)S(1)} %collective-permute-done.13.cross), custom_call_target="tpu_custom_call" | custom-call | flops 1342177280 | bytes 524288 | tf_op jit(solution)/shard_map/output/pallas_call | solution.py:428
  83.0 1.4 %collective-permute-done.21.refs_3_ = bf16[128,256]{1,0:T(8,128)(2,1)S(1)} collective-permute-done((bf16[128,256]{1,0:T(8,128)(2,1)S(1)}, bf16[128,256]{1,0:T(8,128)(2,1)S(1)}, u32[]{:S(2)}, u32[]{:S(2)}) %collective-permute-start.21) | collective-permute-done | bytes 65568 | tf_op jit(solution)/shard_map/ppermute | solution.py:336
  84.4 1.4 %final.1 = (bf16[128,2048]{1,0:T(8,128)(2,1)}, bf16[128,256]{1,0:T(8,128)(2,1)}, bf16[128,256]{1,0:T(8,128)(2,1)}) custom-call(s32[2]{0:T(128)S(1)} %pad_add_fusion.where_ref, bf16[128,1024]{1,0:T(8,128)(2,1)S(1)} %collective-permute-done.14.refs_5_.refs_0_, bf16[128,1024]{1,0:T(8,128)(2,1)S(1)} %collective-permute-done.15.refs_6_.refs_1_, ...), custom_call_target="tpu_custom_call" | custom-call | bytes 524288 | tf_op jit(solution)/shard_map/final/pallas_call | solution.py:437
  (1 shorter events, 0.0 us)
Async XLA Ops:
  2.3 5.7 %collective-permute-start = (bf16[144,512]{1,0:T(8,128)(2,1)S(1)}, bf16[144,512]{1,0:T(8,128)(2,1)S(1)}, u32[]{:S(2)}, u32[]{:S(2)}) collective-permute-start(bf16[144,512]{1,0:T(8,128)(2,1)S(1)} %get-tuple-element.25.refs_3_), channel_id=1, source_target_pairs={{0,1},{1,0},{2,3},{3,2},{4,5},{5,4},{6,7},{7,6},{8,9},{9,8},{10,11... | collective-permute-start | bytes 442376 | tf_op jit(solution)/shard_map/ppermute | solution.py:336
  8.6 26.2 %collective-permute-start.1 = (bf16[128,3072]{1,0:T(8,128)(2,1)S(1)}, bf16[128,3072]{1,0:T(8,128)(2,1)S(1)}, u32[]{:S(2)}, u32[]{:S(2)}) collective-permute-start(bf16[128,3072]{1,0:T(8,128)(2,1)S(1)} %get-tuple-element.29), channel_id=1, source_target_pairs={{0,1},{1,0},{2,3},{3,2},{4,5},{5,4},{6,7},{7,6},{8,9},{9,8},{10,11... | collective-permute-start | bytes 2359304 | tf_op jit(solution)/shard_map/ppermute | solution.py:336
  10.1 8.3 %collective-permute-start.9 = (bf16[272,256]{1,0:T(8,128)(2,1)S(1)}, bf16[272,256]{1,0:T(8,128)(2,1)S(1)}, u32[]{:S(2)}, u32[]{:S(2)}) collective-permute-start(bf16[272,256]{1,0:T(8,128)(2,1)S(1)} %get-tuple-element.31.refs_0_), channel_id=1, source_target_pairs={{0,12},{1,13},{2,14},{3,15},{4,0},{5,1},{6,2},{7,3},{8,4},{9,5},{1... | collective-permute-start | bytes 417800 | tf_op jit(solution)/shard_map/ppermute | solution.py:332
  15.5 10.4 %collective-permute-start.2 = (bf16[272,256]{1,0:T(8,128)(2,1)S(1)}, bf16[272,256]{1,0:T(8,128)(2,1)S(1)}, u32[]{:S(2)}, u32[]{:S(2)}) collective-permute-start(bf16[272,256]{1,0:T(8,128)(2,1)S(1)} %get-tuple-element.31.refs_0_), channel_id=1, source_target_pairs={{0,4},{1,5},{2,6},{3,7},{4,8},{5,9},{6,10},{7,11},{8,12},{9,13},{1... | collective-permute-start | bytes 417800 | tf_op jit(solution)/shard_map/ppermute | solution.py:332
  15.6 11.0 %collective-permute-start.7 = (bf16[272,256]{1,0:T(8,128)(2,1)S(1)}, bf16[272,256]{1,0:T(8,128)(2,1)S(1)}, u32[]{:S(2)}, u32[]{:S(2)}) collective-permute-start(bf16[272,256]{1,0:T(8,128)(2,1)S(1)} %get-tuple-element.31.refs_0_), channel_id=1, source_target_pairs={{0,2},{1,3},{2,4},{3,5},{4,6},{5,7},{6,8},{7,9},{8,10},{9,11},{10,... | collective-permute-start | bytes 417800 | tf_op jit(solution)/shard_map/ppermute | solution.py:332
  18.4 9.9 %collective-permute-start.10 = (bf16[272,256]{1,0:T(8,128)(2,1)S(1)}, bf16[272,256]{1,0:T(8,128)(2,1)S(1)}, u32[]{:S(2)}, u32[]{:S(2)}) collective-permute-start(bf16[272,256]{1,0:T(8,128)(2,1)S(1)} %collective-permute-done.9), channel_id=1, source_target_pairs={{0,12},{1,13},{2,14},{3,15},{4,0},{5,1},{6,2},{7,3},{8,4},{9,5},{1... | collective-permute-start | bytes 417800 | tf_op jit(solution)/shard_map/ppermute | solution.py:332
  26.0 8.1 %collective-permute-start.8 = (bf16[272,256]{1,0:T(8,128)(2,1)S(1)}, bf16[272,256]{1,0:T(8,128)(2,1)S(1)}, u32[]{:S(2)}, u32[]{:S(2)}) collective-permute-start(bf16[272,256]{1,0:T(8,128)(2,1)S(1)} %collective-permute-done.2.after.refs_2_), channel_id=1, source_target_pairs={{0,2},{1,3},{2,4},{3,5},{4,6},{5,7},{6,8},{7,9},{8,10},{9,11},{10,... | collective-permute-start | bytes 417800 | tf_op jit(solution)/shard_map/ppermute | solution.py:332
  26.5 20.2 %collective-permute-start.3 = (bf16[272,256]{1,0:T(8,128)(2,1)S(1)}, bf16[272,256]{1,0:T(8,128)(2,1)S(1)}, u32[]{:S(2)}, u32[]{:S(2)}) collective-permute-start(bf16[272,256]{1,0:T(8,128)(2,1)S(1)} %tied.1.refs_0_), channel_id=1, source_target_pairs={{0,2},{1,3},{2,4},{3,5},{4,6},{5,7},{6,8},{7,9},{8,10},{9,11},{10,... | collective-permute-start | bytes 417800 | tf_op jit(solution)/shard_map/ppermute | solution.py:332
  26.6 21.0 %collective-permute-start.4 = (bf16[272,256]{1,0:T(8,128)(2,1)S(1)}, bf16[272,256]{1,0:T(8,128)(2,1)S(1)}, u32[]{:S(2)}, u32[]{:S(2)}) collective-permute-start(bf16[272,256]{1,0:T(8,128)(2,1)S(1)} %tied.1.refs_0_), channel_id=1, source_target_pairs={{0,4},{1,5},{2,6},{3,7},{4,8},{5,9},{6,10},{7,11},{8,12},{9,13},{1... | collective-permute-start | bytes 417800 | tf_op jit(solution)/shard_map/ppermute | solution.py:332
  28.4 23.1 %collective-permute-start.5 = (bf16[272,256]{1,0:T(8,128)(2,1)S(1)}, bf16[272,256]{1,0:T(8,128)(2,1)S(1)}, u32[]{:S(2)}, u32[]{:S(2)}) collective-permute-start(bf16[272,256]{1,0:T(8,128)(2,1)S(1)} %tied.1.refs_0_), channel_id=1, source_target_pairs={{0,6},{1,7},{2,8},{3,9},{4,10},{5,11},{6,12},{7,13},{8,14},{9,15},... | collective-permute-start | bytes 417800 | tf_op jit(solution)/shard_map/ppermute | solution.py:332
  34.0 18.1 %collective-permute-start.6 = (bf16[272,256]{1,0:T(8,128)(2,1)S(1)}, bf16[272,256]{1,0:T(8,128)(2,1)S(1)}, u32[]{:S(2)}, u32[]{:S(2)}) collective-permute-start(bf16[272,256]{1,0:T(8,128)(2,1)S(1)} %tied.1.refs_0_), channel_id=1, source_target_pairs={{0,8},{1,9},{2,10},{3,11},{4,12},{5,13},{6,14},{7,15},{8,0},{9,1},... | collective-permute-start | bytes 417800 | tf_op jit(solution)/shard_map/ppermute | solution.py:332
  45.2 14.9 %collective-permute-start.18 = (bf16[256,256]{1,0:T(8,128)(2,1)S(1)}, bf16[256,256]{1,0:T(8,128)(2,1)S(1)}, u32[]{:S(2)}, u32[]{:S(2)}) collective-permute-start(bf16[256,256]{1,0:T(8,128)(2,1)S(1)} %get-tuple-element.41), channel_id=1, source_target_pairs={{0,4},{1,5},{2,6},{3,7},{4,8},{5,9},{6,10},{7,11},{8,12},{9,13},{1... | collective-permute-start | bytes 393224 | tf_op jit(solution)/shard_map/ppermute | solution.py:332
  46.7 13.4 %collective-permute-start.11 = (bf16[256,256]{1,0:T(8,128)(2,1)S(1)}, bf16[256,256]{1,0:T(8,128)(2,1)S(1)}, u32[]{:S(2)}, u32[]{:S(2)}) collective-permute-start(bf16[256,256]{1,0:T(8,128)(2,1)S(1)} %get-tuple-element.32), channel_id=1, source_target_pairs={{0,14},{1,15},{2,0},{3,1},{4,2},{5,3},{6,4},{7,5},{8,6},{9,7},{10,... | collective-permute-start | bytes 393224 | tf_op jit(solution)/shard_map/ppermute | solution.py:332
  47.6 25.6 %collective-permute-start.14 = (bf16[128,1024]{1,0:T(8,128)(2,1)S(1)}, bf16[128,1024]{1,0:T(8,128)(2,1)S(1)}, u32[]{:S(2)}, u32[]{:S(2)}) collective-permute-start(bf16[128,1024]{1,0:T(8,128)(2,1)S(1)} %get-tuple-element.36), channel_id=1, source_target_pairs={{0,192},{64,0},{128,64},{192,128},{1,193},{65,1},{129,65},{193,129... | collective-permute-start | bytes 786440 | tf_op jit(solution)/shard_map/ppermute | solution.py:341
  51.5 21.8 %collective-permute-start.15 = (bf16[128,1024]{1,0:T(8,128)(2,1)S(1)}, bf16[128,1024]{1,0:T(8,128)(2,1)S(1)}, u32[]{:S(2)}, u32[]{:S(2)}) collective-permute-start(bf16[128,1024]{1,0:T(8,128)(2,1)S(1)} %get-tuple-element.37), channel_id=1, source_target_pairs={{0,193},{1,192},{2,195},{3,194},{4,197},{5,196},{6,199},{7,198},{8... | collective-permute-start | bytes 786440 | tf_op jit(solution)/shard_map/ppermute | solution.py:349
  52.2 15.7 %collective-permute-start.16 = (bf16[256,256]{1,0:T(8,128)(2,1)S(1)}, bf16[256,256]{1,0:T(8,128)(2,1)S(1)}, u32[]{:S(2)}, u32[]{:S(2)}) collective-permute-start(bf16[256,256]{1,0:T(8,128)(2,1)S(1)} %get-tuple-element.39), channel_id=1, source_target_pairs={{0,12},{1,13},{2,14},{3,15},{4,0},{5,1},{6,2},{7,3},{8,4},{9,5},{1... | collective-permute-start | bytes 393224 | tf_op jit(solution)/shard_map/ppermute | solution.py:332
  60.1 12.1 %collective-permute-start.17 = (bf16[256,256]{1,0:T(8,128)(2,1)S(1)}, bf16[256,256]{1,0:T(8,128)(2,1)S(1)}, u32[]{:S(2)}, u32[]{:S(2)}) collective-permute-start(bf16[256,256]{1,0:T(8,128)(2,1)S(1)} %get-tuple-element.40), channel_id=1, source_target_pairs={{0,10},{1,11},{2,12},{3,13},{4,14},{5,15},{6,0},{7,1},{8,2},{9,3},... | collective-permute-start | bytes 393224 | tf_op jit(solution)/shard_map/ppermute | solution.py:332
  60.1 13.2 %collective-permute-start.19 = (bf16[256,256]{1,0:T(8,128)(2,1)S(1)}, bf16[256,256]{1,0:T(8,128)(2,1)S(1)}, u32[]{:S(2)}, u32[]{:S(2)}) collective-permute-start(bf16[256,256]{1,0:T(8,128)(2,1)S(1)} %collective-permute-done.18), channel_id=1, source_target_pairs={{0,4},{1,5},{2,6},{3,7},{4,8},{5,9},{6,10},{7,11},{8,12},{9,13},{1... | collective-permute-start | bytes 393224 | tf_op jit(solution)/shard_map/ppermute | solution.py:332
  67.9 13.8 %collective-permute-start.12 = (bf16[128,1024]{1,0:T(8,128)(2,1)S(1)}, bf16[128,1024]{1,0:T(8,128)(2,1)S(1)}, u32[]{:S(2)}, u32[]{:S(2)}) collective-permute-start(bf16[128,1024]{1,0:T(8,128)(2,1)S(1)} %get-tuple-element.33), channel_id=1, source_target_pairs={{0,64},{64,128},{128,192},{192,0},{1,65},{65,129},{129,193},{193,1... | collective-permute-start | bytes 786440 | tf_op jit(solution)/shard_map/ppermute | solution.py:341
  72.2 9.4 %collective-permute-start.13 = (bf16[128,1024]{1,0:T(8,128)(2,1)S(1)}, bf16[128,1024]{1,0:T(8,128)(2,1)S(1)}, u32[]{:S(2)}, u32[]{:S(2)}) collective-permute-start(bf16[128,1024]{1,0:T(8,128)(2,1)S(1)} %get-tuple-element.34), channel_id=1, source_target_pairs={{0,65},{1,64},{2,67},{3,66},{4,69},{5,68},{6,71},{7,70},{8,73},{9,... | collective-permute-start | bytes 786440 | tf_op jit(solution)/shard_map/ppermute | solution.py:349
  73.9 6.3 %collective-permute-start.20 = (bf16[256,256]{1,0:T(8,128)(2,1)S(1)}, bf16[256,256]{1,0:T(8,128)(2,1)S(1)}, u32[]{:S(2)}, u32[]{:S(2)}) collective-permute-start(bf16[256,256]{1,0:T(8,128)(2,1)S(1)} %total.1), channel_id=1, source_target_pairs={{0,192},{64,0},{128,64},{192,128},{1,193},{65,1},{129,65},{193,129... | collective-permute-start | bytes 393224 | tf_op jit(solution)/shard_map/ppermute | solution.py:341
  80.2 4.3 %collective-permute-start.21 = (bf16[128,256]{1,0:T(8,128)(2,1)S(1)}, bf16[128,256]{1,0:T(8,128)(2,1)S(1)}, u32[]{:S(2)}, u32[]{:S(2)}) collective-permute-start(bf16[128,256]{1,0:T(8,128)(2,1)S(1)} %slice.4), channel_id=1, source_target_pairs={{0,1},{1,0},{2,3},{3,2},{4,5},{5,4},{6,7},{7,6},{8,9},{9,8},{10,11... | collective-permute-start | bytes 196616 | tf_op jit(solution)/shard_map/ppermute | solution.py:336

commit v6 on v4

--- a/solution.py
+++ b/solution.py
@@ -103,7 +103,7 @@
 
 def total_kernel(where_ref, *refs):
     del where_ref
-    refs[-1][...] = sum(r[...].astype(F32) for r in refs[:SLOTS]).astype(BF16)
+    refs[-1][...] = sum(r[...].astype(F32) for r in refs[:4]).astype(BF16)
 
 
 def output_kernel(where_ref, own, cross, o, token, sems):
@@ -193,6 +193,7 @@
 
 def fwd_kernel(where_ref, q_ref, qx_ref, *refs):
     blocks, refs = refs[:SLOTS], refs[SLOTS + 1 :]
+    blocks = blocks[:1] + blocks[4:] + blocks[1:4]
     o_own, o_cross, cap, s_ref, e_ref, keys, vt_ref = refs
     fill_cap(where_ref, blocks, cap)
     for k, b in enumerate(blocks):
@@ -413,15 +414,18 @@
     b4 = along_z(b4, -2)
     b3 = along_z(b2, 1)
     f0 = tied(where, f0, b2)
-    blocks_f = [f0] + [along_z(f0, k) for k in (1, 2, 3, 4)]
+    f4, f3, f2, f1 = (along_z(f0, k) for k in (4, 3, 2, 1))
+    blocks_f = (f0, f2, f3, f4, f1)
 
     dq_own, dq_cross, parts = run_bwd(where, own, crossed, (b0, b1, b2, b3, b4))
-    terms = [parts[0]] + [along_z(parts[k], -k) for k in range(1, SLOTS)]
+    far = along_z(parts[4], -1)
+    three = (parts[3].astype(F32) + far.astype(F32)).astype(BF16)
+    terms = [parts[0]] + [along_z(parts[k], -k) for k in (1, 2)] + [along_z(three, -3)]
     dq = handed(dq_own, -1), handed_across(dq_cross, -1)
     o_own, o_cross = run_fwd(where, own, crossed, blocks_f, (terms[1],))
     dq = handed(dq_own, -1), handed_across(dq_cross, -1)
     (summed,) = call(
-        total_kernel, [shape(PAIR, 2 * HEAD)], [VMEM] * SLOTS + [ANY] * 2, name="total"
+        total_kernel, [shape(PAIR, 2 * HEAD)], [VMEM] * 4 + [ANY] * 2, name="total"
     )(where, *terms, *dq)
     received = handed(summed, -1)
     attn_out, token = call(

time: 87.2 us -> 84.2 us (0.966)
  the two profiles are of different devices: /device:TPU:56 before, /device:TPU:24 now
where the time goes in v6:
time: 84.2 us; the launch traced here: 84 us
  starting transfers between devices  36.3 us (43%)
  Pallas kernels  23.4 us (28%)
  waiting for transfers between devices  23.2 us (28%)
  between operations  0.95 us (1%)
    ppermute x13, starting transfers between devices, along_z(): lax.ppermute(block, 'cp', [(i, (i + 2 * distance) % n) for i in range(n)])  28 us
    ppermute x13, waiting for transfers between devices, along_z(): lax.ppermute(block, 'cp', [(i, (i + 2 * distance) % n) for i in range(n)])  12.7 us
    pallas_call x1, Pallas kernels, run_bwd(): call(bwd_kernel, outs, 2 + SLOTS, scratch, 5 * MATMUL, 2 ** 22, 'bwd', li...  10.5 us
    ppermute x3, waiting for transfers between devices, handed(): lax.ppermute(block, 'section', [(i, (i + distance) % n) for i in range(n)])  5.44 us
    ppermute x3, waiting for transfers between devices, swapped(): lax.ppermute(block, 'cp', [(i, i ^ 1) for i in range(lax.axis_size('cp'))])  5.03 us
    pallas_call x1, Pallas kernels, run_fwd(): call(fwd_kernel, [shape(ROWS, HALF)] * 2, [VMEM] * (2 + SLOTS) + [ANY] *...  4.96 us
    ppermute x3, starting transfers between devices, handed(): lax.ppermute(block, 'section', [(i, (i + distance) % n) for i in range(n)])  3.18 us
    ppermute x3, starting transfers between devices, swapped(): lax.ppermute(block, 'cp', [(i, i ^ 1) for i in range(lax.axis_size('cp'))])  3.16 us
  transfers between devices with their start and end apart: 21, of which 10 were waited for; matrix products, arithmetic and copies ran while one was open for 0% of the time, Pallas kernels for 24%

profile of v6, /device:TPU:24, one launch (start us, length us, event | category | flops | bytes accessed | tf_op | source)
XLA Modules:
  0.0 84.0 jit_solution(3821786446135164137)
XLA Ops:
  0.6 0.1 pad_add_fusion.where_ref
  0.7 1.6 %split.1 = (bf16[144,512]{1,0:T(8,128)(2,1)S(1)}, bf16[144,512]{1,0:T(8,128)(2,1)S(1)}) custom-call(s32[2]{0:T(128)S(1)} %pad_add_fusion.where_ref, bf16[128,256]{1,0:T(8,128)(2,1)} %bitcast.16, bf16[128,256]{1,0:T(8,128)(2,1)} %bitcast.17, s32[1,128]{1,0:T(1,128)} %refs_2_.1, bf16[128,256]{1,0:T(8,128)(2,1)} %bitcast.18, bf16[128,256]{1,0:T(8,128)(2,1)} %bitcast.19, ...), custom_call_target="tpu_custom_call" | custom-call | bytes 524288 | tf_op jit(solution)/shard_map/split/pallas_call | solution.py:360
  2.3 1.6 %collective-permute-start = (bf16[144,512]{1,0:T(8,128)(2,1)S(1)}, bf16[144,512]{1,0:T(8,128)(2,1)S(1)}, u32[]{:S(2)}, u32[]{:S(2)}) collective-permute-start(bf16[144,512]{1,0:T(8,128)(2,1)S(1)} %get-tuple-element.25.refs_3_), channel_id=1, source_target_pairs={{0,1},{1,0},{2,3},{3,2},{4,5},{5,4},{6,7},{7,6},{8,9},{9,8},{10,11... | collective-permute-start | bytes 442376 | tf_op jit(solution)/shard_map/ppermute | solution.py:337
  3.9 1.9 %halves.1 = (bf16[128,3072]{1,0:T(8,128)(2,1)S(1)}, bf16[128,3072]{1,0:T(8,128)(2,1)S(1)}) custom-call(s32[2]{0:T(128)S(1)} %pad_add_fusion.where_ref, bf16[128,2048]{1,0:T(8,128)(2,1)} %bitcast.13, bf16[128,2048]{1,0:T(8,128)(2,1)} %bitcast.14, bf16[128,2048]{1,0:T(8,128)(2,1)} %bitcast.15, bf16[144,512]{1,0:T(8,128)(2,1)S(1)} %get-tuple-element.25.refs_3_), custom_call_target="tpu_custom_call" | custom-call | bytes 524288 | tf_op jit(solution)/shard_map/halves/pallas_call | solution.py:402
  5.9 2.1 %collective-permute-done.got = bf16[144,512]{1,0:T(8,128)(2,1)S(1)} collective-permute-done((bf16[144,512]{1,0:T(8,128)(2,1)S(1)}, bf16[144,512]{1,0:T(8,128)(2,1)S(1)}, u32[]{:S(2)}, u32[]{:S(2)}) %collective-permute-start) | collective-permute-done | bytes 147488 | tf_op jit(solution)/shard_map/ppermute | solution.py:337
  8.0 0.6 join.1
  8.6 1.6 %collective-permute-start.1 = (bf16[128,3072]{1,0:T(8,128)(2,1)S(1)}, bf16[128,3072]{1,0:T(8,128)(2,1)S(1)}, u32[]{:S(2)}, u32[]{:S(2)}) collective-permute-start(bf16[128,3072]{1,0:T(8,128)(2,1)S(1)} %get-tuple-element.29), channel_id=1, source_target_pairs={{0,1},{1,0},{2,3},{3,2},{4,5},{5,4},{6,7},{7,6},{8,9},{9,8},{10,11... | collective-permute-start | bytes 2359304 | tf_op jit(solution)/shard_map/ppermute | solution.py:337
  10.1 6.3 %collective-permute-start.9 = (bf16[272,256]{1,0:T(8,128)(2,1)S(1)}, bf16[272,256]{1,0:T(8,128)(2,1)S(1)}, u32[]{:S(2)}, u32[]{:S(2)}) collective-permute-start(bf16[272,256]{1,0:T(8,128)(2,1)S(1)} %get-tuple-element.31.refs_0_), channel_id=1, source_target_pairs={{0,12},{1,13},{2,14},{3,15},{4,0},{5,1},{6,2},{7,3},{8,4},{9,5},{1... | collective-permute-start | bytes 417800 | tf_op jit(solution)/shard_map/ppermute | solution.py:333
  16.4 0.0 collective-permute-start.2
  16.5 1.0 %collective-permute-start.7 = (bf16[272,256]{1,0:T(8,128)(2,1)S(1)}, bf16[272,256]{1,0:T(8,128)(2,1)S(1)}, u32[]{:S(2)}, u32[]{:S(2)}) collective-permute-start(bf16[272,256]{1,0:T(8,128)(2,1)S(1)} %get-tuple-element.31.refs_0_), channel_id=1, source_target_pairs={{0,2},{1,3},{2,4},{3,5},{4,6},{5,7},{6,8},{7,9},{8,10},{9,11},{10,... | collective-permute-start | bytes 417800 | tf_op jit(solution)/shard_map/ppermute | solution.py:333
  17.5 3.7 %collective-permute-done.9 = bf16[272,256]{1,0:T(8,128)(2,1)S(1)} collective-permute-done((bf16[272,256]{1,0:T(8,128)(2,1)S(1)}, bf16[272,256]{1,0:T(8,128)(2,1)S(1)}, u32[]{:S(2)}, u32[]{:S(2)}) %collective-permute-start.9) | collective-permute-done | bytes 139296 | tf_op jit(solution)/shard_map/ppermute | solution.py:333
  21.2 4.7 %collective-permute-start.10 = (bf16[272,256]{1,0:T(8,128)(2,1)S(1)}, bf16[272,256]{1,0:T(8,128)(2,1)S(1)}, u32[]{:S(2)}, u32[]{:S(2)}) collective-permute-start(bf16[272,256]{1,0:T(8,128)(2,1)S(1)} %collective-permute-done.9), channel_id=1, source_target_pairs={{0,12},{1,13},{2,14},{3,15},{4,0},{5,1},{6,2},{7,3},{8,4},{9,5},{1... | collective-permute-start | bytes 417800 | tf_op jit(solution)/shard_map/ppermute | solution.py:333
  25.9 0.5 collective-permute-done.2.after.refs_2_
  26.4 1.4 %collective-permute-start.8 = (bf16[272,256]{1,0:T(8,128)(2,1)S(1)}, bf16[272,256]{1,0:T(8,128)(2,1)S(1)}, u32[]{:S(2)}, u32[]{:S(2)}) collective-permute-start(bf16[272,256]{1,0:T(8,128)(2,1)S(1)} %collective-permute-done.2.after.refs_2_), channel_id=1, source_target_pairs={{0,2},{1,3},{2,4},{3,5},{4,6},{5,7},{6,8},{7,9},{8,10},{9,11},{10,... | collective-permute-start | bytes 417800 | tf_op jit(solution)/shard_map/ppermute | solution.py:333
  27.9 0.5 tied.1.refs_0_
  28.4 0.1 collective-permute-start.3
  28.5 0.9 %collective-permute-done.7.refs_1_ = bf16[272,256]{1,0:T(8,128)(2,1)S(1)} collective-permute-done((bf16[272,256]{1,0:T(8,128)(2,1)S(1)}, bf16[272,256]{1,0:T(8,128)(2,1)S(1)}, u32[]{:S(2)}, u32[]{:S(2)}) %collective-permute-start.7) | collective-permute-done | bytes 139296 | tf_op jit(solution)/shard_map/ppermute | solution.py:333
  29.4 1.5 %collective-permute-start.4 = (bf16[272,256]{1,0:T(8,128)(2,1)S(1)}, bf16[272,256]{1,0:T(8,128)(2,1)S(1)}, u32[]{:S(2)}, u32[]{:S(2)}) collective-permute-start(bf16[272,256]{1,0:T(8,128)(2,1)S(1)} %tied.1.refs_0_), channel_id=1, source_target_pairs={{0,6},{1,7},{2,8},{3,9},{4,10},{5,11},{6,12},{7,13},{8,14},{9,15},... | collective-permute-start | bytes 417800 | tf_op jit(solution)/shard_map/ppermute | solution.py:333
  30.9 0.0 collective-permute-done.10.refs_4_
  30.9 3.5 %collective-permute-start.5 = (bf16[272,256]{1,0:T(8,128)(2,1)S(1)}, bf16[272,256]{1,0:T(8,128)(2,1)S(1)}, u32[]{:S(2)}, u32[]{:S(2)}) collective-permute-start(bf16[272,256]{1,0:T(8,128)(2,1)S(1)} %tied.1.refs_0_), channel_id=1, source_target_pairs={{0,8},{1,9},{2,10},{3,11},{4,12},{5,13},{6,14},{7,15},{8,0},{9,1},... | collective-permute-start | bytes 417800 | tf_op jit(solution)/shard_map/ppermute | solution.py:333
  34.4 3.5 %collective-permute-done.8.refs_3_ = bf16[272,256]{1,0:T(8,128)(2,1)S(1)} collective-permute-done((bf16[272,256]{1,0:T(8,128)(2,1)S(1)}, bf16[272,256]{1,0:T(8,128)(2,1)S(1)}, u32[]{:S(2)}, u32[]{:S(2)}) %collective-permute-start.8) | collective-permute-done | bytes 139296 | tf_op jit(solution)/shard_map/ppermute | solution.py:333
  38.0 0.0 collective-permute-done.1.qdx_ref.qx_ref
  38.0 10.5 %bwd.1 = (bf16[128,1024]{1,0:T(8,128)(2,1)S(1)}, bf16[128,1024]{1,0:T(8,128)(2,1)S(1)}, bf16[256,256]{1,0:T(8,128)(2,1)S(1)}, bf16[256,256]{1,0:T(8,128)(2,1)S(1...) custom-call(s32[2]{0:T(128)S(1)} %pad_add_fusion.where_ref, ...), custom_call_target="tpu_custom_call" | custom-call | flops 3355443200 | bytes 4194304 | tf_op jit(solution)/shard_map/bwd/pallas_call | solution.py:318
  48.5 0.1 collective-permute-start.17
  48.5 2.0 %collective-permute-start.6 = (bf16[272,256]{1,0:T(8,128)(2,1)S(1)}, bf16[272,256]{1,0:T(8,128)(2,1)S(1)}, u32[]{:S(2)}, u32[]{:S(2)}) collective-permute-start(bf16[272,256]{1,0:T(8,128)(2,1)S(1)} %tied.1.refs_0_), channel_id=1, source_target_pairs={{0,2},{1,3},{2,4},{3,5},{4,6},{5,7},{6,8},{7,9},{8,10},{9,11},{10,... | collective-permute-start | bytes 417800 | tf_op jit(solution)/shard_map/ppermute | solution.py:333
  50.6 0.0 collective-permute-done.3.refs_1_
  50.6 0.7 collective-permute-start.14
  51.3 0.0 collective-permute-done.4.refs_2_
  51.3 0.4 collective-permute-start.15
  51.7 0.0 collective-permute-done.5.refs_3_
  51.7 1.3 %collective-permute-start.11 = (bf16[256,256]{1,0:T(8,128)(2,1)S(1)}, bf16[256,256]{1,0:T(8,128)(2,1)S(1)}, u32[]{:S(2)}, u32[]{:S(2)}) collective-permute-start(bf16[256,256]{1,0:T(8,128)(2,1)S(1)} %get-tuple-element.32), channel_id=1, source_target_pairs={{0,14},{1,15},{2,0},{3,1},{4,2},{5,3},{6,4},{7,5},{8,6},{9,7},{10,... | collective-permute-start | bytes 393224 | tf_op jit(solution)/shard_map/ppermute | solution.py:333
  53.0 0.8 collective-permute-done.17
  53.8 1.3 %collective-permute-start.16 = (bf16[256,256]{1,0:T(8,128)(2,1)S(1)}, bf16[256,256]{1,0:T(8,128)(2,1)S(1)}, u32[]{:S(2)}, u32[]{:S(2)}) collective-permute-start(bf16[256,256]{1,0:T(8,128)(2,1)S(1)} %get-tuple-element.39), channel_id=1, source_target_pairs={{0,12},{1,13},{2,14},{3,15},{4,0},{5,1},{6,2},{7,3},{8,4},{9,5},{1... | collective-permute-start | bytes 393224 | tf_op jit(solution)/shard_map/ppermute | solution.py:333
  55.1 0.0 collective-permute-done.6.refs_4_
  55.1 4.8 %collective-permute-start.18 = (bf16[256,256]{1,0:T(8,128)(2,1)S(1)}, bf16[256,256]{1,0:T(8,128)(2,1)S(1)}, u32[]{:S(2)}, u32[]{:S(2)}) collective-permute-start(bf16[256,256]{1,0:T(8,128)(2,1)S(1)} %add_convert_fusion), channel_id=1, source_target_pairs={{0,10},{1,11},{2,12},{3,13},{4,14},{5,15},{6,0},{7,1},{8,2},{9,3},... | collective-permute-start | bytes 393224 | tf_op jit(solution)/shard_map/ppermute | solution.py:333
  59.9 0.7 collective-permute-done.11.refs_5_.refs_1_
  60.6 5.0 %fwd.1 = (bf16[128,1024]{1,0:T(8,128)(2,1)S(1)}, bf16[128,1024]{1,0:T(8,128)(2,1)S(1)}) custom-call(s32[2]{0:T(128)S(1)} %pad_add_fusion.where_ref, bf16[128,3072]{1,0:T(8,128)(2,1)S(1)} %get-tuple-element.26.qd_ref.q_ref, bf16[128,3072]{1,0:T(8,128)(2,1)S(1)} %collective-permute-done.1.qdx_ref.qx_ref, bf16[272,256]{1,0:T(8,128)(2,1)S(1)} %tied.1.refs_0_, ...), custom_call_target="tpu_custom_call" | custom-call | flops 1342177280 | bytes 2097152 | tf_op jit(solution)/shard_map/fwd/pallas_call | solution.py:290
  65.6 1.6 %collective-permute-start.12 = (bf16[128,1024]{1,0:T(8,128)(2,1)S(1)}, bf16[128,1024]{1,0:T(8,128)(2,1)S(1)}, u32[]{:S(2)}, u32[]{:S(2)}) collective-permute-start(bf16[128,1024]{1,0:T(8,128)(2,1)S(1)} %get-tuple-element.33), channel_id=1, source_target_pairs={{0,64},{64,128},{128,192},{192,0},{1,65},{65,129},{129,193},{193,1... | collective-permute-start | bytes 786440 | tf_op jit(solution)/shard_map/ppermute | solution.py:342
  67.2 0.0 collective-permute-done.16.refs_2_
  67.2 1.5 %collective-permute-start.13 = (bf16[128,1024]{1,0:T(8,128)(2,1)S(1)}, bf16[128,1024]{1,0:T(8,128)(2,1)S(1)}, u32[]{:S(2)}, u32[]{:S(2)}) collective-permute-start(bf16[128,1024]{1,0:T(8,128)(2,1)S(1)} %get-tuple-element.34), channel_id=1, source_target_pairs={{0,65},{1,64},{2,67},{3,66},{4,69},{5,68},{6,71},{7,70},{8,73},{9,... | collective-permute-start | bytes 786440 | tf_op jit(solution)/shard_map/ppermute | solution.py:350
  68.7 2.6 %collective-permute-done.18.refs_3_ = bf16[256,256]{1,0:T(8,128)(2,1)S(1)} collective-permute-done((bf16[256,256]{1,0:T(8,128)(2,1)S(1)}, bf16[256,256]{1,0:T(8,128)(2,1)S(1)}, u32[]{:S(2)}, u32[]{:S(2)}) %collective-permute-start.18) | collective-permute-done | bytes 131104 | tf_op jit(solution)/shard_map/ppermute | solution.py:333
  71.2 0.0 collective-permute-done.14.refs_4_.refs_0_
  71.3 0.0 collective-permute-done.15.refs_5_.refs_1_
  71.3 0.6 total.1
  71.9 0.8 collective-permute-start.19
  72.7 5.4 %collective-permute-done.19.refs_2_ = bf16[256,256]{1,0:T(8,128)(2,1)S(1)} collective-permute-done((bf16[256,256]{1,0:T(8,128)(2,1)S(1)}, bf16[256,256]{1,0:T(8,128)(2,1)S(1)}, u32[]{:S(2)}, u32[]{:S(2)}) %collective-permute-start.19) | collective-permute-done | bytes 131104 | tf_op jit(solution)/shard_map/ppermute | solution.py:342
  78.1 0.0 collective-permute-start.20
  78.1 0.0 collective-permute-done.12.own
  78.2 0.0 collective-permute-done.13.cross
  78.2 1.4 %output.1 = (bf16[128,2048]{1,0:T(8,128)(2,1)}, bf16[16,128]{1,0:T(8,128)(2,1)S(1)}) custom-call(s32[2]{0:T(128)S(1)} %pad_add_fusion.where_ref, bf16[128,1024]{1,0:T(8,128)(2,1)S(1)} %collective-permute-done.12.own, bf16[128,1024]{1,0:T(8,128)(2,1)S(1)} %collective-permute-done.13.cross), custom_call_target="tpu_custom_call" | custom-call | flops 1342177280 | bytes 524288 | tf_op jit(solution)/shard_map/output/pallas_call | solution.py:431
  79.5 2.9 %collective-permute-done.20.refs_3_ = bf16[128,256]{1,0:T(8,128)(2,1)S(1)} collective-permute-done((bf16[128,256]{1,0:T(8,128)(2,1)S(1)}, bf16[128,256]{1,0:T(8,128)(2,1)S(1)}, u32[]{:S(2)}, u32[]{:S(2)}) %collective-permute-start.20) | collective-permute-done | bytes 65568 | tf_op jit(solution)/shard_map/ppermute | solution.py:337
  82.4 1.4 %final.1 = (bf16[128,2048]{1,0:T(8,128)(2,1)}, bf16[128,256]{1,0:T(8,128)(2,1)}, bf16[128,256]{1,0:T(8,128)(2,1)}) custom-call(s32[2]{0:T(128)S(1)} %pad_add_fusion.where_ref, bf16[128,1024]{1,0:T(8,128)(2,1)S(1)} %collective-permute-done.14.refs_4_.refs_0_, bf16[128,1024]{1,0:T(8,128)(2,1)S(1)} %collective-permute-done.15.refs_5_.refs_1_, ...), custom_call_target="tpu_custom_call" | custom-call | bytes 524288 | tf_op jit(solution)/shard_map/final/pallas_call | solution.py:440
  (2 shorter events, 0.0 us)
Async XLA Ops:
  2.3 5.7 %collective-permute-start = (bf16[144,512]{1,0:T(8,128)(2,1)S(1)}, bf16[144,512]{1,0:T(8,128)(2,1)S(1)}, u32[]{:S(2)}, u32[]{:S(2)}) collective-permute-start(bf16[144,512]{1,0:T(8,128)(2,1)S(1)} %get-tuple-element.25.refs_3_), channel_id=1, source_target_pairs={{0,1},{1,0},{2,3},{3,2},{4,5},{5,4},{6,7},{7,6},{8,9},{9,8},{10,11... | collective-permute-start | bytes 442376 | tf_op jit(solution)/shard_map/ppermute | solution.py:337
  8.6 29.4 %collective-permute-start.1 = (bf16[128,3072]{1,0:T(8,128)(2,1)S(1)}, bf16[128,3072]{1,0:T(8,128)(2,1)S(1)}, u32[]{:S(2)}, u32[]{:S(2)}) collective-permute-start(bf16[128,3072]{1,0:T(8,128)(2,1)S(1)} %get-tuple-element.29), channel_id=1, source_target_pairs={{0,1},{1,0},{2,3},{3,2},{4,5},{5,4},{6,7},{7,6},{8,9},{9,8},{10,11... | collective-permute-start | bytes 2359304 | tf_op jit(solution)/shard_map/ppermute | solution.py:337
  10.1 11.1 %collective-permute-start.9 = (bf16[272,256]{1,0:T(8,128)(2,1)S(1)}, bf16[272,256]{1,0:T(8,128)(2,1)S(1)}, u32[]{:S(2)}, u32[]{:S(2)}) collective-permute-start(bf16[272,256]{1,0:T(8,128)(2,1)S(1)} %get-tuple-element.31.refs_0_), channel_id=1, source_target_pairs={{0,12},{1,13},{2,14},{3,15},{4,0},{5,1},{6,2},{7,3},{8,4},{9,5},{1... | collective-permute-start | bytes 417800 | tf_op jit(solution)/shard_map/ppermute | solution.py:333
  16.4 10.0 %collective-permute-start.2 = (bf16[272,256]{1,0:T(8,128)(2,1)S(1)}, bf16[272,256]{1,0:T(8,128)(2,1)S(1)}, u32[]{:S(2)}, u32[]{:S(2)}) collective-permute-start(bf16[272,256]{1,0:T(8,128)(2,1)S(1)} %get-tuple-element.31.refs_0_), channel_id=1, source_target_pairs={{0,4},{1,5},{2,6},{3,7},{4,8},{5,9},{6,10},{7,11},{8,12},{9,13},{1... | collective-permute-start | bytes 417800 | tf_op jit(solution)/shard_map/ppermute | solution.py:333
  16.5 13.0 %collective-permute-start.7 = (bf16[272,256]{1,0:T(8,128)(2,1)S(1)}, bf16[272,256]{1,0:T(8,128)(2,1)S(1)}, u32[]{:S(2)}, u32[]{:S(2)}) collective-permute-start(bf16[272,256]{1,0:T(8,128)(2,1)S(1)} %get-tuple-element.31.refs_0_), channel_id=1, source_target_pairs={{0,2},{1,3},{2,4},{3,5},{4,6},{5,7},{6,8},{7,9},{8,10},{9,11},{10,... | collective-permute-start | bytes 417800 | tf_op jit(solution)/shard_map/ppermute | solution.py:333
  21.2 9.7 %collective-permute-start.10 = (bf16[272,256]{1,0:T(8,128)(2,1)S(1)}, bf16[272,256]{1,0:T(8,128)(2,1)S(1)}, u32[]{:S(2)}, u32[]{:S(2)}) collective-permute-start(bf16[272,256]{1,0:T(8,128)(2,1)S(1)} %collective-permute-done.9), channel_id=1, source_target_pairs={{0,12},{1,13},{2,14},{3,15},{4,0},{5,1},{6,2},{7,3},{8,4},{9,5},{1... | collective-permute-start | bytes 417800 | tf_op jit(solution)/shard_map/ppermute | solution.py:333
  26.4 11.5 %collective-permute-start.8 = (bf16[272,256]{1,0:T(8,128)(2,1)S(1)}, bf16[272,256]{1,0:T(8,128)(2,1)S(1)}, u32[]{:S(2)}, u32[]{:S(2)}) collective-permute-start(bf16[272,256]{1,0:T(8,128)(2,1)S(1)} %collective-permute-done.2.after.refs_2_), channel_id=1, source_target_pairs={{0,2},{1,3},{2,4},{3,5},{4,6},{5,7},{6,8},{7,9},{8,10},{9,11},{10,... | collective-permute-start | bytes 417800 | tf_op jit(solution)/shard_map/ppermute | solution.py:333
  28.4 22.1 %collective-permute-start.3 = (bf16[272,256]{1,0:T(8,128)(2,1)S(1)}, bf16[272,256]{1,0:T(8,128)(2,1)S(1)}, u32[]{:S(2)}, u32[]{:S(2)}) collective-permute-start(bf16[272,256]{1,0:T(8,128)(2,1)S(1)} %tied.1.refs_0_), channel_id=1, source_target_pairs={{0,4},{1,5},{2,6},{3,7},{4,8},{5,9},{6,10},{7,11},{8,12},{9,13},{1... | collective-permute-start | bytes 417800 | tf_op jit(solution)/shard_map/ppermute | solution.py:333
  29.4 21.9 %collective-permute-start.4 = (bf16[272,256]{1,0:T(8,128)(2,1)S(1)}, bf16[272,256]{1,0:T(8,128)(2,1)S(1)}, u32[]{:S(2)}, u32[]{:S(2)}) collective-permute-start(bf16[272,256]{1,0:T(8,128)(2,1)S(1)} %tied.1.refs_0_), channel_id=1, source_target_pairs={{0,6},{1,7},{2,8},{3,9},{4,10},{5,11},{6,12},{7,13},{8,14},{9,15},... | collective-permute-start | bytes 417800 | tf_op jit(solution)/shard_map/ppermute | solution.py:333
  30.9 20.8 %collective-permute-start.5 = (bf16[272,256]{1,0:T(8,128)(2,1)S(1)}, bf16[272,256]{1,0:T(8,128)(2,1)S(1)}, u32[]{:S(2)}, u32[]{:S(2)}) collective-permute-start(bf16[272,256]{1,0:T(8,128)(2,1)S(1)} %tied.1.refs_0_), channel_id=1, source_target_pairs={{0,8},{1,9},{2,10},{3,11},{4,12},{5,13},{6,14},{7,15},{8,0},{9,1},... | collective-permute-start | bytes 417800 | tf_op jit(solution)/shard_map/ppermute | solution.py:333
  48.5 5.3 %collective-permute-start.17 = (bf16[256,256]{1,0:T(8,128)(2,1)S(1)}, bf16[256,256]{1,0:T(8,128)(2,1)S(1)}, u32[]{:S(2)}, u32[]{:S(2)}) collective-permute-start(bf16[256,256]{1,0:T(8,128)(2,1)S(1)} %get-tuple-element.41), channel_id=1, source_target_pairs={{0,14},{1,15},{2,0},{3,1},{4,2},{5,3},{6,4},{7,5},{8,6},{9,7},{10,... | collective-permute-start | bytes 393224 | tf_op jit(solution)/shard_map/ppermute | solution.py:333
  48.5 6.6 %collective-permute-start.6 = (bf16[272,256]{1,0:T(8,128)(2,1)S(1)}, bf16[272,256]{1,0:T(8,128)(2,1)S(1)}, u32[]{:S(2)}, u32[]{:S(2)}) collective-permute-start(bf16[272,256]{1,0:T(8,128)(2,1)S(1)} %tied.1.refs_0_), channel_id=1, source_target_pairs={{0,2},{1,3},{2,4},{3,5},{4,6},{5,7},{6,8},{7,9},{8,10},{9,11},{10,... | collective-permute-start | bytes 417800 | tf_op jit(solution)/shard_map/ppermute | solution.py:333
  50.6 20.7 %collective-permute-start.14 = (bf16[128,1024]{1,0:T(8,128)(2,1)S(1)}, bf16[128,1024]{1,0:T(8,128)(2,1)S(1)}, u32[]{:S(2)}, u32[]{:S(2)}) collective-permute-start(bf16[128,1024]{1,0:T(8,128)(2,1)S(1)} %get-tuple-element.36), channel_id=1, source_target_pairs={{0,192},{64,0},{128,64},{192,128},{1,193},{65,1},{129,65},{193,129... | collective-permute-start | bytes 786440 | tf_op jit(solution)/shard_map/ppermute | solution.py:342
  51.3 19.9 %collective-permute-start.15 = (bf16[128,1024]{1,0:T(8,128)(2,1)S(1)}, bf16[128,1024]{1,0:T(8,128)(2,1)S(1)}, u32[]{:S(2)}, u32[]{:S(2)}) collective-permute-start(bf16[128,1024]{1,0:T(8,128)(2,1)S(1)} %get-tuple-element.37), channel_id=1, source_target_pairs={{0,193},{1,192},{2,195},{3,194},{4,197},{5,196},{6,199},{7,198},{8... | collective-permute-start | bytes 786440 | tf_op jit(solution)/shard_map/ppermute | solution.py:350
  51.7 8.9 %collective-permute-start.11 = (bf16[256,256]{1,0:T(8,128)(2,1)S(1)}, bf16[256,256]{1,0:T(8,128)(2,1)S(1)}, u32[]{:S(2)}, u32[]{:S(2)}) collective-permute-start(bf16[256,256]{1,0:T(8,128)(2,1)S(1)} %get-tuple-element.32), channel_id=1, source_target_pairs={{0,14},{1,15},{2,0},{3,1},{4,2},{5,3},{6,4},{7,5},{8,6},{9,7},{10,... | collective-permute-start | bytes 393224 | tf_op jit(solution)/shard_map/ppermute | solution.py:333
  53.8 13.4 %collective-permute-start.16 = (bf16[256,256]{1,0:T(8,128)(2,1)S(1)}, bf16[256,256]{1,0:T(8,128)(2,1)S(1)}, u32[]{:S(2)}, u32[]{:S(2)}) collective-permute-start(bf16[256,256]{1,0:T(8,128)(2,1)S(1)} %get-tuple-element.39), channel_id=1, source_target_pairs={{0,12},{1,13},{2,14},{3,15},{4,0},{5,1},{6,2},{7,3},{8,4},{9,5},{1... | collective-permute-start | bytes 393224 | tf_op jit(solution)/shard_map/ppermute | solution.py:333
  55.1 16.1 %collective-permute-start.18 = (bf16[256,256]{1,0:T(8,128)(2,1)S(1)}, bf16[256,256]{1,0:T(8,128)(2,1)S(1)}, u32[]{:S(2)}, u32[]{:S(2)}) collective-permute-start(bf16[256,256]{1,0:T(8,128)(2,1)S(1)} %add_convert_fusion), channel_id=1, source_target_pairs={{0,10},{1,11},{2,12},{3,13},{4,14},{5,15},{6,0},{7,1},{8,2},{9,3},... | collective-permute-start | bytes 393224 | tf_op jit(solution)/shard_map/ppermute | solution.py:333
  65.6 12.6 %collective-permute-start.12 = (bf16[128,1024]{1,0:T(8,128)(2,1)S(1)}, bf16[128,1024]{1,0:T(8,128)(2,1)S(1)}, u32[]{:S(2)}, u32[]{:S(2)}) collective-permute-start(bf16[128,1024]{1,0:T(8,128)(2,1)S(1)} %get-tuple-element.33), channel_id=1, source_target_pairs={{0,64},{64,128},{128,192},{192,0},{1,65},{65,129},{129,193},{193,1... | collective-permute-start | bytes 786440 | tf_op jit(solution)/shard_map/ppermute | solution.py:342
  67.2 11.0 %collective-permute-start.13 = (bf16[128,1024]{1,0:T(8,128)(2,1)S(1)}, bf16[128,1024]{1,0:T(8,128)(2,1)S(1)}, u32[]{:S(2)}, u32[]{:S(2)}) collective-permute-start(bf16[128,1024]{1,0:T(8,128)(2,1)S(1)} %get-tuple-element.34), channel_id=1, source_target_pairs={{0,65},{1,64},{2,67},{3,66},{4,69},{5,68},{6,71},{7,70},{8,73},{9,... | collective-permute-start | bytes 786440 | tf_op jit(solution)/shard_map/ppermute | solution.py:350
  71.9 6.3 %collective-permute-start.19 = (bf16[256,256]{1,0:T(8,128)(2,1)S(1)}, bf16[256,256]{1,0:T(8,128)(2,1)S(1)}, u32[]{:S(2)}, u32[]{:S(2)}) collective-permute-start(bf16[256,256]{1,0:T(8,128)(2,1)S(1)} %total.1), channel_id=1, source_target_pairs={{0,192},{64,0},{128,64},{192,128},{1,193},{65,1},{129,65},{193,129... | collective-permute-start | bytes 393224 | tf_op jit(solution)/shard_map/ppermute | solution.py:342
  78.1 4.3 %collective-permute-start.20 = (bf16[128,256]{1,0:T(8,128)(2,1)S(1)}, bf16[128,256]{1,0:T(8,128)(2,1)S(1)}, u32[]{:S(2)}, u32[]{:S(2)}) collective-permute-start(bf16[128,256]{1,0:T(8,128)(2,1)S(1)} %slice.4), channel_id=1, source_target_pairs={{0,1},{1,0},{2,3},{3,2},{4,5},{5,4},{6,7},{7,6},{8,9},{9,8},{10,11... | collective-permute-start | bytes 196616 | tf_op jit(solution)/shard_map/ppermute | solution.py:337

commit v7 on v6

--- a/solution.py
+++ b/solution.py
@@ -422,7 +422,7 @@
     three = (parts[3].astype(F32) + far.astype(F32)).astype(BF16)
     terms = [parts[0]] + [along_z(parts[k], -k) for k in (1, 2)] + [along_z(three, -3)]
     dq = handed(dq_own, -1), handed_across(dq_cross, -1)
-    o_own, o_cross = run_fwd(where, own, crossed, blocks_f, (terms[1],))
+    o_own, o_cross = run_fwd(where, own, crossed, blocks_f, (three,))
     dq = handed(dq_own, -1), handed_across(dq_cross, -1)
     (summed,) = call(
         total_kernel, [shape(PAIR, 2 * HEAD)], [VMEM] * 4 + [ANY] * 2, name="total"

time: 84.2 us -> 84.1 us (level)
  transfers between devices with their start and end apart: 21 -> 21, of which waited for: 10 -> 9; matrix products, arithmetic and copies ran while one was open for 0% -> 0% of each run, Pallas kernels for 24% -> 24%
where the time goes in v7:
time: 84.1 us; the launch traced here: 84 us
  starting transfers between devices  35.8 us (43%)
  waiting for transfers between devices  23.7 us (28%)
  Pallas kernels  23.4 us (28%)
  between operations  0.96 us (1%)
    ppermute x13, starting transfers between devices, along_z(): lax.ppermute(block, 'cp', [(i, (i + 2 * distance) % n) for i in range(n)])  28.1 us
    ppermute x13, waiting for transfers between devices, along_z(): lax.ppermute(block, 'cp', [(i, (i + 2 * distance) % n) for i in range(n)])  13.2 us
    pallas_call x1, Pallas kernels, run_bwd(): call(bwd_kernel, outs, 2 + SLOTS, scratch, 5 * MATMUL, 2 ** 22, 'bwd', li...  10.4 us
    ppermute x3, waiting for transfers between devices, handed(): lax.ppermute(block, 'section', [(i, (i + distance) % n) for i in range(n)])  5.44 us
    ppermute x3, waiting for transfers between devices, swapped(): lax.ppermute(block, 'cp', [(i, i ^ 1) for i in range(lax.axis_size('cp'))])  5.03 us
    pallas_call x1, Pallas kernels, run_fwd(): call(fwd_kernel, [shape(ROWS, HALF)] * 2, [VMEM] * (2 + SLOTS) + [ANY] *...  4.96 us
    ppermute x3, starting transfers between devices, swapped(): lax.ppermute(block, 'cp', [(i, i ^ 1) for i in range(lax.axis_size('cp'))])  3.16 us
    ppermute x3, starting transfers between devices, handed(): lax.ppermute(block, 'section', [(i, (i + distance) % n) for i in range(n)])  3.15 us
  transfers between devices with their start and end apart: 21, of which 9 were waited for; matrix products, arithmetic and copies ran while one was open for 0% of the time, Pallas kernels for 24%

profile of v7, /device:TPU:24, one launch (start us, length us, event | category | flops | bytes accessed | tf_op | source)
XLA Modules:
  0.0 84.0 jit_solution(1638587551127846991)
XLA Ops:
  0.6 0.1 pad_add_fusion.where_ref
  0.7 1.6 %split.1 = (bf16[144,512]{1,0:T(8,128)(2,1)S(1)}, bf16[144,512]{1,0:T(8,128)(2,1)S(1)}) custom-call(s32[2]{0:T(128)S(1)} %pad_add_fusion.where_ref, bf16[128,256]{1,0:T(8,128)(2,1)} %bitcast.16, bf16[128,256]{1,0:T(8,128)(2,1)} %bitcast.17, s32[1,128]{1,0:T(1,128)} %refs_2_.1, bf16[128,256]{1,0:T(8,128)(2,1)} %bitcast.18, bf16[128,256]{1,0:T(8,128)(2,1)} %bitcast.19, ...), custom_call_target="tpu_custom_call" | custom-call | bytes 524288 | tf_op jit(solution)/shard_map/split/pallas_call | solution.py:360
  2.3 1.6 %collective-permute-start = (bf16[144,512]{1,0:T(8,128)(2,1)S(1)}, bf16[144,512]{1,0:T(8,128)(2,1)S(1)}, u32[]{:S(2)}, u32[]{:S(2)}) collective-permute-start(bf16[144,512]{1,0:T(8,128)(2,1)S(1)} %get-tuple-element.25.refs_3_), channel_id=1, source_target_pairs={{0,1},{1,0},{2,3},{3,2},{4,5},{5,4},{6,7},{7,6},{8,9},{9,8},{10,11... | collective-permute-start | bytes 442376 | tf_op jit(solution)/shard_map/ppermute | solution.py:337
  3.9 1.9 %halves.1 = (bf16[128,3072]{1,0:T(8,128)(2,1)S(1)}, bf16[128,3072]{1,0:T(8,128)(2,1)S(1)}) custom-call(s32[2]{0:T(128)S(1)} %pad_add_fusion.where_ref, bf16[128,2048]{1,0:T(8,128)(2,1)} %bitcast.13, bf16[128,2048]{1,0:T(8,128)(2,1)} %bitcast.14, bf16[128,2048]{1,0:T(8,128)(2,1)} %bitcast.15, bf16[144,512]{1,0:T(8,128)(2,1)S(1)} %get-tuple-element.25.refs_3_), custom_call_target="tpu_custom_call" | custom-call | bytes 524288 | tf_op jit(solution)/shard_map/halves/pallas_call | solution.py:402
  5.9 2.1 %collective-permute-done.got = bf16[144,512]{1,0:T(8,128)(2,1)S(1)} collective-permute-done((bf16[144,512]{1,0:T(8,128)(2,1)S(1)}, bf16[144,512]{1,0:T(8,128)(2,1)S(1)}, u32[]{:S(2)}, u32[]{:S(2)}) %collective-permute-start) | collective-permute-done | bytes 147488 | tf_op jit(solution)/shard_map/ppermute | solution.py:337
  8.0 0.6 join.1
  8.6 1.6 %collective-permute-start.1 = (bf16[128,3072]{1,0:T(8,128)(2,1)S(1)}, bf16[128,3072]{1,0:T(8,128)(2,1)S(1)}, u32[]{:S(2)}, u32[]{:S(2)}) collective-permute-start(bf16[128,3072]{1,0:T(8,128)(2,1)S(1)} %get-tuple-element.29), channel_id=1, source_target_pairs={{0,1},{1,0},{2,3},{3,2},{4,5},{5,4},{6,7},{7,6},{8,9},{9,8},{10,11... | collective-permute-start | bytes 2359304 | tf_op jit(solution)/shard_map/ppermute | solution.py:337
  10.1 6.3 %collective-permute-start.9 = (bf16[272,256]{1,0:T(8,128)(2,1)S(1)}, bf16[272,256]{1,0:T(8,128)(2,1)S(1)}, u32[]{:S(2)}, u32[]{:S(2)}) collective-permute-start(bf16[272,256]{1,0:T(8,128)(2,1)S(1)} %get-tuple-element.31.refs_0_), channel_id=1, source_target_pairs={{0,12},{1,13},{2,14},{3,15},{4,0},{5,1},{6,2},{7,3},{8,4},{9,5},{1... | collective-permute-start | bytes 417800 | tf_op jit(solution)/shard_map/ppermute | solution.py:333
  16.4 0.0 collective-permute-start.2
  16.5 1.0 %collective-permute-start.7 = (bf16[272,256]{1,0:T(8,128)(2,1)S(1)}, bf16[272,256]{1,0:T(8,128)(2,1)S(1)}, u32[]{:S(2)}, u32[]{:S(2)}) collective-permute-start(bf16[272,256]{1,0:T(8,128)(2,1)S(1)} %get-tuple-element.31.refs_0_), channel_id=1, source_target_pairs={{0,2},{1,3},{2,4},{3,5},{4,6},{5,7},{6,8},{7,9},{8,10},{9,11},{10,... | collective-permute-start | bytes 417800 | tf_op jit(solution)/shard_map/ppermute | solution.py:333
  17.5 3.7 %collective-permute-done.9 = bf16[272,256]{1,0:T(8,128)(2,1)S(1)} collective-permute-done((bf16[272,256]{1,0:T(8,128)(2,1)S(1)}, bf16[272,256]{1,0:T(8,128)(2,1)S(1)}, u32[]{:S(2)}, u32[]{:S(2)}) %collective-permute-start.9) | collective-permute-done | bytes 139296 | tf_op jit(solution)/shard_map/ppermute | solution.py:333
  21.2 4.7 %collective-permute-start.10 = (bf16[272,256]{1,0:T(8,128)(2,1)S(1)}, bf16[272,256]{1,0:T(8,128)(2,1)S(1)}, u32[]{:S(2)}, u32[]{:S(2)}) collective-permute-start(bf16[272,256]{1,0:T(8,128)(2,1)S(1)} %collective-permute-done.9), channel_id=1, source_target_pairs={{0,12},{1,13},{2,14},{3,15},{4,0},{5,1},{6,2},{7,3},{8,4},{9,5},{1... | collective-permute-start | bytes 417800 | tf_op jit(solution)/shard_map/ppermute | solution.py:333
  25.9 0.5 collective-permute-done.2.after.refs_2_
  26.4 1.4 %collective-permute-start.8 = (bf16[272,256]{1,0:T(8,128)(2,1)S(1)}, bf16[272,256]{1,0:T(8,128)(2,1)S(1)}, u32[]{:S(2)}, u32[]{:S(2)}) collective-permute-start(bf16[272,256]{1,0:T(8,128)(2,1)S(1)} %collective-permute-done.2.after.refs_2_), channel_id=1, source_target_pairs={{0,2},{1,3},{2,4},{3,5},{4,6},{5,7},{6,8},{7,9},{8,10},{9,11},{10,... | collective-permute-start | bytes 417800 | tf_op jit(solution)/shard_map/ppermute | solution.py:333
  27.9 0.5 tied.1.refs_0_
  28.4 0.1 collective-permute-start.3
  28.5 0.9 %collective-permute-done.7.refs_1_ = bf16[272,256]{1,0:T(8,128)(2,1)S(1)} collective-permute-done((bf16[272,256]{1,0:T(8,128)(2,1)S(1)}, bf16[272,256]{1,0:T(8,128)(2,1)S(1)}, u32[]{:S(2)}, u32[]{:S(2)}) %collective-permute-start.7) | collective-permute-done | bytes 139296 | tf_op jit(solution)/shard_map/ppermute | solution.py:333
  29.4 1.5 %collective-permute-start.4 = (bf16[272,256]{1,0:T(8,128)(2,1)S(1)}, bf16[272,256]{1,0:T(8,128)(2,1)S(1)}, u32[]{:S(2)}, u32[]{:S(2)}) collective-permute-start(bf16[272,256]{1,0:T(8,128)(2,1)S(1)} %tied.1.refs_0_), channel_id=1, source_target_pairs={{0,6},{1,7},{2,8},{3,9},{4,10},{5,11},{6,12},{7,13},{8,14},{9,15},... | collective-permute-start | bytes 417800 | tf_op jit(solution)/shard_map/ppermute | solution.py:333
  30.9 0.0 collective-permute-done.10.refs_4_
  30.9 3.5 %collective-permute-start.5 = (bf16[272,256]{1,0:T(8,128)(2,1)S(1)}, bf16[272,256]{1,0:T(8,128)(2,1)S(1)}, u32[]{:S(2)}, u32[]{:S(2)}) collective-permute-start(bf16[272,256]{1,0:T(8,128)(2,1)S(1)} %tied.1.refs_0_), channel_id=1, source_target_pairs={{0,8},{1,9},{2,10},{3,11},{4,12},{5,13},{6,14},{7,15},{8,0},{9,1},... | collective-permute-start | bytes 417800 | tf_op jit(solution)/shard_map/ppermute | solution.py:333
  34.4 3.5 %collective-permute-done.8.refs_3_ = bf16[272,256]{1,0:T(8,128)(2,1)S(1)} collective-permute-done((bf16[272,256]{1,0:T(8,128)(2,1)S(1)}, bf16[272,256]{1,0:T(8,128)(2,1)S(1)}, u32[]{:S(2)}, u32[]{:S(2)}) %collective-permute-start.8) | collective-permute-done | bytes 139296 | tf_op jit(solution)/shard_map/ppermute | solution.py:333
  38.0 0.0 collective-permute-done.1.qdx_ref.qx_ref
  38.0 10.4 %bwd.1 = (bf16[128,1024]{1,0:T(8,128)(2,1)S(1)}, bf16[128,1024]{1,0:T(8,128)(2,1)S(1)}, bf16[256,256]{1,0:T(8,128)(2,1)S(1)}, bf16[256,256]{1,0:T(8,128)(2,1)S(1...) custom-call(s32[2]{0:T(128)S(1)} %pad_add_fusion.where_ref, ...), custom_call_target="tpu_custom_call" | custom-call | flops 3355443200 | bytes 4194304 | tf_op jit(solution)/shard_map/bwd/pallas_call | solution.py:318
  48.4 0.1 collective-permute-start.11
  48.5 2.0 %collective-permute-start.6 = (bf16[272,256]{1,0:T(8,128)(2,1)S(1)}, bf16[272,256]{1,0:T(8,128)(2,1)S(1)}, u32[]{:S(2)}, u32[]{:S(2)}) collective-permute-start(bf16[272,256]{1,0:T(8,128)(2,1)S(1)} %tied.1.refs_0_), channel_id=1, source_target_pairs={{0,2},{1,3},{2,4},{3,5},{4,6},{5,7},{6,8},{7,9},{8,10},{9,11},{10,... | collective-permute-start | bytes 417800 | tf_op jit(solution)/shard_map/ppermute | solution.py:333
  50.5 0.0 collective-permute-done.3.refs_1_
  50.5 0.7 collective-permute-start.14
  51.3 0.0 collective-permute-done.4.refs_2_
  51.3 0.4 collective-permute-start.15
  51.7 0.0 collective-permute-done.5.refs_3_
  51.7 1.3 %collective-permute-start.16 = (bf16[256,256]{1,0:T(8,128)(2,1)S(1)}, bf16[256,256]{1,0:T(8,128)(2,1)S(1)}, u32[]{:S(2)}, u32[]{:S(2)}) collective-permute-start(bf16[256,256]{1,0:T(8,128)(2,1)S(1)} %get-tuple-element.40), channel_id=1, source_target_pairs={{0,14},{1,15},{2,0},{3,1},{4,2},{5,3},{6,4},{7,5},{8,6},{9,7},{10,... | collective-permute-start | bytes 393224 | tf_op jit(solution)/shard_map/ppermute | solution.py:333
  53.0 0.7 collective-permute-done.11
  53.8 1.3 %collective-permute-start.17 = (bf16[256,256]{1,0:T(8,128)(2,1)S(1)}, bf16[256,256]{1,0:T(8,128)(2,1)S(1)}, u32[]{:S(2)}, u32[]{:S(2)}) collective-permute-start(bf16[256,256]{1,0:T(8,128)(2,1)S(1)} %get-tuple-element.41), channel_id=1, source_target_pairs={{0,12},{1,13},{2,14},{3,15},{4,0},{5,1},{6,2},{7,3},{8,4},{9,5},{1... | collective-permute-start | bytes 393224 | tf_op jit(solution)/shard_map/ppermute | solution.py:333
  55.1 0.0 collective-permute-done.6.refs_4_
  55.1 4.8 %collective-permute-start.18 = (bf16[256,256]{1,0:T(8,128)(2,1)S(1)}, bf16[256,256]{1,0:T(8,128)(2,1)S(1)}, u32[]{:S(2)}, u32[]{:S(2)}) collective-permute-start(bf16[256,256]{1,0:T(8,128)(2,1)S(1)} %add_convert_fusion.refs_5_), channel_id=1, source_target_pairs={{0,10},{1,11},{2,12},{3,13},{4,14},{5,15},{6,0},{7,1},{8,2},{9,3},... | collective-permute-start | bytes 393224 | tf_op jit(solution)/shard_map/ppermute | solution.py:333
  59.9 5.0 %fwd.1 = (bf16[128,1024]{1,0:T(8,128)(2,1)S(1)}, bf16[128,1024]{1,0:T(8,128)(2,1)S(1)}) custom-call(s32[2]{0:T(128)S(1)} %pad_add_fusion.where_ref, bf16[128,3072]{1,0:T(8,128)(2,1)S(1)} %get-tuple-element.26.qd_ref.q_ref, bf16[128,3072]{1,0:T(8,128)(2,1)S(1)} %collective-permute-done.1.qdx_ref.qx_ref, bf16[272,256]{1,0:T(8,128)(2,1)S(1)} %tied.1.refs_0_, ...), custom_call_target="tpu_custom_call" | custom-call | flops 1342177280 | bytes 2097152 | tf_op jit(solution)/shard_map/fwd/pallas_call | solution.py:290
  64.9 0.0 collective-permute-done.16.refs_1_
  64.9 1.6 %collective-permute-start.12 = (bf16[128,1024]{1,0:T(8,128)(2,1)S(1)}, bf16[128,1024]{1,0:T(8,128)(2,1)S(1)}, u32[]{:S(2)}, u32[]{:S(2)}) collective-permute-start(bf16[128,1024]{1,0:T(8,128)(2,1)S(1)} %get-tuple-element.34), channel_id=1, source_target_pairs={{0,64},{64,128},{128,192},{192,0},{1,65},{65,129},{129,193},{193,1... | collective-permute-start | bytes 786440 | tf_op jit(solution)/shard_map/ppermute | solution.py:342
  66.5 0.0 collective-permute-done.17.refs_2_
  66.5 1.0 %collective-permute-start.13 = (bf16[128,1024]{1,0:T(8,128)(2,1)S(1)}, bf16[128,1024]{1,0:T(8,128)(2,1)S(1)}, u32[]{:S(2)}, u32[]{:S(2)}) collective-permute-start(bf16[128,1024]{1,0:T(8,128)(2,1)S(1)} %get-tuple-element.35), channel_id=1, source_target_pairs={{0,65},{1,64},{2,67},{3,66},{4,69},{5,68},{6,71},{7,70},{8,73},{9,... | collective-permute-start | bytes 786440 | tf_op jit(solution)/shard_map/ppermute | solution.py:350
  67.5 3.7 %collective-permute-done.18.refs_3_ = bf16[256,256]{1,0:T(8,128)(2,1)S(1)} collective-permute-done((bf16[256,256]{1,0:T(8,128)(2,1)S(1)}, bf16[256,256]{1,0:T(8,128)(2,1)S(1)}, u32[]{:S(2)}, u32[]{:S(2)}) %collective-permute-start.18) | collective-permute-done | bytes 131104 | tf_op jit(solution)/shard_map/ppermute | solution.py:333
  71.2 0.0 collective-permute-done.14.refs_4_.refs_0_
  71.2 0.0 collective-permute-done.15.refs_5_.refs_1_
  71.2 0.6 total.1
  71.9 0.8 collective-permute-start.19
  72.7 5.4 %collective-permute-done.19.refs_2_ = bf16[256,256]{1,0:T(8,128)(2,1)S(1)} collective-permute-done((bf16[256,256]{1,0:T(8,128)(2,1)S(1)}, bf16[256,256]{1,0:T(8,128)(2,1)S(1)}, u32[]{:S(2)}, u32[]{:S(2)}) %collective-permute-start.19) | collective-permute-done | bytes 131104 | tf_op jit(solution)/shard_map/ppermute | solution.py:342
  78.1 0.0 collective-permute-start.20
  78.1 0.0 collective-permute-done.12.own
  78.1 0.0 collective-permute-done.13.cross
  78.2 1.4 %output.1 = (bf16[128,2048]{1,0:T(8,128)(2,1)}, bf16[16,128]{1,0:T(8,128)(2,1)S(1)}) custom-call(s32[2]{0:T(128)S(1)} %pad_add_fusion.where_ref, bf16[128,1024]{1,0:T(8,128)(2,1)S(1)} %collective-permute-done.12.own, bf16[128,1024]{1,0:T(8,128)(2,1)S(1)} %collective-permute-done.13.cross), custom_call_target="tpu_custom_call" | custom-call | flops 1342177280 | bytes 524288 | tf_op jit(solution)/shard_map/output/pallas_call | solution.py:431
  79.5 2.9 %collective-permute-done.20.refs_3_ = bf16[128,256]{1,0:T(8,128)(2,1)S(1)} collective-permute-done((bf16[128,256]{1,0:T(8,128)(2,1)S(1)}, bf16[128,256]{1,0:T(8,128)(2,1)S(1)}, u32[]{:S(2)}, u32[]{:S(2)}) %collective-permute-start.20) | collective-permute-done | bytes 65568 | tf_op jit(solution)/shard_map/ppermute | solution.py:337
  82.4 1.4 %final.1 = (bf16[128,2048]{1,0:T(8,128)(2,1)}, bf16[128,256]{1,0:T(8,128)(2,1)}, bf16[128,256]{1,0:T(8,128)(2,1)}) custom-call(s32[2]{0:T(128)S(1)} %pad_add_fusion.where_ref, bf16[128,1024]{1,0:T(8,128)(2,1)S(1)} %collective-permute-done.14.refs_4_.refs_0_, bf16[128,1024]{1,0:T(8,128)(2,1)S(1)} %collective-permute-done.15.refs_5_.refs_1_, ...), custom_call_target="tpu_custom_call" | custom-call | bytes 524288 | tf_op jit(solution)/shard_map/final/pallas_call | solution.py:440
  (2 shorter events, 0.0 us)
Async XLA Ops:
  2.3 5.7 %collective-permute-start = (bf16[144,512]{1,0:T(8,128)(2,1)S(1)}, bf16[144,512]{1,0:T(8,128)(2,1)S(1)}, u32[]{:S(2)}, u32[]{:S(2)}) collective-permute-start(bf16[144,512]{1,0:T(8,128)(2,1)S(1)} %get-tuple-element.25.refs_3_), channel_id=1, source_target_pairs={{0,1},{1,0},{2,3},{3,2},{4,5},{5,4},{6,7},{7,6},{8,9},{9,8},{10,11... | collective-permute-start | bytes 442376 | tf_op jit(solution)/shard_map/ppermute | solution.py:337
  8.6 29.4 %collective-permute-start.1 = (bf16[128,3072]{1,0:T(8,128)(2,1)S(1)}, bf16[128,3072]{1,0:T(8,128)(2,1)S(1)}, u32[]{:S(2)}, u32[]{:S(2)}) collective-permute-start(bf16[128,3072]{1,0:T(8,128)(2,1)S(1)} %get-tuple-element.29), channel_id=1, source_target_pairs={{0,1},{1,0},{2,3},{3,2},{4,5},{5,4},{6,7},{7,6},{8,9},{9,8},{10,11... | collective-permute-start | bytes 2359304 | tf_op jit(solution)/shard_map/ppermute | solution.py:337
  10.1 11.1 %collective-permute-start.9 = (bf16[272,256]{1,0:T(8,128)(2,1)S(1)}, bf16[272,256]{1,0:T(8,128)(2,1)S(1)}, u32[]{:S(2)}, u32[]{:S(2)}) collective-permute-start(bf16[272,256]{1,0:T(8,128)(2,1)S(1)} %get-tuple-element.31.refs_0_), channel_id=1, source_target_pairs={{0,12},{1,13},{2,14},{3,15},{4,0},{5,1},{6,2},{7,3},{8,4},{9,5},{1... | collective-permute-start | bytes 417800 | tf_op jit(solution)/shard_map/ppermute | solution.py:333
  16.4 10.0 %collective-permute-start.2 = (bf16[272,256]{1,0:T(8,128)(2,1)S(1)}, bf16[272,256]{1,0:T(8,128)(2,1)S(1)}, u32[]{:S(2)}, u32[]{:S(2)}) collective-permute-start(bf16[272,256]{1,0:T(8,128)(2,1)S(1)} %get-tuple-element.31.refs_0_), channel_id=1, source_target_pairs={{0,4},{1,5},{2,6},{3,7},{4,8},{5,9},{6,10},{7,11},{8,12},{9,13},{1... | collective-permute-start | bytes 417800 | tf_op jit(solution)/shard_map/ppermute | solution.py:333
  16.5 13.0 %collective-permute-start.7 = (bf16[272,256]{1,0:T(8,128)(2,1)S(1)}, bf16[272,256]{1,0:T(8,128)(2,1)S(1)}, u32[]{:S(2)}, u32[]{:S(2)}) collective-permute-start(bf16[272,256]{1,0:T(8,128)(2,1)S(1)} %get-tuple-element.31.refs_0_), channel_id=1, source_target_pairs={{0,2},{1,3},{2,4},{3,5},{4,6},{5,7},{6,8},{7,9},{8,10},{9,11},{10,... | collective-permute-start | bytes 417800 | tf_op jit(solution)/shard_map/ppermute | solution.py:333
  21.2 9.7 %collective-permute-start.10 = (bf16[272,256]{1,0:T(8,128)(2,1)S(1)}, bf16[272,256]{1,0:T(8,128)(2,1)S(1)}, u32[]{:S(2)}, u32[]{:S(2)}) collective-permute-start(bf16[272,256]{1,0:T(8,128)(2,1)S(1)} %collective-permute-done.9), channel_id=1, source_target_pairs={{0,12},{1,13},{2,14},{3,15},{4,0},{5,1},{6,2},{7,3},{8,4},{9,5},{1... | collective-permute-start | bytes 417800 | tf_op jit(solution)/shard_map/ppermute | solution.py:333
  26.4 11.5 %collective-permute-start.8 = (bf16[272,256]{1,0:T(8,128)(2,1)S(1)}, bf16[272,256]{1,0:T(8,128)(2,1)S(1)}, u32[]{:S(2)}, u32[]{:S(2)}) collective-permute-start(bf16[272,256]{1,0:T(8,128)(2,1)S(1)} %collective-permute-done.2.after.refs_2_), channel_id=1, source_target_pairs={{0,2},{1,3},{2,4},{3,5},{4,6},{5,7},{6,8},{7,9},{8,10},{9,11},{10,... | collective-permute-start | bytes 417800 | tf_op jit(solution)/shard_map/ppermute | solution.py:333
  28.4 22.1 %collective-permute-start.3 = (bf16[272,256]{1,0:T(8,128)(2,1)S(1)}, bf16[272,256]{1,0:T(8,128)(2,1)S(1)}, u32[]{:S(2)}, u32[]{:S(2)}) collective-permute-start(bf16[272,256]{1,0:T(8,128)(2,1)S(1)} %tied.1.refs_0_), channel_id=1, source_target_pairs={{0,4},{1,5},{2,6},{3,7},{4,8},{5,9},{6,10},{7,11},{8,12},{9,13},{1... | collective-permute-start | bytes 417800 | tf_op jit(solution)/shard_map/ppermute | solution.py:333
  29.4 21.9 %collective-permute-start.4 = (bf16[272,256]{1,0:T(8,128)(2,1)S(1)}, bf16[272,256]{1,0:T(8,128)(2,1)S(1)}, u32[]{:S(2)}, u32[]{:S(2)}) collective-permute-start(bf16[272,256]{1,0:T(8,128)(2,1)S(1)} %tied.1.refs_0_), channel_id=1, source_target_pairs={{0,6},{1,7},{2,8},{3,9},{4,10},{5,11},{6,12},{7,13},{8,14},{9,15},... | collective-permute-start | bytes 417800 | tf_op jit(solution)/shard_map/ppermute | solution.py:333
  30.9 20.8 %collective-permute-start.5 = (bf16[272,256]{1,0:T(8,128)(2,1)S(1)}, bf16[272,256]{1,0:T(8,128)(2,1)S(1)}, u32[]{:S(2)}, u32[]{:S(2)}) collective-permute-start(bf16[272,256]{1,0:T(8,128)(2,1)S(1)} %tied.1.refs_0_), channel_id=1, source_target_pairs={{0,8},{1,9},{2,10},{3,11},{4,12},{5,13},{6,14},{7,15},{8,0},{9,1},... | collective-permute-start | bytes 417800 | tf_op jit(solution)/shard_map/ppermute | solution.py:333
  48.4 5.3 %collective-permute-start.11 = (bf16[256,256]{1,0:T(8,128)(2,1)S(1)}, bf16[256,256]{1,0:T(8,128)(2,1)S(1)}, u32[]{:S(2)}, u32[]{:S(2)}) collective-permute-start(bf16[256,256]{1,0:T(8,128)(2,1)S(1)} %get-tuple-element.33), channel_id=1, source_target_pairs={{0,14},{1,15},{2,0},{3,1},{4,2},{5,3},{6,4},{7,5},{8,6},{9,7},{10,... | collective-permute-start | bytes 393224 | tf_op jit(solution)/shard_map/ppermute | solution.py:333
  48.5 6.6 %collective-permute-start.6 = (bf16[272,256]{1,0:T(8,128)(2,1)S(1)}, bf16[272,256]{1,0:T(8,128)(2,1)S(1)}, u32[]{:S(2)}, u32[]{:S(2)}) collective-permute-start(bf16[272,256]{1,0:T(8,128)(2,1)S(1)} %tied.1.refs_0_), channel_id=1, source_target_pairs={{0,2},{1,3},{2,4},{3,5},{4,6},{5,7},{6,8},{7,9},{8,10},{9,11},{10,... | collective-permute-start | bytes 417800 | tf_op jit(solution)/shard_map/ppermute | solution.py:333
  50.5 20.7 %collective-permute-start.14 = (bf16[128,1024]{1,0:T(8,128)(2,1)S(1)}, bf16[128,1024]{1,0:T(8,128)(2,1)S(1)}, u32[]{:S(2)}, u32[]{:S(2)}) collective-permute-start(bf16[128,1024]{1,0:T(8,128)(2,1)S(1)} %get-tuple-element.37), channel_id=1, source_target_pairs={{0,192},{64,0},{128,64},{192,128},{1,193},{65,1},{129,65},{193,129... | collective-permute-start | bytes 786440 | tf_op jit(solution)/shard_map/ppermute | solution.py:342
  51.3 20.0 %collective-permute-start.15 = (bf16[128,1024]{1,0:T(8,128)(2,1)S(1)}, bf16[128,1024]{1,0:T(8,128)(2,1)S(1)}, u32[]{:S(2)}, u32[]{:S(2)}) collective-permute-start(bf16[128,1024]{1,0:T(8,128)(2,1)S(1)} %get-tuple-element.38), channel_id=1, source_target_pairs={{0,193},{1,192},{2,195},{3,194},{4,197},{5,196},{6,199},{7,198},{8... | collective-permute-start | bytes 786440 | tf_op jit(solution)/shard_map/ppermute | solution.py:350
  51.7 13.2 %collective-permute-start.16 = (bf16[256,256]{1,0:T(8,128)(2,1)S(1)}, bf16[256,256]{1,0:T(8,128)(2,1)S(1)}, u32[]{:S(2)}, u32[]{:S(2)}) collective-permute-start(bf16[256,256]{1,0:T(8,128)(2,1)S(1)} %get-tuple-element.40), channel_id=1, source_target_pairs={{0,14},{1,15},{2,0},{3,1},{4,2},{5,3},{6,4},{7,5},{8,6},{9,7},{10,... | collective-permute-start | bytes 393224 | tf_op jit(solution)/shard_map/ppermute | solution.py:333
  53.8 12.7 %collective-permute-start.17 = (bf16[256,256]{1,0:T(8,128)(2,1)S(1)}, bf16[256,256]{1,0:T(8,128)(2,1)S(1)}, u32[]{:S(2)}, u32[]{:S(2)}) collective-permute-start(bf16[256,256]{1,0:T(8,128)(2,1)S(1)} %get-tuple-element.41), channel_id=1, source_target_pairs={{0,12},{1,13},{2,14},{3,15},{4,0},{5,1},{6,2},{7,3},{8,4},{9,5},{1... | collective-permute-start | bytes 393224 | tf_op jit(solution)/shard_map/ppermute | solution.py:333
  55.1 16.1 %collective-permute-start.18 = (bf16[256,256]{1,0:T(8,128)(2,1)S(1)}, bf16[256,256]{1,0:T(8,128)(2,1)S(1)}, u32[]{:S(2)}, u32[]{:S(2)}) collective-permute-start(bf16[256,256]{1,0:T(8,128)(2,1)S(1)} %add_convert_fusion.refs_5_), channel_id=1, source_target_pairs={{0,10},{1,11},{2,12},{3,13},{4,14},{5,15},{6,0},{7,1},{8,2},{9,3},... | collective-permute-start | bytes 393224 | tf_op jit(solution)/shard_map/ppermute | solution.py:333
  64.9 13.2 %collective-permute-start.12 = (bf16[128,1024]{1,0:T(8,128)(2,1)S(1)}, bf16[128,1024]{1,0:T(8,128)(2,1)S(1)}, u32[]{:S(2)}, u32[]{:S(2)}) collective-permute-start(bf16[128,1024]{1,0:T(8,128)(2,1)S(1)} %get-tuple-element.34), channel_id=1, source_target_pairs={{0,64},{64,128},{128,192},{192,0},{1,65},{65,129},{129,193},{193,1... | collective-permute-start | bytes 786440 | tf_op jit(solution)/shard_map/ppermute | solution.py:342
  66.5 11.6 %collective-permute-start.13 = (bf16[128,1024]{1,0:T(8,128)(2,1)S(1)}, bf16[128,1024]{1,0:T(8,128)(2,1)S(1)}, u32[]{:S(2)}, u32[]{:S(2)}) collective-permute-start(bf16[128,1024]{1,0:T(8,128)(2,1)S(1)} %get-tuple-element.35), channel_id=1, source_target_pairs={{0,65},{1,64},{2,67},{3,66},{4,69},{5,68},{6,71},{7,70},{8,73},{9,... | collective-permute-start | bytes 786440 | tf_op jit(solution)/shard_map/ppermute | solution.py:350
  71.9 6.3 %collective-permute-start.19 = (bf16[256,256]{1,0:T(8,128)(2,1)S(1)}, bf16[256,256]{1,0:T(8,128)(2,1)S(1)}, u32[]{:S(2)}, u32[]{:S(2)}) collective-permute-start(bf16[256,256]{1,0:T(8,128)(2,1)S(1)} %total.1), channel_id=1, source_target_pairs={{0,192},{64,0},{128,64},{192,128},{1,193},{65,1},{129,65},{193,129... | collective-permute-start | bytes 393224 | tf_op jit(solution)/shard_map/ppermute | solution.py:342
  78.1 4.3 %collective-permute-start.20 = (bf16[128,256]{1,0:T(8,128)(2,1)S(1)}, bf16[128,256]{1,0:T(8,128)(2,1)S(1)}, u32[]{:S(2)}, u32[]{:S(2)}) collective-permute-start(bf16[128,256]{1,0:T(8,128)(2,1)S(1)} %slice.4), channel_id=1, source_target_pairs={{0,1},{1,0},{2,3},{3,2},{4,5},{5,4},{6,7},{7,6},{8,9},{9,8},{10,11... | collective-permute-start | bytes 196616 | tf_op jit(solution)/shard_map/ppermute | solution.py:337

commit v8 on v7

--- a/solution.py
+++ b/solution.py
@@ -420,7 +420,7 @@
     dq_own, dq_cross, parts = run_bwd(where, own, crossed, (b0, b1, b2, b3, b4))
     far = along_z(parts[4], -1)
     three = (parts[3].astype(F32) + far.astype(F32)).astype(BF16)
-    terms = [parts[0]] + [along_z(parts[k], -k) for k in (1, 2)] + [along_z(three, -3)]
+    terms = [parts[0]] + [along_z(parts[k], -k) for k in (2, 1)] + [along_z(three, -3)]
     dq = handed(dq_own, -1), handed_across(dq_cross, -1)
     o_own, o_cross = run_fwd(where, own, crossed, blocks_f, (three,))
     dq = handed(dq_own, -1), handed_across(dq_cross, -1)

time: 84.1 us -> 83.3 us (level)
  the two profiles are of different devices: /device:TPU:24 before, /device:TPU:56 now
where the time goes in v8:
time: 83.3 us; the launch traced here: 83.1 us
  starting transfers between devices  36.9 us (44%)
  Pallas kernels  23.4 us (28%)
  waiting for transfers between devices  21.8 us (26%)
  between operations  0.92 us (1%)
    ppermute x13, starting transfers between devices, along_z(): lax.ppermute(block, 'cp', [(i, (i + 2 * distance) % n) for i in range(n)])  27.4 us
    ppermute x13, waiting for transfers between devices, along_z(): lax.ppermute(block, 'cp', [(i, (i + 2 * distance) % n) for i in range(n)])  11.8 us
    pallas_call x1, Pallas kernels, run_bwd(): call(bwd_kernel, outs, 2 + SLOTS, scratch, 5 * MATMUL, 2 ** 22, 'bwd', li...  10.4 us
    ppermute x3, waiting for transfers between devices, handed(): lax.ppermute(block, 'section', [(i, (i + distance) % n) for i in range(n)])  5.73 us
    pallas_call x1, Pallas kernels, run_fwd(): call(fwd_kernel, [shape(ROWS, HALF)] * 2, [VMEM] * (2 + SLOTS) + [ANY] *...  4.98 us
    ppermute x3, waiting for transfers between devices, swapped(): lax.ppermute(block, 'cp', [(i, i ^ 1) for i in range(lax.axis_size('cp'))])  4.29 us
    ppermute x3, starting transfers between devices, swapped(): lax.ppermute(block, 'cp', [(i, i ^ 1) for i in range(lax.axis_size('cp'))])  3.92 us
    ppermute x2, starting transfers between devices, handed_across(): return lax.ppermute(block, ('section', 'cp'), route)  2.81 us
  transfers between devices with their start and end apart: 21, of which 10 were waited for; matrix products, arithmetic and copies ran while one was open for 0% of the time, Pallas kernels for 24%

profile of v8, /device:TPU:56, one launch (start us, length us, event | category | flops | bytes accessed | tf_op | source)
XLA Modules:
  0.0 83.1 jit_solution(1853949490055499054)
XLA Ops:
  0.6 0.1 pad_add_fusion.where_ref
  0.7 1.6 %split.1 = (bf16[144,512]{1,0:T(8,128)(2,1)S(1)}, bf16[144,512]{1,0:T(8,128)(2,1)S(1)}) custom-call(s32[2]{0:T(128)S(1)} %pad_add_fusion.where_ref, bf16[128,256]{1,0:T(8,128)(2,1)} %bitcast.16, bf16[128,256]{1,0:T(8,128)(2,1)} %bitcast.17, s32[1,128]{1,0:T(1,128)} %refs_2_.1, bf16[128,256]{1,0:T(8,128)(2,1)} %bitcast.18, bf16[128,256]{1,0:T(8,128)(2,1)} %bitcast.19, ...), custom_call_target="tpu_custom_call" | custom-call | bytes 524288 | tf_op jit(solution)/shard_map/split/pallas_call | solution.py:360
  2.3 1.6 %collective-permute-start = (bf16[144,512]{1,0:T(8,128)(2,1)S(1)}, bf16[144,512]{1,0:T(8,128)(2,1)S(1)}, u32[]{:S(2)}, u32[]{:S(2)}) collective-permute-start(bf16[144,512]{1,0:T(8,128)(2,1)S(1)} %get-tuple-element.25.refs_3_), channel_id=1, source_target_pairs={{0,1},{1,0},{2,3},{3,2},{4,5},{5,4},{6,7},{7,6},{8,9},{9,8},{10,11... | collective-permute-start | bytes 442376 | tf_op jit(solution)/shard_map/ppermute | solution.py:337
  3.9 1.9 %halves.1 = (bf16[128,3072]{1,0:T(8,128)(2,1)S(1)}, bf16[128,3072]{1,0:T(8,128)(2,1)S(1)}) custom-call(s32[2]{0:T(128)S(1)} %pad_add_fusion.where_ref, bf16[128,2048]{1,0:T(8,128)(2,1)} %bitcast.13, bf16[128,2048]{1,0:T(8,128)(2,1)} %bitcast.14, bf16[128,2048]{1,0:T(8,128)(2,1)} %bitcast.15, bf16[144,512]{1,0:T(8,128)(2,1)S(1)} %get-tuple-element.25.refs_3_), custom_call_target="tpu_custom_call" | custom-call | bytes 524288 | tf_op jit(solution)/shard_map/halves/pallas_call | solution.py:402
  5.9 2.1 %collective-permute-done.got = bf16[144,512]{1,0:T(8,128)(2,1)S(1)} collective-permute-done((bf16[144,512]{1,0:T(8,128)(2,1)S(1)}, bf16[144,512]{1,0:T(8,128)(2,1)S(1)}, u32[]{:S(2)}, u32[]{:S(2)}) %collective-permute-start) | collective-permute-done | bytes 147488 | tf_op jit(solution)/shard_map/ppermute | solution.py:337
  8.0 0.6 join.1
  8.6 1.6 %collective-permute-start.1 = (bf16[128,3072]{1,0:T(8,128)(2,1)S(1)}, bf16[128,3072]{1,0:T(8,128)(2,1)S(1)}, u32[]{:S(2)}, u32[]{:S(2)}) collective-permute-start(bf16[128,3072]{1,0:T(8,128)(2,1)S(1)} %get-tuple-element.29), channel_id=1, source_target_pairs={{0,1},{1,0},{2,3},{3,2},{4,5},{5,4},{6,7},{7,6},{8,9},{9,8},{10,11... | collective-permute-start | bytes 2359304 | tf_op jit(solution)/shard_map/ppermute | solution.py:337
  10.1 5.4 %collective-permute-start.9 = (bf16[272,256]{1,0:T(8,128)(2,1)S(1)}, bf16[272,256]{1,0:T(8,128)(2,1)S(1)}, u32[]{:S(2)}, u32[]{:S(2)}) collective-permute-start(bf16[272,256]{1,0:T(8,128)(2,1)S(1)} %get-tuple-element.31.refs_0_), channel_id=1, source_target_pairs={{0,12},{1,13},{2,14},{3,15},{4,0},{5,1},{6,2},{7,3},{8,4},{9,5},{1... | collective-permute-start | bytes 417800 | tf_op jit(solution)/shard_map/ppermute | solution.py:333
  15.5 0.0 collective-permute-start.2
  15.6 1.0 %collective-permute-start.7 = (bf16[272,256]{1,0:T(8,128)(2,1)S(1)}, bf16[272,256]{1,0:T(8,128)(2,1)S(1)}, u32[]{:S(2)}, u32[]{:S(2)}) collective-permute-start(bf16[272,256]{1,0:T(8,128)(2,1)S(1)} %get-tuple-element.31.refs_0_), channel_id=1, source_target_pairs={{0,2},{1,3},{2,4},{3,5},{4,6},{5,7},{6,8},{7,9},{8,10},{9,11},{10,... | collective-permute-start | bytes 417800 | tf_op jit(solution)/shard_map/ppermute | solution.py:333
  16.6 1.9 %collective-permute-done.9 = bf16[272,256]{1,0:T(8,128)(2,1)S(1)} collective-permute-done((bf16[272,256]{1,0:T(8,128)(2,1)S(1)}, bf16[272,256]{1,0:T(8,128)(2,1)S(1)}, u32[]{:S(2)}, u32[]{:S(2)}) %collective-permute-start.9) | collective-permute-done | bytes 139296 | tf_op jit(solution)/shard_map/ppermute | solution.py:333
  18.4 4.6 %collective-permute-start.10 = (bf16[272,256]{1,0:T(8,128)(2,1)S(1)}, bf16[272,256]{1,0:T(8,128)(2,1)S(1)}, u32[]{:S(2)}, u32[]{:S(2)}) collective-permute-start(bf16[272,256]{1,0:T(8,128)(2,1)S(1)} %collective-permute-done.9), channel_id=1, source_target_pairs={{0,12},{1,13},{2,14},{3,15},{4,0},{5,1},{6,2},{7,3},{8,4},{9,5},{1... | collective-permute-start | bytes 417800 | tf_op jit(solution)/shard_map/ppermute | solution.py:333
  23.0 2.9 %collective-permute-done.2.after.refs_2_ = bf16[272,256]{1,0:T(8,128)(2,1)S(1)} collective-permute-done((bf16[272,256]{1,0:T(8,128)(2,1)S(1)}, bf16[272,256]{1,0:T(8,128)(2,1)S(1)}, u32[]{:S(2)}, u32[]{:S(2)}) %collective-permute-start.2) | collective-permute-done | bytes 139296 | tf_op jit(solution)/shard_map/ppermute | solution.py:333
  26.0 0.0 collective-permute-start.8
  26.0 0.5 tied.1.refs_0_
  26.5 1.8 %collective-permute-start.3 = (bf16[272,256]{1,0:T(8,128)(2,1)S(1)}, bf16[272,256]{1,0:T(8,128)(2,1)S(1)}, u32[]{:S(2)}, u32[]{:S(2)}) collective-permute-start(bf16[272,256]{1,0:T(8,128)(2,1)S(1)} %tied.1.refs_0_), channel_id=1, source_target_pairs={{0,4},{1,5},{2,6},{3,7},{4,8},{5,9},{6,10},{7,11},{8,12},{9,13},{1... | collective-permute-start | bytes 417800 | tf_op jit(solution)/shard_map/ppermute | solution.py:333
  28.3 0.0 collective-permute-done.7.refs_1_
  28.3 0.8 collective-permute-start.4
  29.0 0.0 collective-permute-done.10.refs_4_
  29.0 5.0 %collective-permute-start.5 = (bf16[272,256]{1,0:T(8,128)(2,1)S(1)}, bf16[272,256]{1,0:T(8,128)(2,1)S(1)}, u32[]{:S(2)}, u32[]{:S(2)}) collective-permute-start(bf16[272,256]{1,0:T(8,128)(2,1)S(1)} %tied.1.refs_0_), channel_id=1, source_target_pairs={{0,8},{1,9},{2,10},{3,11},{4,12},{5,13},{6,14},{7,15},{8,0},{9,1},... | collective-permute-start | bytes 417800 | tf_op jit(solution)/shard_map/ppermute | solution.py:333
  34.0 0.5 collective-permute-done.8.refs_3_
  34.5 0.0 collective-permute-done.1.qdx_ref.qx_ref
  34.5 10.4 %bwd.1 = (bf16[128,1024]{1,0:T(8,128)(2,1)S(1)}, bf16[128,1024]{1,0:T(8,128)(2,1)S(1)}, bf16[256,256]{1,0:T(8,128)(2,1)S(1)}, bf16[256,256]{1,0:T(8,128)(2,1)S(1...) custom-call(s32[2]{0:T(128)S(1)} %pad_add_fusion.where_ref, ...), custom_call_target="tpu_custom_call" | custom-call | flops 3355443200 | bytes 4194304 | tf_op jit(solution)/shard_map/bwd/pallas_call | solution.py:318
  44.9 3.7 %collective-permute-start.11 = (bf16[256,256]{1,0:T(8,128)(2,1)S(1)}, bf16[256,256]{1,0:T(8,128)(2,1)S(1)}, u32[]{:S(2)}, u32[]{:S(2)}) collective-permute-start(bf16[256,256]{1,0:T(8,128)(2,1)S(1)} %get-tuple-element.33), channel_id=1, source_target_pairs={{0,14},{1,15},{2,0},{3,1},{4,2},{5,3},{6,4},{7,5},{8,6},{9,7},{10,... | collective-permute-start | bytes 393224 | tf_op jit(solution)/shard_map/ppermute | solution.py:333
  48.6 0.0 collective-permute-start.6
  48.6 0.0 collective-permute-done.3.refs_1_
  48.6 0.7 collective-permute-start.14
  49.4 0.0 collective-permute-done.4.refs_2_
  49.4 0.7 collective-permute-start.15
  50.1 0.0 collective-permute-done.5.refs_3_
  50.1 2.5 %collective-permute-start.16 = (bf16[256,256]{1,0:T(8,128)(2,1)S(1)}, bf16[256,256]{1,0:T(8,128)(2,1)S(1)}, u32[]{:S(2)}, u32[]{:S(2)}) collective-permute-start(bf16[256,256]{1,0:T(8,128)(2,1)S(1)} %get-tuple-element.40), channel_id=1, source_target_pairs={{0,12},{1,13},{2,14},{3,15},{4,0},{5,1},{6,2},{7,3},{8,4},{9,5},{1... | collective-permute-start | bytes 393224 | tf_op jit(solution)/shard_map/ppermute | solution.py:333
  52.6 0.1 collective-permute-done.11
  52.7 2.6 %collective-permute-start.17 = (bf16[256,256]{1,0:T(8,128)(2,1)S(1)}, bf16[256,256]{1,0:T(8,128)(2,1)S(1)}, u32[]{:S(2)}, u32[]{:S(2)}) collective-permute-start(bf16[256,256]{1,0:T(8,128)(2,1)S(1)} %get-tuple-element.41), channel_id=1, source_target_pairs={{0,14},{1,15},{2,0},{3,1},{4,2},{5,3},{6,4},{7,5},{8,6},{9,7},{10,... | collective-permute-start | bytes 393224 | tf_op jit(solution)/shard_map/ppermute | solution.py:333
  55.3 0.0 collective-permute-done.6.refs_4_
  55.3 0.1 collective-permute-start.18
  55.4 5.0 %fwd.1 = (bf16[128,1024]{1,0:T(8,128)(2,1)S(1)}, bf16[128,1024]{1,0:T(8,128)(2,1)S(1)}) custom-call(s32[2]{0:T(128)S(1)} %pad_add_fusion.where_ref, bf16[128,3072]{1,0:T(8,128)(2,1)S(1)} %get-tuple-element.26.qd_ref.q_ref, bf16[128,3072]{1,0:T(8,128)(2,1)S(1)} %collective-permute-done.1.qdx_ref.qx_ref, bf16[272,256]{1,0:T(8,128)(2,1)S(1)} %tied.1.refs_0_, ...), custom_call_target="tpu_custom_call" | custom-call | flops 1342177280 | bytes 2097152 | tf_op jit(solution)/shard_map/fwd/pallas_call | solution.py:290
  60.4 0.1 collective-permute-done.16.refs_1_
  60.5 1.4 %collective-permute-start.12 = (bf16[128,1024]{1,0:T(8,128)(2,1)S(1)}, bf16[128,1024]{1,0:T(8,128)(2,1)S(1)}, u32[]{:S(2)}, u32[]{:S(2)}) collective-permute-start(bf16[128,1024]{1,0:T(8,128)(2,1)S(1)} %get-tuple-element.34), channel_id=1, source_target_pairs={{0,64},{64,128},{128,192},{192,0},{1,65},{65,129},{129,193},{193,1... | collective-permute-start | bytes 786440 | tf_op jit(solution)/shard_map/ppermute | solution.py:342
  61.9 2.5 %collective-permute-done.17.refs_2_ = bf16[256,256]{1,0:T(8,128)(2,1)S(1)} collective-permute-done((bf16[256,256]{1,0:T(8,128)(2,1)S(1)}, bf16[256,256]{1,0:T(8,128)(2,1)S(1)}, u32[]{:S(2)}, u32[]{:S(2)}) %collective-permute-start.17) | collective-permute-done | bytes 131104 | tf_op jit(solution)/shard_map/ppermute | solution.py:333
  64.4 2.1 %collective-permute-start.13 = (bf16[128,1024]{1,0:T(8,128)(2,1)S(1)}, bf16[128,1024]{1,0:T(8,128)(2,1)S(1)}, u32[]{:S(2)}, u32[]{:S(2)}) collective-permute-start(bf16[128,1024]{1,0:T(8,128)(2,1)S(1)} %get-tuple-element.35), channel_id=1, source_target_pairs={{0,65},{1,64},{2,67},{3,66},{4,69},{5,68},{6,71},{7,70},{8,73},{9,... | collective-permute-start | bytes 786440 | tf_op jit(solution)/shard_map/ppermute | solution.py:350
  66.5 3.9 %collective-permute-done.18.refs_3_ = bf16[256,256]{1,0:T(8,128)(2,1)S(1)} collective-permute-done((bf16[256,256]{1,0:T(8,128)(2,1)S(1)}, bf16[256,256]{1,0:T(8,128)(2,1)S(1)}, u32[]{:S(2)}, u32[]{:S(2)}) %collective-permute-start.18) | collective-permute-done | bytes 131104 | tf_op jit(solution)/shard_map/ppermute | solution.py:333
  70.4 0.0 collective-permute-done.14.refs_4_.refs_0_
  70.4 0.0 collective-permute-done.15.refs_5_.refs_1_
  70.4 0.6 total.1
  71.0 0.5 collective-permute-start.19
  71.5 5.7 %collective-permute-done.19.refs_2_ = bf16[256,256]{1,0:T(8,128)(2,1)S(1)} collective-permute-done((bf16[256,256]{1,0:T(8,128)(2,1)S(1)}, bf16[256,256]{1,0:T(8,128)(2,1)S(1)}, u32[]{:S(2)}, u32[]{:S(2)}) %collective-permute-start.19) | collective-permute-done | bytes 131104 | tf_op jit(solution)/shard_map/ppermute | solution.py:342
  77.3 0.8 collective-permute-start.20
  78.0 0.0 collective-permute-done.12.own
  78.0 0.0 collective-permute-done.13.cross
  78.0 1.4 %output.1 = (bf16[128,2048]{1,0:T(8,128)(2,1)}, bf16[16,128]{1,0:T(8,128)(2,1)S(1)}) custom-call(s32[2]{0:T(128)S(1)} %pad_add_fusion.where_ref, bf16[128,1024]{1,0:T(8,128)(2,1)S(1)} %collective-permute-done.12.own, bf16[128,1024]{1,0:T(8,128)(2,1)S(1)} %collective-permute-done.13.cross), custom_call_target="tpu_custom_call" | custom-call | flops 1342177280 | bytes 524288 | tf_op jit(solution)/shard_map/output/pallas_call | solution.py:431
  79.4 2.1 %collective-permute-done.20.refs_3_ = bf16[128,256]{1,0:T(8,128)(2,1)S(1)} collective-permute-done((bf16[128,256]{1,0:T(8,128)(2,1)S(1)}, bf16[128,256]{1,0:T(8,128)(2,1)S(1)}, u32[]{:S(2)}, u32[]{:S(2)}) %collective-permute-start.20) | collective-permute-done | bytes 65568 | tf_op jit(solution)/shard_map/ppermute | solution.py:337
  81.5 1.4 %final.1 = (bf16[128,2048]{1,0:T(8,128)(2,1)}, bf16[128,256]{1,0:T(8,128)(2,1)}, bf16[128,256]{1,0:T(8,128)(2,1)}) custom-call(s32[2]{0:T(128)S(1)} %pad_add_fusion.where_ref, bf16[128,1024]{1,0:T(8,128)(2,1)S(1)} %collective-permute-done.14.refs_4_.refs_0_, bf16[128,1024]{1,0:T(8,128)(2,1)S(1)} %collective-permute-done.15.refs_5_.refs_1_, ...), custom_call_target="tpu_custom_call" | custom-call | bytes 524288 | tf_op jit(solution)/shard_map/final/pallas_call | solution.py:440
  (2 shorter events, 0.0 us)
Async XLA Ops:
  2.3 5.7 %collective-permute-start = (bf16[144,512]{1,0:T(8,128)(2,1)S(1)}, bf16[144,512]{1,0:T(8,128)(2,1)S(1)}, u32[]{:S(2)}, u32[]{:S(2)}) collective-permute-start(bf16[144,512]{1,0:T(8,128)(2,1)S(1)} %get-tuple-element.25.refs_3_), channel_id=1, source_target_pairs={{0,1},{1,0},{2,3},{3,2},{4,5},{5,4},{6,7},{7,6},{8,9},{9,8},{10,11... | collective-permute-start | bytes 442376 | tf_op jit(solution)/shard_map/ppermute | solution.py:337
  8.6 25.9 %collective-permute-start.1 = (bf16[128,3072]{1,0:T(8,128)(2,1)S(1)}, bf16[128,3072]{1,0:T(8,128)(2,1)S(1)}, u32[]{:S(2)}, u32[]{:S(2)}) collective-permute-start(bf16[128,3072]{1,0:T(8,128)(2,1)S(1)} %get-tuple-element.29), channel_id=1, source_target_pairs={{0,1},{1,0},{2,3},{3,2},{4,5},{5,4},{6,7},{7,6},{8,9},{9,8},{10,11... | collective-permute-start | bytes 2359304 | tf_op jit(solution)/shard_map/ppermute | solution.py:337
  10.1 8.3 %collective-permute-start.9 = (bf16[272,256]{1,0:T(8,128)(2,1)S(1)}, bf16[272,256]{1,0:T(8,128)(2,1)S(1)}, u32[]{:S(2)}, u32[]{:S(2)}) collective-permute-start(bf16[272,256]{1,0:T(8,128)(2,1)S(1)} %get-tuple-element.31.refs_0_), channel_id=1, source_target_pairs={{0,12},{1,13},{2,14},{3,15},{4,0},{5,1},{6,2},{7,3},{8,4},{9,5},{1... | collective-permute-start | bytes 417800 | tf_op jit(solution)/shard_map/ppermute | solution.py:333
  15.5 10.4 %collective-permute-start.2 = (bf16[272,256]{1,0:T(8,128)(2,1)S(1)}, bf16[272,256]{1,0:T(8,128)(2,1)S(1)}, u32[]{:S(2)}, u32[]{:S(2)}) collective-permute-start(bf16[272,256]{1,0:T(8,128)(2,1)S(1)} %get-tuple-element.31.refs_0_), channel_id=1, source_target_pairs={{0,4},{1,5},{2,6},{3,7},{4,8},{5,9},{6,10},{7,11},{8,12},{9,13},{1... | collective-permute-start | bytes 417800 | tf_op jit(solution)/shard_map/ppermute | solution.py:333
  15.6 12.7 %collective-permute-start.7 = (bf16[272,256]{1,0:T(8,128)(2,1)S(1)}, bf16[272,256]{1,0:T(8,128)(2,1)S(1)}, u32[]{:S(2)}, u32[]{:S(2)}) collective-permute-start(bf16[272,256]{1,0:T(8,128)(2,1)S(1)} %get-tuple-element.31.refs_0_), channel_id=1, source_target_pairs={{0,2},{1,3},{2,4},{3,5},{4,6},{5,7},{6,8},{7,9},{8,10},{9,11},{10,... | collective-permute-start | bytes 417800 | tf_op jit(solution)/shard_map/ppermute | solution.py:333
  18.4 10.6 %collective-permute-start.10 = (bf16[272,256]{1,0:T(8,128)(2,1)S(1)}, bf16[272,256]{1,0:T(8,128)(2,1)S(1)}, u32[]{:S(2)}, u32[]{:S(2)}) collective-permute-start(bf16[272,256]{1,0:T(8,128)(2,1)S(1)} %collective-permute-done.9), channel_id=1, source_target_pairs={{0,12},{1,13},{2,14},{3,15},{4,0},{5,1},{6,2},{7,3},{8,4},{9,5},{1... | collective-permute-start | bytes 417800 | tf_op jit(solution)/shard_map/ppermute | solution.py:333
  26.0 8.5 %collective-permute-start.8 = (bf16[272,256]{1,0:T(8,128)(2,1)S(1)}, bf16[272,256]{1,0:T(8,128)(2,1)S(1)}, u32[]{:S(2)}, u32[]{:S(2)}) collective-permute-start(bf16[272,256]{1,0:T(8,128)(2,1)S(1)} %collective-permute-done.2.after.refs_2_), channel_id=1, source_target_pairs={{0,2},{1,3},{2,4},{3,5},{4,6},{5,7},{6,8},{7,9},{8,10},{9,11},{10,... | collective-permute-start | bytes 417800 | tf_op jit(solution)/shard_map/ppermute | solution.py:333
  26.5 22.1 %collective-permute-start.3 = (bf16[272,256]{1,0:T(8,128)(2,1)S(1)}, bf16[272,256]{1,0:T(8,128)(2,1)S(1)}, u32[]{:S(2)}, u32[]{:S(2)}) collective-permute-start(bf16[272,256]{1,0:T(8,128)(2,1)S(1)} %tied.1.refs_0_), channel_id=1, source_target_pairs={{0,4},{1,5},{2,6},{3,7},{4,8},{5,9},{6,10},{7,11},{8,12},{9,13},{1... | collective-permute-start | bytes 417800 | tf_op jit(solution)/shard_map/ppermute | solution.py:333
  28.3 21.1 %collective-permute-start.4 = (bf16[272,256]{1,0:T(8,128)(2,1)S(1)}, bf16[272,256]{1,0:T(8,128)(2,1)S(1)}, u32[]{:S(2)}, u32[]{:S(2)}) collective-permute-start(bf16[272,256]{1,0:T(8,128)(2,1)S(1)} %tied.1.refs_0_), channel_id=1, source_target_pairs={{0,6},{1,7},{2,8},{3,9},{4,10},{5,11},{6,12},{7,13},{8,14},{9,15},... | collective-permute-start | bytes 417800 | tf_op jit(solution)/shard_map/ppermute | solution.py:333
  29.0 21.0 %collective-permute-start.5 = (bf16[272,256]{1,0:T(8,128)(2,1)S(1)}, bf16[272,256]{1,0:T(8,128)(2,1)S(1)}, u32[]{:S(2)}, u32[]{:S(2)}) collective-permute-start(bf16[272,256]{1,0:T(8,128)(2,1)S(1)} %tied.1.refs_0_), channel_id=1, source_target_pairs={{0,8},{1,9},{2,10},{3,11},{4,12},{5,13},{6,14},{7,15},{8,0},{9,1},... | collective-permute-start | bytes 417800 | tf_op jit(solution)/shard_map/ppermute | solution.py:333
  44.9 7.8 %collective-permute-start.11 = (bf16[256,256]{1,0:T(8,128)(2,1)S(1)}, bf16[256,256]{1,0:T(8,128)(2,1)S(1)}, u32[]{:S(2)}, u32[]{:S(2)}) collective-permute-start(bf16[256,256]{1,0:T(8,128)(2,1)S(1)} %get-tuple-element.33), channel_id=1, source_target_pairs={{0,14},{1,15},{2,0},{3,1},{4,2},{5,3},{6,4},{7,5},{8,6},{9,7},{10,... | collective-permute-start | bytes 393224 | tf_op jit(solution)/shard_map/ppermute | solution.py:333
  48.6 6.7 %collective-permute-start.6 = (bf16[272,256]{1,0:T(8,128)(2,1)S(1)}, bf16[272,256]{1,0:T(8,128)(2,1)S(1)}, u32[]{:S(2)}, u32[]{:S(2)}) collective-permute-start(bf16[272,256]{1,0:T(8,128)(2,1)S(1)} %tied.1.refs_0_), channel_id=1, source_target_pairs={{0,2},{1,3},{2,4},{3,5},{4,6},{5,7},{6,8},{7,9},{8,10},{9,11},{10,... | collective-permute-start | bytes 417800 | tf_op jit(solution)/shard_map/ppermute | solution.py:333
  48.6 21.7 %collective-permute-start.14 = (bf16[128,1024]{1,0:T(8,128)(2,1)S(1)}, bf16[128,1024]{1,0:T(8,128)(2,1)S(1)}, u32[]{:S(2)}, u32[]{:S(2)}) collective-permute-start(bf16[128,1024]{1,0:T(8,128)(2,1)S(1)} %get-tuple-element.37), channel_id=1, source_target_pairs={{0,192},{64,0},{128,64},{192,128},{1,193},{65,1},{129,65},{193,129... | collective-permute-start | bytes 786440 | tf_op jit(solution)/shard_map/ppermute | solution.py:342
  49.4 21.0 %collective-permute-start.15 = (bf16[128,1024]{1,0:T(8,128)(2,1)S(1)}, bf16[128,1024]{1,0:T(8,128)(2,1)S(1)}, u32[]{:S(2)}, u32[]{:S(2)}) collective-permute-start(bf16[128,1024]{1,0:T(8,128)(2,1)S(1)} %get-tuple-element.38), channel_id=1, source_target_pairs={{0,193},{1,192},{2,195},{3,194},{4,197},{5,196},{6,199},{7,198},{8... | collective-permute-start | bytes 786440 | tf_op jit(solution)/shard_map/ppermute | solution.py:350
  50.1 10.4 %collective-permute-start.16 = (bf16[256,256]{1,0:T(8,128)(2,1)S(1)}, bf16[256,256]{1,0:T(8,128)(2,1)S(1)}, u32[]{:S(2)}, u32[]{:S(2)}) collective-permute-start(bf16[256,256]{1,0:T(8,128)(2,1)S(1)} %get-tuple-element.40), channel_id=1, source_target_pairs={{0,12},{1,13},{2,14},{3,15},{4,0},{5,1},{6,2},{7,3},{8,4},{9,5},{1... | collective-permute-start | bytes 393224 | tf_op jit(solution)/shard_map/ppermute | solution.py:333
  52.7 11.7 %collective-permute-start.17 = (bf16[256,256]{1,0:T(8,128)(2,1)S(1)}, bf16[256,256]{1,0:T(8,128)(2,1)S(1)}, u32[]{:S(2)}, u32[]{:S(2)}) collective-permute-start(bf16[256,256]{1,0:T(8,128)(2,1)S(1)} %get-tuple-element.41), channel_id=1, source_target_pairs={{0,14},{1,15},{2,0},{3,1},{4,2},{5,3},{6,4},{7,5},{8,6},{9,7},{10,... | collective-permute-start | bytes 393224 | tf_op jit(solution)/shard_map/ppermute | solution.py:333
  55.3 15.0 %collective-permute-start.18 = (bf16[256,256]{1,0:T(8,128)(2,1)S(1)}, bf16[256,256]{1,0:T(8,128)(2,1)S(1)}, u32[]{:S(2)}, u32[]{:S(2)}) collective-permute-start(bf16[256,256]{1,0:T(8,128)(2,1)S(1)} %add_convert_fusion.refs_5_), channel_id=1, source_target_pairs={{0,10},{1,11},{2,12},{3,13},{4,14},{5,15},{6,0},{7,1},{8,2},{9,3},... | collective-permute-start | bytes 393224 | tf_op jit(solution)/shard_map/ppermute | solution.py:333
  60.5 17.6 %collective-permute-start.12 = (bf16[128,1024]{1,0:T(8,128)(2,1)S(1)}, bf16[128,1024]{1,0:T(8,128)(2,1)S(1)}, u32[]{:S(2)}, u32[]{:S(2)}) collective-permute-start(bf16[128,1024]{1,0:T(8,128)(2,1)S(1)} %get-tuple-element.34), channel_id=1, source_target_pairs={{0,64},{64,128},{128,192},{192,0},{1,65},{65,129},{129,193},{193,1... | collective-permute-start | bytes 786440 | tf_op jit(solution)/shard_map/ppermute | solution.py:342
  64.4 13.6 %collective-permute-start.13 = (bf16[128,1024]{1,0:T(8,128)(2,1)S(1)}, bf16[128,1024]{1,0:T(8,128)(2,1)S(1)}, u32[]{:S(2)}, u32[]{:S(2)}) collective-permute-start(bf16[128,1024]{1,0:T(8,128)(2,1)S(1)} %get-tuple-element.35), channel_id=1, source_target_pairs={{0,65},{1,64},{2,67},{3,66},{4,69},{5,68},{6,71},{7,70},{8,73},{9,... | collective-permute-start | bytes 786440 | tf_op jit(solution)/shard_map/ppermute | solution.py:350
  71.0 6.3 %collective-permute-start.19 = (bf16[256,256]{1,0:T(8,128)(2,1)S(1)}, bf16[256,256]{1,0:T(8,128)(2,1)S(1)}, u32[]{:S(2)}, u32[]{:S(2)}) collective-permute-start(bf16[256,256]{1,0:T(8,128)(2,1)S(1)} %total.1), channel_id=1, source_target_pairs={{0,192},{64,0},{128,64},{192,128},{1,193},{65,1},{129,65},{193,129... | collective-permute-start | bytes 393224 | tf_op jit(solution)/shard_map/ppermute | solution.py:342
  77.3 4.3 %collective-permute-start.20 = (bf16[128,256]{1,0:T(8,128)(2,1)S(1)}, bf16[128,256]{1,0:T(8,128)(2,1)S(1)}, u32[]{:S(2)}, u32[]{:S(2)}) collective-permute-start(bf16[128,256]{1,0:T(8,128)(2,1)S(1)} %slice.4), channel_id=1, source_target_pairs={{0,1},{1,0},{2,3},{3,2},{4,5},{5,4},{6,7},{7,6},{8,9},{9,8},{10,11... | collective-permute-start | bytes 196616 | tf_op jit(solution)/shard_map/ppermute | solution.py:337
